TPU v7x, 32 devices: a whole 2x2x4 slice. The times are simulated.
32 devices in a mesh: dp: 16 (over z, y, core), tensor: 2 (over x).
Axes of the slice: x: 2, y: 2, z: 4, core: 2. Of those that a mesh axis runs over, the one named last changes fastest.
Arguments:
- block_input: bfloat16 [32768, 768], P(('dp', 'tensor')), may hold values from -15 to 15
- cotangent: bfloat16 [32768, 768], P(('dp', 'tensor')), may hold values from -6 to 6
- w_qkv: bfloat16 [768, 3, 768], P('dp', None, 'tensor'), may hold values from -0.21875 to 0.21875
- w_out: bfloat16 [768, 768], P('tensor', 'dp'), may hold values from -0.875 to 0.875
- w_up: bfloat16 [768, 3072], P('dp', 'tensor'), may hold values from -0.21875 to 0.21875
- w_down: bfloat16 [3072, 768], P('tensor', 'dp'), may hold values from -0.109375 to 0.109375
- w_mod: bfloat16 [768, 4608], P(None, ('dp', 'tensor')), may hold values from -0.21875 to 0.21875
- time_table: bfloat16 [256, 768], P(('dp', 'tensor')), may hold values from -5 to 5
- prompt_len: int32 [16], P('dp'), may hold values from 512 to 1024, as said below
- cont_len: int32 [16, 8], P('dp'), may hold values from 64 to 128, as said below
- timestep: int32 [16, 9], P('dp'), may hold values from 0 to 255
Outputs:
- block_output: bfloat16 [32768, 768], P(('dp', 'tensor'))
- input_grad: float32 [32768, 768], P(('dp', 'tensor'))
- qkv_grad: float32 [768, 3, 768], P('dp', None, 'tensor')
- out_grad: float32 [768, 768], P('tensor', 'dp')
- up_grad: float32 [768, 3072], P('dp', 'tensor')
- down_grad: float32 [3072, 768], P('tensor', 'dp')
- mod_grad: float32 [768, 4608], P(None, ('dp', 'tensor'))
- table_grad: float32 [256, 768], P(('dp', 'tensor'))
- stats: float32 [3], replicated
Inputs may be any that keep to these rules, and one draw needn't show every extreme that they name: `prompt_len`: some group has exactly 1024 valid prompt tokens and some 1024 // 2. `cont_len`: some continuation has exactly 128 valid tokens and some 128 // 2.
All inputs are finite; a program needn't handle non-finite values.
Results may differ from a plain program's by a relative error of at most 0.01575.
The roundings to bfloat16 on the way count: a program that leaves them out, or rounds other values in their place, can miss the bound.
Values may be sent and summed in bfloat16 or wider, within the bound.
No kernel may reach another device: no remote copies, remote signals or barrier semaphores. Data moves between devices by JAX's collectives and lax.ppermute only.
A program may use at most 320 MiB of HBM per device.

v0:
```python
import jax
import jax.numpy as jnp
from jax import lax
from jax.sharding import PartitionSpec as P

HEAD_DIM = 64
PROMPT = 1024
CONT = 128
NCONT = 8
STEPS = 256
QBLOCK = 512
GRP_TOK = 2048


masked_score = -1e30


def norm_modulate(inputs, shifts, scales):
    average = jnp.mean(inputs, -1, keepdims=True)
    centred = inputs - average
    spread = jnp.mean(centred * centred, -1, keepdims=True)
    return centred * lax.rsqrt(spread + 1e-05) * (1.0 + scales) + shifts


def rotate(heads, places):
    half_dim = heads.shape[-1] // 2
    freqs = 10000.0 ** (-jnp.arange(half_dim, dtype=jnp.float32) / half_dim)
    angles = places[:, None] * freqs[None, :]
    cosine = jnp.cos(angles)[:, None, :]
    sine = jnp.sin(angles)[:, None, :]
    first = heads[..., :half_dim]
    second = heads[..., half_dim:]
    return jnp.concatenate([first * cosine - second * sine, second * cosine + first * sine], -1)


def allowed_pairs(query_pos, key_pos, key_valid):
    query_cont = query_pos >= PROMPT
    key_cont = key_pos >= PROMPT
    query_id = jnp.maximum(query_pos - PROMPT, 0) // CONT
    key_id = jnp.maximum(key_pos - PROMPT, 0) // CONT
    earlier = key_pos[None, :] <= query_pos[:, None]
    to_prompt = jnp.logical_not(key_cont)[None, :] & (query_cont[:, None] | earlier)
    to_self = (
        key_cont[None, :] & query_cont[:, None] & (key_id[None, :] == query_id[:, None]) & earlier
    )
    return key_valid[None, :] & (to_prompt | to_self)


def layout(prompt_len, cont_len, groups_here):
    index_all = jnp.arange(groups_here * GRP_TOK, dtype=jnp.int32)
    member = index_all // GRP_TOK
    inside = index_all % GRP_TOK
    in_cont = inside >= PROMPT
    offset = jnp.maximum(inside - PROMPT, 0)
    cont_id = offset // CONT
    within = offset % CONT
    pick_group = member[:, None] == jnp.arange(groups_here, dtype=jnp.int32)[None, :]
    prompt_row = jnp.sum(jnp.where(pick_group, prompt_len[None, :], 0), 1)
    slot_index = member * NCONT + cont_id
    pick_slot = slot_index[:, None] == jnp.arange(groups_here * NCONT, dtype=jnp.int32)[None, :]
    cont_row = jnp.sum(jnp.where(pick_slot, cont_len.reshape(-1)[None, :], 0), 1)
    places = jnp.where(in_cont, prompt_row + within, inside).astype(jnp.float32)
    valid = jnp.where(in_cont, within < cont_row, inside < prompt_row)
    segment = member * (NCONT + 1) + jnp.where(in_cont, 1 + cont_id, 0)
    return (places, valid, segment)


def transpose_dot(left, right):
    return lax.dot_general(
        left, right, (((0,), (0,)), ((), ())), preferred_element_type=jnp.float32
    )


def right_dot(left, right):
    return lax.dot_general(
        left, right, (((1,), (1,)), ((), ())), preferred_element_type=jnp.float32
    )


def body(
    block_input,
    cotangent,
    w_qkv,
    w_out,
    w_up,
    w_down,
    w_mod,
    time_table,
    prompt_len,
    cont_len,
    timestep,
):
    local_rows = block_input.shape[0]
    model_width = block_input.shape[1]
    groups_here = prompt_len.shape[0]
    total_rows = groups_here * GRP_TOK
    segments_here = groups_here * (NCONT + 1)
    dp_count = lax.axis_size("dp")
    tensor_count = lax.axis_size("tensor")
    row_start = lax.axis_index("tensor") * local_rows
    places, valid, segment = layout(prompt_len, cont_len, groups_here)
    valid_local = lax.dynamic_slice_in_dim(valid, row_start, local_rows, 0)
    segment_local = lax.dynamic_slice_in_dim(segment, row_start, local_rows, 0)
    seg_table = (
        segment_local[:, None] == jnp.arange(segments_here, dtype=jnp.int32)[None, :]
    ).astype(jnp.float32)

    def fetch_attn():
        return (
            lax.all_gather(w_qkv, "dp", axis=0, tiled=True),
            lax.all_gather(w_out, "dp", axis=1, tiled=True),
        )

    def fetch_mlp():
        return (
            lax.all_gather(w_up, "dp", axis=0, tiled=True),
            lax.all_gather(w_down, "dp", axis=1, tiled=True),
        )

    step_rows = lax.all_gather(timestep, "dp", axis=0, tiled=True).reshape(-1)
    table_full = lax.all_gather(time_table, ("dp", "tensor"), axis=0, tiled=True)
    step_all = (step_rows[:, None] == jnp.arange(STEPS, dtype=jnp.int32)[None, :]).astype(
        jnp.float32
    )
    cond_all = jnp.dot(
        step_all.astype(jnp.bfloat16), table_full, preferred_element_type=jnp.float32
    ).astype(jnp.bfloat16)
    col_width = w_mod.shape[1]
    col_part = jnp.dot(cond_all, w_mod, preferred_element_type=jnp.float32)
    own_cols = lax.all_to_all(col_part, "dp", split_axis=0, concat_axis=1, tiled=True)
    halves = lax.all_gather(
        own_cols.reshape(segments_here, dp_count, 1, col_width), "tensor", axis=2, tiled=True
    )
    modulate = halves.reshape(segments_here, 6 * model_width)
    row_mod = jnp.dot(seg_table, modulate, precision=lax.Precision.HIGHEST).reshape(
        local_rows, 6, model_width
    )
    inputs = block_input.astype(jnp.float32)
    normed = norm_modulate(inputs, row_mod[:, 0], row_mod[:, 1]).astype(jnp.bfloat16)
    normed_all = lax.all_gather(normed, "tensor", axis=0, tiled=True)
    qkv_full, out_full = fetch_attn()
    joined = jnp.einsum("rd,dcf->rcf", normed_all, qkv_full, preferred_element_type=jnp.float32)
    head_width = joined.shape[2]
    heads_here = head_width // HEAD_DIM
    queries = rotate(joined[:, 0].reshape(total_rows, heads_here, HEAD_DIM), places).astype(
        jnp.bfloat16
    )
    keys_rot = rotate(joined[:, 1].reshape(total_rows, heads_here, HEAD_DIM), places).astype(
        jnp.bfloat16
    )
    values = joined[:, 2].reshape(total_rows, heads_here, HEAD_DIM).astype(jnp.bfloat16)
    scaling = HEAD_DIM ** (-0.5)
    block_count = total_rows // QBLOCK
    key_pos = jnp.arange(GRP_TOK, dtype=jnp.int32)

    def block_scores(block_index):
        start = block_index * QBLOCK
        key_start = start // GRP_TOK * GRP_TOK
        query_blk = lax.dynamic_slice_in_dim(queries, start, QBLOCK, 0)
        query_pos = start - key_start + jnp.arange(QBLOCK, dtype=jnp.int32)
        allowed = allowed_pairs(query_pos, key_pos, valid)
        scores = (
            jnp.einsum("qhd,khd->hqk", query_blk, keys_rot, preferred_element_type=jnp.float32)
            * scaling
        )
        return (
            jnp.where(allowed[None], scores, masked_score),
            query_blk,
            keys_rot,
            values,
            key_start,
        )

    def forward_block(block_index):
        scores, query_blk, key_blk, value_blk, key_start = block_scores(block_index)
        highest = jnp.max(scores, -1, keepdims=True)
        exponent = jnp.exp(scores - highest)
        total_weight = jnp.sum(exponent, -1, keepdims=True)
        probability = (exponent / total_weight).astype(jnp.bfloat16)
        outputs = jnp.einsum(
            "hqk,khd->qhd", probability, value_blk, preferred_element_type=jnp.float32
        )
        return (outputs, (highest + jnp.log(total_weight))[..., 0])

    block_outs, log_total = lax.map(forward_block, jnp.arange(block_count, dtype=jnp.int32))
    attended = block_outs.reshape(total_rows, head_width).astype(jnp.bfloat16)
    attn_branch = lax.psum_scatter(
        jnp.dot(attended, out_full, preferred_element_type=jnp.float32).astype(jnp.bfloat16),
        "tensor",
        scatter_dimension=0,
        tiled=True,
    ).astype(jnp.float32)
    middle = inputs + row_mod[:, 2] * attn_branch
    normed_two = norm_modulate(middle, row_mod[:, 3], row_mod[:, 4]).astype(jnp.bfloat16)
    normed_two_all = lax.all_gather(normed_two, "tensor", axis=0, tiled=True)
    up_full, down_full = fetch_mlp()
    pre_act = jnp.dot(normed_two_all, up_full, preferred_element_type=jnp.float32)
    gelu_value, gelu_back = jax.vjp(lambda inner: jax.nn.gelu(inner, approximate=False), pre_act)
    hidden = gelu_value.astype(jnp.bfloat16)
    mlp_branch = lax.psum_scatter(
        jnp.dot(hidden, down_full, preferred_element_type=jnp.float32).astype(jnp.bfloat16),
        "tensor",
        scatter_dimension=0,
        tiled=True,
    ).astype(jnp.float32)
    result = middle + row_mod[:, 5] * mlp_branch
    weight_valid = valid_local.astype(jnp.float32)[:, None]
    attn_part = row_mod[:, 2] * attn_branch
    mlp_part = row_mod[:, 5] * mlp_branch
    local_sums = jnp.stack(
        [
            jnp.sum(weight_valid * result * result),
            jnp.sum(weight_valid * attn_part * attn_part),
            jnp.sum(weight_valid * mlp_part * mlp_part),
            jnp.sum(weight_valid) * model_width,
        ]
    )
    totals = lax.psum(local_sums, ("dp", "tensor"))
    stats = jnp.sqrt(totals[:3] / totals[3])
    qkv_full, out_full = fetch_attn()
    up_full, down_full = fetch_mlp()
    upstream = cotangent.astype(jnp.float32)
    mlp_grad = (upstream * row_mod[:, 5]).astype(jnp.bfloat16)
    gate_two_grad = upstream * mlp_branch
    mlp_grad_all = lax.all_gather(mlp_grad, "tensor", axis=0, tiled=True)
    down_grad = transpose_dot(hidden, mlp_grad_all)
    pre_grad = gelu_back(right_dot(mlp_grad_all, down_full))[0].astype(jnp.bfloat16)
    up_grad = transpose_dot(normed_two_all, pre_grad)
    normed_two_grad = lax.psum_scatter(
        right_dot(pre_grad, up_full).astype(jnp.bfloat16), "tensor", scatter_dimension=0, tiled=True
    ).astype(jnp.float32)
    norm_two_value, norm_two_back = jax.vjp(norm_modulate, middle, row_mod[:, 3], row_mod[:, 4])
    middle_part, shift_two_grad, scale_two_grad = norm_two_back(normed_two_grad)
    middle_grad = upstream + middle_part
    attn_grad = (middle_grad * row_mod[:, 2]).astype(jnp.bfloat16)
    gate_one_grad = middle_grad * attn_branch
    attn_grad_all = lax.all_gather(attn_grad, "tensor", axis=0, tiled=True)
    out_grad = transpose_dot(attended, attn_grad_all)
    attended_grad = (
        right_dot(attn_grad_all, out_full)
        .astype(jnp.bfloat16)
        .reshape(total_rows, heads_here, HEAD_DIM)
    )

    def backward_block(running, block_index):
        key_grad, value_grad = running
        scores, query_blk, key_blk, value_blk, key_start = block_scores(block_index)
        probability = jnp.exp(scores - log_total[block_index][..., None])
        grad_blk = lax.dynamic_slice_in_dim(attended_grad, block_index * QBLOCK, QBLOCK, 0)
        prob_grad = jnp.einsum(
            "qhd,khd->hqk", grad_blk, value_blk, preferred_element_type=jnp.float32
        )
        centre = jnp.sum(probability * prob_grad, -1, keepdims=True)
        score_grad = (probability * (prob_grad - centre)).astype(jnp.bfloat16)
        query_grad = (
            jnp.einsum("hqk,khd->qhd", score_grad, key_blk, preferred_element_type=jnp.float32)
            * scaling
        )
        key_part = (
            jnp.einsum("hqk,qhd->khd", score_grad, query_blk, preferred_element_type=jnp.float32)
            * scaling
        )
        value_part = jnp.einsum(
            "hqk,qhd->khd",
            probability.astype(jnp.bfloat16),
            grad_blk,
            preferred_element_type=jnp.float32,
        )
        key_grad = key_grad + key_part
        value_grad = value_grad + value_part
        return ((key_grad, value_grad), query_grad)

    zero_heads = jnp.zeros((total_rows, heads_here, HEAD_DIM), jnp.float32)
    (key_grads, value_grads), query_blocks = lax.scan(
        backward_block, (zero_heads, zero_heads), jnp.arange(block_count, dtype=jnp.int32)
    )
    query_grads = rotate(query_blocks.reshape(total_rows, heads_here, HEAD_DIM), -places)
    key_grads = rotate(key_grads, -places)
    joined_grad = jnp.stack(
        [
            query_grads.reshape(total_rows, head_width),
            key_grads.reshape(total_rows, head_width),
            value_grads.reshape(total_rows, head_width),
        ],
        1,
    ).astype(jnp.bfloat16)
    qkv_grad = jnp.einsum(
        "rd,rcf->dcf", normed_all, joined_grad, preferred_element_type=jnp.float32
    )
    normed_grad = lax.psum_scatter(
        jnp.einsum("rcf,dcf->rd", joined_grad, qkv_full, preferred_element_type=jnp.float32).astype(
            jnp.bfloat16
        ),
        "tensor",
        scatter_dimension=0,
        tiled=True,
    ).astype(jnp.float32)
    norm_one_value, norm_one_back = jax.vjp(norm_modulate, inputs, row_mod[:, 0], row_mod[:, 1])
    input_part, shift_one_grad, scale_one_grad = norm_one_back(normed_grad)
    input_grad = middle_grad + input_part
    row_grads = jnp.stack(
        [
            shift_one_grad,
            scale_one_grad,
            gate_one_grad,
            shift_two_grad,
            scale_two_grad,
            gate_two_grad,
        ],
        1,
    ).reshape(local_rows, 6 * model_width)
    modulate_grad = lax.dot_general(
        seg_table,
        row_grads,
        (((0,), (0,)), ((), ())),
        precision=lax.Precision.HIGHEST,
        preferred_element_type=jnp.float32,
    ).astype(jnp.bfloat16)
    arrived = lax.all_to_all(
        lax.all_to_all(
            modulate_grad.reshape(segments_here, dp_count, tensor_count, col_width),
            "dp",
            split_axis=1,
            concat_axis=0,
            tiled=True,
        ),
        "tensor",
        split_axis=2,
        concat_axis=0,
        tiled=True,
    ).reshape(-1, col_width)
    half_rows = step_rows.shape[0]
    upper = arrived[:half_rows]
    lower = arrived[half_rows:]
    mod_grad = transpose_dot(cond_all, upper) + transpose_dot(cond_all, lower)
    condition_grad = right_dot(upper, w_mod) + right_dot(lower, w_mod)
    table_part = lax.dot_general(
        step_all,
        condition_grad,
        (((0,), (0,)), ((), ())),
        precision=lax.Precision.HIGHEST,
        preferred_element_type=jnp.float32,
    )
    table_grad = lax.psum_scatter(table_part, ("dp", "tensor"), scatter_dimension=0, tiled=True)
    qkv_grad, out_grad, up_grad, down_grad = (
        lax.psum_scatter(qkv_grad, "dp", scatter_dimension=0, tiled=True),
        lax.psum_scatter(out_grad, "dp", scatter_dimension=1, tiled=True),
        lax.psum_scatter(up_grad, "dp", scatter_dimension=0, tiled=True),
        lax.psum_scatter(down_grad, "dp", scatter_dimension=1, tiled=True),
    )
    return (
        result.astype(jnp.bfloat16),
        input_grad,
        qkv_grad,
        out_grad,
        up_grad,
        down_grad,
        mod_grad,
        table_grad,
        stats,
    )


def solution(mesh):
    return jax.shard_map(
        body,
        mesh=mesh,
        in_specs=(
            P(("dp", "tensor"), None),
            P(("dp", "tensor"), None),
            P("dp", None, "tensor"),
            P("tensor", "dp"),
            P("dp", "tensor"),
            P("tensor", "dp"),
            P(None, ("dp", "tensor")),
            P(("dp", "tensor"), None),
            P("dp"),
            P("dp", None),
            P("dp", None),
        ),
        out_specs=(
            P(("dp", "tensor"), None),
            P(("dp", "tensor"), None),
            P("dp", None, "tensor"),
            P("tensor", "dp"),
            P("dp", "tensor"),
            P("tensor", "dp"),
            P(None, ("dp", "tensor")),
            P(("dp", "tensor"), None),
            P(),
        ),
        check_vma=False,
    )
```

profile of v0, /device:TPU:0, one launch (start us, length us, event | category | flops | bytes accessed | tf_op | source)
XLA Modules:
  0.0 1697.2 jit_solution(8475118025361316098)
XLA Ops:
  7.2 23.3 %all-gather.1 = s32[16,1,9]{2,1,0:T(1,128)S(1)} all-gather(s32[1,1,9]{2,1,0:T(1,128)} %bitcast.245), channel_id=1, replica_groups=mesh['dp'=16,'tensor'=2] {'dp'}, dimensions={0}, use_global_device_ids=true | all-gather | bytes 612 | tf_op jit(solution)/shard_map/all_gather | solution.py:120
  31.8 67.2 %all_gather.38 = bf16[256,768]{1,0:T(8,128)(2,1)S(1)} all-gather(bf16[8,768]{1,0:T(8,128)(2,1)} %param.22), channel_id=1, replica_groups=mesh['dp'=16,'tensor'=2] {'dp','tensor'}, dimensions={0}, use_global_device_ids=true | all-gather | bytes 405504 | tf_op jit(solution)/shard_map/all_gather | solution.py:121
  114.0 28.3 %all-gather = f32[9,16,288]{1,0,2:T(8,128)} all-gather(f32[9,16,144]{1,0,2:T(8,128)S(1)} %copy.69), channel_id=2, replica_groups=mesh['dp'=16,'tensor'=2] {'tensor'}, dimensions={2}, use_global_device_ids=true | all-gather | bytes 248832 | tf_op jit(solution)/shard_map/all_gather | solution.py:131
  162.8 21.7 %all_gather.42 = bf16[384,768]{0,1:T(8,128)(2,1)} all-gather(bf16[384,48]{0,1:T(8,128)(2,1)S(1)} %copy-done.50), channel_id=1, replica_groups=mesh['dp'=16,'tensor'=2] {'dp'}, dimensions={1}, use_global_device_ids=true | all-gather | bytes 626688 | tf_op jit(solution)/shard_map/all_gather | solution.py:111
  203.6 42.8 %all-gather.12.cloned.1.call-done = bf16[768,3,384]{2,0,1:T(8,128)(2,1)} async-done(((bf16[48,3,384]{2,0,1:T(8,128)(2,1)}), bf16[768,3,384]{2,0,1:T(8,128)(2,1)}) %all-gather.12.cloned.1.call-update) | async-done | bytes 1769488 | tf_op jit(solution)/shard_map/all_gather | solution.py:110
  256.1 160.8 %while.36 = (s32[]{:T(128)}, bf16[4,512,6,64]{1,3,2,0:T(8,128)(2,1)}, f32[4,6,512]{2,1,0:T(8,128)}, pred[2048]{0:T(1024)(128)(4,1)S(1)}, s32[4]{0:T(128)S(1)}, /...) while((s32[]{:T(128)}, ...), condition=%wide.region_6.7_spmd.clone.clone, body=%wide.region_3.6_spmd.clone.clone.sunk | while | flops 1695575552 | bytes 96746944 | solution.py:185
  428.3 39.9 %reduce-scatter.10.cloned.1.call-done = bf16[1024,768]{0,1:T(8,128)(2,1)} async-done(((bf16[2048,768]{0,1:T(8,128)(2,1)}), bf16[1024,768]{0,1:T(8,128)(2,1)}) %reduce-scatter.10.cloned.1.call-update) | async-done | bytes 1572880 | tf_op jit(solution)/shard_map/reduce_scatter | solution.py:187
  481.0 31.9 %all-gather.16.cloned.1.call-done = bf16[768,1536]{1,0:T(8,128)(2,1)} async-done(((bf16[48,1536]{1,0:T(8,128)(2,1)}), bf16[768,1536]{1,0:T(8,128)(2,1)}) %all-gather.16.cloned.1.call-update) | async-done | bytes 2359312 | tf_op jit(solution)/shard_map/all_gather | solution.py:116
  512.9 45.2 %all-gather.14.cloned.1.call-done = bf16[2048,768]{0,1:T(8,128)(2,1)} async-done(((bf16[1024,768]{0,1:T(8,128)(2,1)}), bf16[2048,768]{0,1:T(8,128)(2,1)}) %all-gather.14.cloned.1.call-update) | async-done | bytes 3145744 | tf_op jit(solution)/shard_map/all_gather | solution.py:195
  558.1 35.4 %multiply_convert_fusion.1 = (bf16[2048,1536]{1,0:T(8,128)(2,1)}, f32[2048,1536]{1,0:T(8,128)}, f32[2048,1536]{1,0:T(8,128)}) fusion(bf16[2048,768]{0,1:T(8,128)(2,1)} %all-gather.14.cloned.1.call-done, bf16[768,1536]{1,0:T(8,128)(2,1)} %all-gather.16.cloned.1.call-done), kind=kOutput, calls=%fused_computation.90 | convolution fusion | flops 5036310528 | bytes 36962304 | tf_op jit(solution)/shard_map/dot_general | solution.py:197
  611.9 36.8 %all-gather.20.cloned.1.call-done = bf16[2048,768]{0,1:T(8,128)(2,1)} async-done(((bf16[1024,768]{0,1:T(8,128)(2,1)}), bf16[2048,768]{0,1:T(8,128)(2,1)}) %all-gather.20.cloned.1.call-update) | async-done | bytes 3145744 | tf_op jit(solution)/shard_map/all_gather | solution.py:225
  673.1 21.3 %reduce-scatter.12.cloned.1.call-done = bf16[1024,768]{0,1:T(8,128)(2,1)} async-done(((bf16[2048,768]{0,1:T(8,128)(2,1)}), bf16[1024,768]{0,1:T(8,128)(2,1)}) %reduce-scatter.12.cloned.1.call-update) | async-done | bytes 1572880 | tf_op jit(solution)/shard_map/reduce_scatter | solution.py:200
  694.4 45.6 %reduce-scatter.14.cloned.1.call-done = bf16[1024,768]{0,1:T(8,128)(2,1)} async-done(((bf16[2048,768]{0,1:T(8,128)(2,1)}), bf16[1024,768]{0,1:T(8,128)(2,1)}) %reduce-scatter.14.cloned.1.call-update) | async-done | bytes 1572880 | tf_op jit(solution)/shard_map/reduce_scatter | solution.py:229
  756.7 45.0 %all-gather.22.cloned.1.call-done = bf16[2048,768]{0,1:T(8,128)(2,1)} async-done(((bf16[1024,768]{0,1:T(8,128)(2,1)}), bf16[2048,768]{0,1:T(8,128)(2,1)}) %all-gather.22.cloned.1.call-update) | async-done | bytes 3145744 | tf_op jit(solution)/shard_map/all_gather | solution.py:237
  806.2 419.9 %while.37 = (s32[]{:T(128)}, f32[2048,6,64]{0,2,1:T(8,128)}, f32[2048,6,64]{0,2,1:T(8,128)}, f32[4,512,6,64]{1,0,3,2:T(4,128)}, s32[4]{0:T(128)S(1)}, /*index=5*...) while((s32[]{:T(128)}, f32[2048,6,64]{0,2,1:T(8,128)}, ...), condition=%wide.region_16.17_spmd.clone.clone, body=%wide.region_14.16_spmd.clone.clone.sunk | while | flops 4134497792 | bytes 215866832 | solution.py:274
  854.5 21.3 %multiply_convert_fusion.4 = bf16[6,512,2048]{2,1,0:T(8,128)(2,1)} fusion(f32[6,512,2048]{2,1,0:T(8,128)} %get-tuple-element.747, f32[6,512,2048]{2,1,0:T(8,128)} %fusion.221, f32[6,512]{1,0:T(8,128)S(1)} %get-tuple-element.748, f32[6,512]{1,0:T(8,128)S(1)} %dynamic-slice_bitcast_fusion.2, pred[512,2048]{1,0:T(8,128)(4,1)S(1)} %fusion.223), kind=kLoop, calls=%fused_computation.40.clone.1 | loop fusion | flops 37748736 | bytes 63987712 | tf_op jit(solution)/shard_map/while/body/eval_jaxpr/convert_element_type | solution.py:254
  958.8 21.3 %multiply_convert_fusion.4 = bf16[6,512,2048]{2,1,0:T(8,128)(2,1)} fusion(f32[6,512,2048]{2,1,0:T(8,128)} %get-tuple-element.747, f32[6,512,2048]{2,1,0:T(8,128)} %fusion.221, f32[6,512]{1,0:T(8,128)S(1)} %get-tuple-element.748, f32[6,512]{1,0:T(8,128)S(1)} %dynamic-slice_bitcast_fusion.2, pred[512,2048]{1,0:T(8,128)(4,1)S(1)} %fusion.223), kind=kLoop, calls=%fused_computation.40.clone.1 | loop fusion | flops 37748736 | bytes 63987712 | tf_op jit(solution)/shard_map/while/body/eval_jaxpr/convert_element_type | solution.py:254
  1064.1 21.3 %multiply_convert_fusion.4 = bf16[6,512,2048]{2,1,0:T(8,128)(2,1)} fusion(f32[6,512,2048]{2,1,0:T(8,128)} %get-tuple-element.747, f32[6,512,2048]{2,1,0:T(8,128)} %fusion.221, f32[6,512]{1,0:T(8,128)S(1)} %get-tuple-element.748, f32[6,512]{1,0:T(8,128)S(1)} %dynamic-slice_bitcast_fusion.2, pred[512,2048]{1,0:T(8,128)(4,1)S(1)} %fusion.223), kind=kLoop, calls=%fused_computation.40.clone.1 | loop fusion | flops 37748736 | bytes 63987712 | tf_op jit(solution)/shard_map/while/body/eval_jaxpr/convert_element_type | solution.py:254
  1169.4 21.3 %multiply_convert_fusion.4 = bf16[6,512,2048]{2,1,0:T(8,128)(2,1)} fusion(f32[6,512,2048]{2,1,0:T(8,128)} %get-tuple-element.747, f32[6,512,2048]{2,1,0:T(8,128)} %fusion.221, f32[6,512]{1,0:T(8,128)S(1)} %get-tuple-element.748, f32[6,512]{1,0:T(8,128)S(1)} %dynamic-slice_bitcast_fusion.2, pred[512,2048]{1,0:T(8,128)(4,1)S(1)} %fusion.223), kind=kLoop, calls=%fused_computation.40.clone.1 | loop fusion | flops 37748736 | bytes 63987712 | tf_op jit(solution)/shard_map/while/body/eval_jaxpr/convert_element_type | solution.py:254
  1280.1 39.5 %psum.7 = f32[4]{0:T(128)S(1)} all-reduce(f32[4]{0:T(128)S(1)} %pad_maximum_fusion.7), channel_id=1, replica_groups=mesh['dp'=16,'tensor'=2] {'dp','tensor'}, use_global_device_ids=true, to_apply=%region_29.30 | all-reduce | flops 4 | bytes 32 | tf_op jit(solution)/shard_map/psum | solution.py:218
  1392.4 65.7 %reduce-scatter.22.cloned.1.call-done = f32[48,1536]{1,0:T(8,128)} async-done(((f32[768,1536]{1,0:T(8,128)}), f32[48,1536]{1,0:T(8,128)}) %reduce-scatter.22.cloned.1.call-update) | async-done | bytes 294928 | tf_op jit(solution)/shard_map/reduce_scatter | solution.py:348
  1458.0 61.2 %reduce-scatter.20.cloned.1.call-done = f32[384,48]{0,1:T(8,128)} async-done(((f32[384,768]{0,1:T(8,128)}), f32[384,48]{0,1:T(8,128)}) %reduce-scatter.20.cloned.1.call-update) | async-done | bytes 73744 | tf_op jit(solution)/shard_map/reduce_scatter | solution.py:347
  1519.3 71.4 %reduce-scatter.18.cloned.1.call-done = f32[48,3,384]{2,0,1:T(8,128)} async-done(((f32[768,3,384]{2,0,1:T(8,128)}), f32[48,3,384]{2,0,1:T(8,128)}) %reduce-scatter.18.cloned.1.call-update) | async-done | bytes 221200 | tf_op jit(solution)/shard_map/reduce_scatter | solution.py:346
  1590.7 99.8 %reduce-scatter.26.cloned.1.call-done = f32[8,768]{1,0:T(8,128)} async-done(((f32[256,768]{1,0:T(8,128)}), f32[8,768]{1,0:T(8,128)}) %reduce-scatter.26.cloned.1.call-update) | async-done | bytes 24592 | tf_op jit(solution)/shard_map/reduce_scatter | solution.py:344
  (366 shorter events, 760.2 us)
Async XLA Ops:
  7.2 92.7 %copy-start = (bf16[768,144]{0,1:T(8,128)(2,1)S(1)}, bf16[768,144]{0,1:T(8,128)(2,1)}, u32[]{:S(2)}) copy-start(bf16[768,144]{0,1:T(8,128)(2,1)} %param.21) | copy-start | bytes 663556
  7.2 97.4 %copy-start.28 = (bf16[1024,768]{1,0:T(8,128)(2,1)S(1)}, bf16[1024,768]{1,0:T(8,128)(2,1)}, u32[]{:S(2)}) copy-start(bf16[1024,768]{1,0:T(8,128)(2,1)} %param.15) | copy-start | bytes 4718596
  31.8 67.4 %copy-start.51 = (s32[144]{0:T(256)}, s32[144]{0:T(256)S(1)}, u32[]{:S(2)}) copy-start(s32[144]{0:T(256)S(1)} %eq.103) | copy-start | bytes 1732
  101.0 10.8 all-to-all-start
  104.5 99.0 %all-gather.10.cloned.1.call-start = ((), (), s32[]{:S(2)}) async-start(), calls=%async_computation.12 | async-start | bytes 4718592 | tf_op jit(solution)/shard_map/all_gather | solution.py:140
  161.2 85.2 %all-gather.12.cloned.1.call-start = ((), (), s32[]{:S(2)}) async-start(), calls=%async_computation.13 | async-start | bytes 1880064 | tf_op jit(solution)/shard_map/all_gather | solution.py:110
  161.9 306.3 %reduce-scatter.10.cloned.1.call-start = ((), (), s32[]{:S(2)}) async-start(), calls=%async_computation.14 | async-start | bytes 4718592 | tf_op jit(solution)/shard_map/reduce_scatter | solution.py:187
  425.8 87.1 %all-gather.16.cloned.1.call-start = ((), (), s32[]{:S(2)}) async-start(), calls=%async_computation.16 | async-start | bytes 2506752 | tf_op jit(solution)/shard_map/all_gather | solution.py:116
  426.4 131.7 %all-gather.14.cloned.1.call-start = ((), (), s32[]{:S(2)}) async-start(), calls=%async_computation.15 | async-start | bytes 4718592 | tf_op jit(solution)/shard_map/all_gather | solution.py:195
  471.5 276.3 %copy-start.38 = (f32[1024]{0:T(1024)}, f32[1024]{0:T(1024)S(1)}, u32[]{:S(2)}) copy-start(f32[1024]{0:T(1024)S(1)} %broadcast_multiply_fusion) | copy-start | bytes 12292
  471.9 275.9 %copy-start.44 = (f32[1024]{0:T(1024)}, f32[1024]{0:T(1024)S(1)}, u32[]{:S(2)}) copy-start(f32[1024]{0:T(1024)S(1)} %fusion.136) | copy-start | bytes 12292
  479.6 123.1 %all-gather.18.cloned.1.call-start = ((), (), s32[]{:S(2)}) async-start(), calls=%async_computation.17 | async-start | bytes 2506752 | tf_op jit(solution)/shard_map/all_gather | solution.py:117
  480.2 168.5 %all-gather.20.cloned.1.call-start = ((), (), s32[]{:S(2)}) async-start(), calls=%async_computation.19 | async-start | bytes 4718592 | tf_op jit(solution)/shard_map/all_gather | solution.py:225
  480.9 213.4 %reduce-scatter.12.cloned.1.call-start = ((), (), s32[]{:S(2)}) async-start(), calls=%async_computation.18 | async-start | bytes 4718592 | tf_op jit(solution)/shard_map/reduce_scatter | solution.py:200
  611.8 128.1 %reduce-scatter.14.cloned.1.call-start = ((), (), s32[]{:S(2)}) async-start(), calls=%async_computation.20 | async-start | bytes 4718592 | tf_op jit(solution)/shard_map/reduce_scatter | solution.py:229
  673.0 128.7 %all-gather.22.cloned.1.call-start = ((), (), s32[]{:S(2)}) async-start(), calls=%async_computation.21 | async-start | bytes 4718592 | tf_op jit(solution)/shard_map/all_gather | solution.py:237
  756.6 576.0 %reduce-scatter.16.cloned.1.call-start = ((), (), s32[]{:S(2)}) async-start(), calls=%async_computation.22 | async-start | bytes 4718592 | tf_op jit(solution)/shard_map/reduce_scatter | solution.py:290
  1251.4 140.9 %reduce-scatter.24.cloned.1.call-start = ((), (), s32[]{:S(2)}) async-start(), calls=%async_computation.26 | async-start | bytes 5013504 | tf_op jit(solution)/shard_map/reduce_scatter | solution.py:349
  1261.0 197.0 %reduce-scatter.22.cloned.1.call-start = ((), (), s32[]{:S(2)}) async-start(), calls=%async_computation.25 | async-start | bytes 5013504 | tf_op jit(solution)/shard_map/reduce_scatter | solution.py:348
  1270.6 248.6 %reduce-scatter.20.cloned.1.call-start = ((), (), s32[]{:S(2)}) async-start(), calls=%async_computation.24 | async-start | bytes 1253376 | tf_op jit(solution)/shard_map/reduce_scatter | solution.py:347
  1276.8 313.9 %reduce-scatter.18.cloned.1.call-start = ((), (), s32[]{:S(2)}) async-start(), calls=%async_computation.23 | async-start | bytes 3760128 | tf_op jit(solution)/shard_map/reduce_scatter | solution.py:346
  1354.2 15.8 all-to-all-start.1
  1370.8 8.0 all-to-all-start.2
  1374.2 316.3 %reduce-scatter.26.cloned.1.call-start = ((), (), s32[]{:S(2)}) async-start(), calls=%async_computation.27 | async-start | bytes 811008 | tf_op jit(solution)/shard_map/reduce_scatter | solution.py:344
  (58 other events, 668.3 us)
Sparse Core Ops, SparseCore 0:
  161.3 42.2 all-gather.9
  205.9 40.4 all-gather.11
  425.9 42.2 reduce-scatter.9
  470.6 42.2 all-gather.15
  514.3 43.6 all-gather.13
  560.5 42.2 all-gather.17
  604.9 43.7 all-gather.19
  651.0 43.3 reduce-scatter.11
  696.6 43.3 reduce-scatter.13
  756.7 44.9 all-gather.21
  1251.6 43.8 reduce-scatter.15
  1299.7 78.1 reduce-scatter.23
  1382.8 75.1 reduce-scatter.21
  1462.1 57.1 reduce-scatter.19
  1523.6 67.0 reduce-scatter.17
  1596.2 94.2 reduce-scatter.25
where the time goes:
time: 1700 us
  waiting for transfers between devices  648 us (38%)
  matrix products  477 us (28%)
  other arithmetic  220 us (13%)
  blocking collectives  180 us (11%)
  local copies, waits for them, and re-layouts  129 us (8%)
    reduce_scatter x1, waiting for transfers between devices, body(): lax.psum_scatter(table_part, ('dp', 'tensor'), scatter_dimension=0, tiled...  99.8 us
    dot_general x8, matrix products, block_scores(): jnp.einsum('qhd,khd->hqk', query_blk, keys_rot, preferred_element_type=jn...  90.7 us
    convert_element_type x4, other arithmetic, backward_block(): score_grad = (probability * (prob_grad - centre)).astype(jnp.bfloat16)  85.4 us
    dot_general x4, matrix products, backward_block(): jnp.einsum('qhd,khd->hqk', grad_blk, value_blk, preferred_element_type=jn...  72.7 us
    reduce_scatter x1, waiting for transfers between devices, body(): lax.psum_scatter(qkv_grad, 'dp', scatter_dimension=0, tiled=True)  71.4 us
    dynamic_update_slice x8, local copies, waits for them, and re-layouts, body(): lax.map(forward_block, jnp.arange(block_count, dtype=jnp.int32))  67.5 us
    all_gather x1, blocking collectives, body(): lax.all_gather(time_table, ('dp', 'tensor'), axis=0, tiled=True)  67.2 us
    reduce_scatter x1, waiting for transfers between devices, body(): lax.psum_scatter(up_grad, 'dp', scatter_dimension=0, tiled=True)  65.7 us
  transfers between devices with their start and end apart: 19, of which 17 were waited for; matrix products, arithmetic and copies ran while one was open for 9% of the time, Pallas kernels for 0%

commit v1 on v0

v1 whole, which is shorter than its diff:
```python
import math

import jax
import jax.numpy as jnp
from jax import lax
from jax.experimental import pallas as pl
from jax.experimental.pallas import tpu as pltpu
from jax.sharding import PartitionSpec as P

HEAD_DIM = 64
PROMPT = 1024
CONT = 128
NCONT = 8
STEPS = 256
SEGS = 1 + NCONT

bf16 = jnp.bfloat16
f32 = jnp.float32
NN = (((1,), (0,)), ((), ()))
NT = (((1,), (1,)), ((), ()))
TN = (((0,), (0,)), ((), ()))
SCALE = HEAD_DIM ** (-0.5)
SCALE2 = SCALE * math.log2(math.e)
NEG = -1e30


def dot(left, right, dims=NN):
    return lax.dot_general(left, right, dims, preferred_element_type=f32)


def lanes(shape):
    return lax.broadcasted_iota(jnp.int32, shape, 1)


def rows(shape):
    return lax.broadcasted_iota(jnp.int32, shape, 0)


def swap(x, axis, bit):
    count = lax.axis_size(axis)
    return lax.ppermute(x, axis, [(i, i ^ bit) for i in range(count)])


def dp_bits():
    count = lax.axis_size("dp")
    return [1 << k for k in reversed(range(count.bit_length() - 1))]


def bit_of(index, bit):
    return (index // bit) % 2


def join_halves(own, other, mine, axis):
    low = jnp.where(mine == 0, own, other)
    high = jnp.where(mine == 0, other, own)
    return jnp.stack([low, high], axis)


def gather_weights(piece, swap_first):
    me = lax.axis_index("dp")
    bits = dp_bits()
    cur, other, axis = piece, None, 0
    for bit in bits[:-2]:
        cur = join_halves(cur, swap(cur, "dp", bit), bit_of(me, bit), axis)
        axis += 1
    if swap_first:
        cur = jnp.stack([cur, swap(cur, "tensor", 1)], 0)
        for bit in bits[-2:]:
            cur = join_halves(cur, swap(cur, "dp", bit), bit_of(me, bit), axis + 1)
            axis += 1
    else:
        bit = bits[-2]
        cur = join_halves(cur, swap(cur, "dp", bit), bit_of(me, bit), axis)
        axis += 1
        cur = jnp.stack([cur, swap(cur, "tensor", 1)], 0)
        bit = bits[-1]
        cur = join_halves(cur, swap(cur, "dp", bit), bit_of(me, bit), axis + 1)
    cur = cur.reshape(2, -1, piece.shape[-1])
    return cur[0], cur[1]


def scatter_grads(mine, other, swap_first):
    me = lax.axis_index("dp")
    bits = dp_bits()
    columns = mine.shape[-1]
    cur = jnp.stack([mine, other], 0).astype(bf16)
    cur = cur.reshape((2,) + (2,) * len(bits) + (-1, columns))

    def halve(cur, bit, axis):
        b = bit_of(me, bit)
        keep = lax.dynamic_index_in_dim(cur, b, axis, keepdims=False)
        send = lax.dynamic_index_in_dim(cur, 1 - b, axis, keepdims=False)
        return keep.astype(f32) + swap(send, "dp", bit).astype(f32)

    order = list(reversed(bits))
    cur = halve(cur, order[0], len(bits)).astype(bf16)
    if swap_first:
        cur = (cur[0].astype(f32) + swap(cur[1], "tensor", 1).astype(f32)).astype(bf16)
        cur = halve(cur, order[1], len(bits) - 2).astype(bf16)
    else:
        cur = halve(cur, order[1], len(bits) - 1).astype(bf16)
        cur = (cur[0].astype(f32) + swap(cur[1], "tensor", 1).astype(f32)).astype(bf16)
    axis = len(bits) - 3
    for bit in order[2:]:
        total = halve(cur, bit, axis)
        cur = total.astype(bf16)
        axis -= 1
    return total


def turn(x, cosine, sine):
    lane = lanes(x.shape) % 64
    swapped = jnp.where(lane < 32, -pltpu.roll(x, 96, 1), pltpu.roll(x, 32, 1))
    return x * cosine + swapped * sine


def turn_back(x, cosine, sine):
    lane = lanes(x.shape) % 64
    swapped = jnp.where(lane < 32, pltpu.roll(x, 96, 1), -pltpu.roll(x, 32, 1))
    return x * cosine + swapped * sine


def project_kernel(turned, x_ref, w_ref, cos_ref, sin_ref, out_ref):
    joined = dot(x_ref[...], w_ref[...])
    part = pl.program_id(0)

    @pl.when(part < turned)
    def _():
        for c in range(joined.shape[1] // 128):
            cut = slice(c * 128, (c + 1) * 128)
            out_ref[:, cut] = turn(joined[:, cut], cos_ref[...], sin_ref[...]).astype(bf16)

    @pl.when(part >= turned)
    def _():
        out_ref[...] = joined.astype(bf16)


def project(x, w, cosine, sine, first, turned):
    count, width = x.shape
    head_width = w.shape[1] // 3
    parts = 3 - first
    whole = pl.BlockSpec((count, 128), lambda p: (0, 0))
    return pl.pallas_call(
        lambda *refs: project_kernel(turned, *refs),
        grid=(parts,),
        in_specs=[
            pl.BlockSpec((count, width), lambda p: (0, 0)),
            pl.BlockSpec((width, head_width), lambda p: (0, p + first)),
            whole,
            whole,
        ],
        out_specs=pl.BlockSpec((count, head_width), lambda p: (0, p)),
        out_shape=jax.ShapeDtypeStruct((count, parts * head_width), bf16),
        compiler_params=pltpu.CompilerParams(vmem_limit_bytes=32 * 2**20),
        cost_estimate=pl.CostEstimate(
            flops=2 * count * width * parts * head_width,
            bytes_accessed=2 * (count * width + parts * head_width * (count + width)),
            transcendentals=0,
        ),
        name="project",
    )(x, w, cosine, sine)


def forward_kernel(info, q_ref, kp_ref, vp_ref, ko_ref, vo_ref, o_ref, lse_ref):
    role = info[0]
    prompt_count = info[1]
    count = q_ref.shape[0]
    lane = lanes((count, 128))
    row = rows((count, 128))
    tile = 256
    blocks = count // tile

    def prepare(h):
        sel = (lane // 64) == h
        extra = 64 * (1 - h)
        q = jnp.where(sel, q_ref[...], jnp.where(lane == extra, 1.0, 0.0).astype(bf16))
        bias = jnp.where((lane == extra) & (row >= prompt_count), NEG, 0.0).astype(bf16)
        k = jnp.where(sel, kp_ref[...], bias)
        v = jnp.where(sel, vp_ref[...], jnp.ones((), bf16))
        return sel, q, k, v

    def finish(h, i, o, top):
        extra = 64 * (1 - h)
        weight = o[:, extra : extra + 1]
        lse = top * SCALE2 + jnp.log2(weight)
        turned = jnp.transpose(jnp.broadcast_to(lse, (tile, 128)))
        lse_ref[0, h : h + 1, i * tile : (i + 1) * tile] = turned[0:1, :]
        return o * (1.0 / weight)

    def store(outs):
        for i in range(blocks):
            merged = jnp.where(lanes((tile, 128)) < 64, outs[0][i], outs[1][i])
            o_ref[i * tile : (i + 1) * tile, :] = merged.astype(bf16)

    @pl.when(role == 0)
    def _():
        outs = []
        for h in range(2):
            sel, q, k, v = prepare(h)
            heads = []
            for i in range(blocks):
                start, stop = i * tile, (i + 1) * tile
                s = dot(q[start:stop], k[:stop], NT)
                near = jnp.where(lanes((tile, tile)) <= rows((tile, tile)), s[:, start:], NEG)
                top = jnp.max(near, 1, keepdims=True)
                if i:
                    top = jnp.maximum(top, jnp.max(s[:, :start], 1, keepdims=True))
                o = dot(jnp.exp2(near * SCALE2 - top * SCALE2).astype(bf16), v[start:stop])
                if i:
                    o = o + dot(
                        jnp.exp2(s[:, :start] * SCALE2 - top * SCALE2).astype(bf16), v[:start]
                    )
                heads.append(finish(h, i, o, top))
            outs.append(heads)
        store(outs)

    @pl.when(role != 0)
    def _():
        outs = []
        for h in range(2):
            sel, q, k, v = prepare(h)
            own_k = jnp.where(sel, ko_ref[...], jnp.zeros((), bf16))
            own_v = jnp.where(sel, vo_ref[...], jnp.ones((), bf16))
            heads = []
            for i in range(blocks):
                start, stop = i * tile, (i + 1) * tile
                s = dot(q[start:stop], k, NT)
                cuts = [slice(r, r + CONT) for r in range(start, stop, CONT)]
                near = []
                for cut in cuts:
                    piece = dot(q[cut], own_k[cut], NT)
                    col, line = lanes((CONT, CONT)), rows((CONT, CONT))
                    fine = (col <= line) & (col < info[2 + cut.start // CONT])
                    near.append(jnp.where(fine, piece, NEG))
                near = jnp.concatenate(near, 0)
                top = jnp.maximum(
                    jnp.max(s, 1, keepdims=True), jnp.max(near, 1, keepdims=True)
                )
                far_weight = jnp.exp2(s * SCALE2 - top * SCALE2).astype(bf16)
                near_weight = jnp.exp2(near * SCALE2 - top * SCALE2).astype(bf16)
                own = [
                    dot(near_weight[n * CONT : (n + 1) * CONT], own_v[cut])
                    for n, cut in enumerate(cuts)
                ]
                heads.append(finish(h, i, dot(far_weight, v) + jnp.concatenate(own, 0), top))
            outs.append(heads)
        store(outs)


def attend(info, joined, prompt):
    count = joined.shape[0]
    head_width = joined.shape[1] // 3
    pairs = head_width // 128

    def spec(offset):
        return pl.BlockSpec((count, 128), lambda h, s: (0, offset + h))

    return pl.pallas_call(
        forward_kernel,
        grid_spec=pltpu.PrefetchScalarGridSpec(
            num_scalar_prefetch=1,
            grid=(pairs,),
            in_specs=[spec(0), spec(0), spec(pairs), spec(pairs), spec(2 * pairs)],
            out_specs=[spec(0), pl.BlockSpec((1, 2, count), lambda h, s: (h, 0, 0))],
        ),
        out_shape=[
            jax.ShapeDtypeStruct((count, head_width), bf16),
            jax.ShapeDtypeStruct((pairs, 2, count), f32),
        ],
        compiler_params=pltpu.CompilerParams(vmem_limit_bytes=40 * 2**20),
        cost_estimate=pl.CostEstimate(
            flops=18 * count * count * 128 * pairs * 2,
            bytes_accessed=8 * count * head_width * 2,
            transcendentals=2 * pairs * count * count,
        ),
        name="attend",
    )(info, joined, prompt, prompt, joined, joined)


def backward_kernel(
    info,
    q_ref,
    do_ref,
    o_ref,
    lse_ref,
    kp_ref,
    vp_ref,
    ko_ref,
    vo_ref,
    co_ref,
    so_ref,
    cp_ref,
    sp_ref,
    dq_ref,
    dko_ref,
    dvo_ref,
    dkp_ref,
    dvp_ref,
    dq_acc,
):
    role = info[0]
    prompt_count = info[1]
    count = q_ref.shape[0]
    tile = 256
    lane = lanes((count, 128))
    none = jnp.zeros((), bf16)
    products = jnp.transpose(do_ref[...].astype(f32) * o_ref[...].astype(f32))
    deltas = [jnp.sum(products[64 * h : 64 * h + 64], 0, keepdims=True) for h in range(2)]

    def far_block(j, first):
        start, stop = j * tile, (j + 1) * tile
        cut = slice(start, stop)
        q_from = start if first else 0
        lane_k = lanes((tile, 128))
        row_k = rows((tile, 128)) + start
        key_parts, value_parts = [], []
        for h in range(2):
            extra = 64 * (1 - h)
            sel = (lane_k // 64) == h
            bias = jnp.where((lane_k == extra) & (row_k >= prompt_count), NEG, 0.0).astype(bf16)
            k = jnp.where(sel, kp_ref[cut, :], bias)
            k_plain = jnp.where(sel, kp_ref[cut, :], none)
            v = jnp.where(sel, vp_ref[cut, :], none)
            lane_q = lane[q_from:]
            ones = jnp.where(lane_q == extra, 1.0, 0.0).astype(bf16)
            q = jnp.where((lane_q // 64) == h, q_ref[q_from:, :], ones)
            s = dot(k, q, NT)
            if first:
                near = jnp.where(rows((tile, tile)) <= lanes((tile, tile)), s[:, :tile], NEG)
                s = jnp.concatenate([near, s[:, tile:]], 1) if stop < count else near
            weight = jnp.exp2(s * SCALE2 - lse_ref[0, h : h + 1, q_from:])
            grad = dot(v, do_ref[q_from:, :], NT)
            score = (weight * (grad - deltas[h][:, q_from:])).astype(bf16)
            value_parts.append(dot(weight.astype(bf16), do_ref[q_from:, :]))
            key_parts.append(dot(score, q_ref[q_from:, :]))
            query_part = dot(score, k_plain, TN)
            if j == 0 and h == 0:
                dq_acc[...] = query_part
            else:
                dq_acc[q_from:, :] += query_part
        key_grad = jnp.where(lane_k < 64, key_parts[0], key_parts[1]) * SCALE
        value_grad = jnp.where(lane_k < 64, value_parts[0], value_parts[1])
        dkp_ref[cut, :] = turn_back(key_grad, cp_ref[cut, :], sp_ref[cut, :]).astype(bf16)
        dvp_ref[cut, :] = value_grad.astype(bf16)

    @pl.when(role == 0)
    def _():
        for j in range(count // tile):
            far_block(j, True)
        dko_ref[...] = jnp.zeros_like(dko_ref)
        dvo_ref[...] = jnp.zeros_like(dvo_ref)

    @pl.when(role != 0)
    def _():
        for j in range(count // tile):
            far_block(j, False)
        lane_k = lanes((CONT, CONT))
        row_k = rows((CONT, CONT))
        for i in range(count // CONT):
            cut = slice(i * CONT, (i + 1) * CONT)
            key_parts, value_parts, query_part = [], [], None
            for h in range(2):
                sel = (lane_k // 64) == h
                k = jnp.where(sel, ko_ref[cut, :], none)
                v = jnp.where(sel, vo_ref[cut, :], none)
                fine = (row_k <= lane_k) & (row_k < info[2 + i])
                s = jnp.where(fine, dot(k, q_ref[cut, :], NT), NEG)
                weight = jnp.exp2(s * SCALE2 - lse_ref[0, h : h + 1, cut])
                grad = dot(v, do_ref[cut, :], NT)
                score = (weight * (grad - deltas[h][:, cut])).astype(bf16)
                value_parts.append(dot(weight.astype(bf16), do_ref[cut, :]))
                key_parts.append(dot(score, q_ref[cut, :]))
                part = dot(score, k, TN)
                query_part = part if query_part is None else query_part + part
            dq_acc[cut, :] += query_part
            key_grad = jnp.where(lane_k < 64, key_parts[0], key_parts[1]) * SCALE
            value_grad = jnp.where(lane_k < 64, value_parts[0], value_parts[1])
            dko_ref[cut, :] = turn_back(key_grad, co_ref[cut, :], so_ref[cut, :]).astype(bf16)
            dvo_ref[cut, :] = value_grad.astype(bf16)

    dq_ref[...] = turn_back(dq_acc[...] * SCALE, co_ref[...], so_ref[...]).astype(bf16)


def attend_back(info, joined, prompt, grad, out, lse, tables):
    count = joined.shape[0]
    head_width = joined.shape[1] // 3
    pairs = head_width // 128

    def spec(offset):
        return pl.BlockSpec((count, 128), lambda h, s: (0, offset + h))

    table = pl.BlockSpec((count, 128), lambda h, s: (0, 0))
    return pl.pallas_call(
        backward_kernel,
        grid_spec=pltpu.PrefetchScalarGridSpec(
            num_scalar_prefetch=1,
            grid=(pairs,),
            in_specs=[
                spec(0),
                spec(0),
                spec(0),
                pl.BlockSpec((1, 2, count), lambda h, s: (h, 0, 0)),
                spec(0),
                spec(pairs),
                spec(pairs),
                spec(2 * pairs),
                table,
                table,
                table,
                table,
            ],
            out_specs=[spec(0)] * 5,
            scratch_shapes=[pltpu.VMEM((count, 128), f32)],
        ),
        out_shape=[jax.ShapeDtypeStruct((count, head_width), bf16)] * 5,
        compiler_params=pltpu.CompilerParams(vmem_limit_bytes=48 * 2**20),
        cost_estimate=pl.CostEstimate(
            flops=40 * count * count * 128 * pairs * 2,
            bytes_accessed=14 * count * head_width * 2,
            transcendentals=2 * pairs * count * count,
        ),
        name="attend_back",
    )(info, joined, grad, out, lse, prompt, prompt, joined, joined, *tables)


def norm_parts(inputs):
    average = jnp.mean(inputs, -1, keepdims=True)
    centred = inputs - average
    spread = jnp.mean(centred * centred, -1, keepdims=True)
    inverse = lax.rsqrt(spread + 1e-05)
    return centred * inverse, inverse


def norm_back(unit, inverse, grad, scales):
    inner = grad * (1.0 + scales)
    first = jnp.mean(inner, -1, keepdims=True)
    second = jnp.mean(inner * unit, -1, keepdims=True)
    return inverse * (inner - first - unit * second)


def split_three(values):
    high = lax.reduce_precision(values, 8, 7)
    rest = values - high
    mid = lax.reduce_precision(rest, 8, 7)
    return high, mid, rest - mid


def body(
    block_input,
    cotangent,
    w_qkv,
    w_out,
    w_up,
    w_down,
    w_mod,
    time_table,
    prompt_len,
    cont_len,
    timestep,
):
    count, width = block_input.shape
    tiles = count // CONT
    dp_count = lax.axis_size("dp")
    tensor_count = lax.axis_size("tensor")
    devices = dp_count * tensor_count
    both = ("dp", "tensor")
    role = lax.axis_index("tensor")
    is_prompt = role == 0

    qkv_piece = w_qkv.reshape(w_qkv.shape[0], -1)
    head_width = w_qkv.shape[2]
    hidden_width = w_up.shape[1]
    cut_qkv = 640
    rest_a = jnp.concatenate([w_out.T, w_up], 1)
    rest_b = w_down.T
    qkv_a = gather_weights(qkv_piece[:, :cut_qkv], True)
    qkv_b = gather_weights(qkv_piece[:, cut_qkv:], False)
    qkv = [jnp.concatenate([qkv_a[t], qkv_b[t]], 1) for t in range(2)]

    steps = jnp.pad(timestep.reshape(1, -1), ((0, 0), (0, width - SEGS))).astype(bf16)
    packet = jnp.concatenate([time_table, steps], 0)
    table_rows = time_table.shape[0]
    packet = jnp.pad(packet, ((0, 16 - packet.shape[0]), (0, 0)))
    packets = lax.all_to_all(
        jnp.broadcast_to(packet[None], (devices,) + packet.shape), both, 0, 0, tiled=True
    )
    table_full = packets[:, :table_rows].reshape(STEPS, width)
    step_rows = packets[::tensor_count, table_rows, :SEGS].astype(jnp.int32)
    step_pad = jnp.pad(step_rows, ((0, 0), (0, 16 - SEGS))).reshape(-1)
    pick = (step_pad[:, None] == jnp.arange(STEPS, dtype=jnp.int32)[None, :]).astype(bf16)
    cond = dot(pick, table_full).astype(bf16)
    col_width = w_mod.shape[1]
    col_part = dot(cond, w_mod).reshape(dp_count, 1, 16, col_width)
    col_part = jnp.broadcast_to(col_part, (dp_count, tensor_count, 16, col_width))
    arrived = lax.all_to_all(
        col_part.reshape(devices, 16, col_width), both, 0, 0, tiled=True
    )
    modulate = jnp.transpose(arrived, (1, 0, 2)).reshape(16, 6, width)
    prompt_mod = modulate[0]
    mods = jnp.where(
        is_prompt, jnp.broadcast_to(modulate[0:1], (tiles, 6, width)), modulate[1 : 1 + tiles]
    )
    mods = [mods[:, n][:, None, :] for n in range(6)]

    prompt_rows = jnp.where(is_prompt, block_input, swap(block_input, "tensor", 1))

    half = HEAD_DIM // 2
    freqs = 10000.0 ** (-(jnp.arange(128, dtype=jnp.int32) % half).astype(f32) / half)
    inside = jnp.arange(count, dtype=jnp.int32)
    prompt_count = prompt_len[0]
    own_places = jnp.where(is_prompt, inside, prompt_count + inside % CONT).astype(f32)
    own_angles = own_places[:, None] * freqs[None, :]
    prompt_angles = inside.astype(f32)[:, None] * freqs[None, :]
    own_cos, own_sin = jnp.cos(own_angles), jnp.sin(own_angles)
    prompt_cos, prompt_sin = jnp.cos(prompt_angles), jnp.sin(prompt_angles)
    own_len = jnp.where(
        is_prompt,
        jnp.clip(prompt_count - CONT * jnp.arange(NCONT, dtype=jnp.int32), 0, CONT),
        cont_len[0],
    )
    info = jnp.concatenate([jnp.stack([role, prompt_count]), own_len]).astype(jnp.int32)
    valid = (inside % CONT < own_len[inside // CONT]).astype(f32).reshape(tiles, CONT, 1)

    inputs = block_input.astype(f32).reshape(tiles, CONT, width)
    unit_one, inverse_one = norm_parts(inputs)
    normed = (unit_one * (1.0 + mods[1]) + mods[0]).astype(bf16).reshape(count, width)
    prompt_unit, _ = norm_parts(prompt_rows.astype(f32))
    prompt_normed = (prompt_unit * (1.0 + prompt_mod[1]) + prompt_mod[0]).astype(bf16)
    joined, prompts, attended, lses = [], [], [], []
    for t in range(2):
        joined.append(project(normed, qkv[t], own_cos, own_sin, 0, 2))
        prompts.append(project(prompt_normed, qkv[t], prompt_cos, prompt_sin, 1, 1))
        out, lse = attend(info, joined[t], prompts[t])
        attended.append(out)
        lses.append(lse)

    part_a = gather_weights(rest_a, True)
    down_t = gather_weights(rest_b, False)
    out_t = [part[:, :head_width] for part in part_a]
    up = [part[:, head_width:] for part in part_a]

    attn_branch = dot(attended[0], out_t[0], NT) + dot(attended[1], out_t[1], NT)
    attn_branch = attn_branch.reshape(tiles, CONT, width)
    attn_part = mods[2] * attn_branch
    middle = inputs + attn_part
    unit_two, inverse_two = norm_parts(middle)
    normed_two = (unit_two * (1.0 + mods[4]) + mods[3]).astype(bf16).reshape(count, width)

    hidden, slope = [], []
    for t in range(2):
        pre_act = dot(normed_two, up[t])
        cdf = 0.5 * (1.0 + lax.erf(pre_act * (2.0**-0.5)))
        pdf = jnp.exp(-0.5 * pre_act * pre_act) * ((2.0 * math.pi) ** -0.5)
        hidden.append((pre_act * cdf).astype(bf16))
        slope.append((cdf + pre_act * pdf).astype(bf16))
    mlp_branch = dot(hidden[0], down_t[0], NT) + dot(hidden[1], down_t[1], NT)
    mlp_branch = mlp_branch.reshape(tiles, CONT, width)
    mlp_part = mods[5] * mlp_branch
    result = middle + mlp_part

    upstream = cotangent.astype(f32).reshape(tiles, CONT, width)
    mlp_grad = (upstream * mods[5]).astype(bf16).reshape(count, width)
    gate_two_grad = jnp.sum(upstream * mlp_branch, 1)
    down_grads = [dot(mlp_grad, hidden[t], TN).astype(bf16) for t in range(2)]
    pre_grad = [(dot(mlp_grad, down_t[t]) * slope[t].astype(f32)).astype(bf16) for t in range(2)]
    up_grads = [dot(normed_two, pre_grad[t], TN).astype(bf16) for t in range(2)]
    normed_two_grad = dot(pre_grad[0], up[0], NT) + dot(pre_grad[1], up[1], NT)
    normed_two_grad = normed_two_grad.reshape(tiles, CONT, width)
    shift_two_grad = jnp.sum(normed_two_grad, 1)
    scale_two_grad = jnp.sum(normed_two_grad * unit_two, 1)
    middle_grad = upstream + norm_back(unit_two, inverse_two, normed_two_grad, mods[4])
    attn_grad = (middle_grad * mods[2]).astype(bf16).reshape(count, width)
    gate_one_grad = jnp.sum(middle_grad * attn_branch, 1)
    out_grads = [dot(attn_grad, attended[t], TN).astype(bf16) for t in range(2)]

    down_grad = scatter_grads(down_grads[0], down_grads[1], False)
    part_grad = scatter_grads(
        jnp.concatenate([out_grads[0], up_grads[0]], 1),
        jnp.concatenate([out_grads[1], up_grads[1]], 1),
        True,
    )
    out_grad = part_grad[:, :head_width]
    up_grad = part_grad[:, head_width:]

    tables = (own_cos, own_sin, prompt_cos, prompt_sin)
    prompt_sum, own_sum, qkv_grads = None, None, []
    for t in range(2):
        attended_grad = dot(attn_grad, out_t[t]).astype(bf16)
        dq, dk, dv, dk_prompt, dv_prompt = attend_back(
            info, joined[t], prompts[t], attended_grad, attended[t], lses[t], tables
        )
        wq, wk, wv = (qkv[t][:, n * head_width : (n + 1) * head_width] for n in range(3))
        prompt_part = dot(dk_prompt, wk, NT) + dot(dv_prompt, wv, NT)
        own_part = dot(dq, wq, NT) + dot(dk, wk, NT) + dot(dv, wv, NT)
        prompt_sum = prompt_part if t == 0 else prompt_sum + prompt_part
        own_sum = own_part if t == 0 else own_sum + own_part
        qkv_grads.append(
            jnp.concatenate(
                [
                    dot(normed, dq, TN),
                    dot(normed, dk, TN) + dot(prompt_normed, dk_prompt, TN),
                    dot(normed, dv, TN) + dot(prompt_normed, dv_prompt, TN),
                ],
                1,
            ).astype(bf16)
        )
    arrived_prompt = swap(prompt_sum.astype(bf16), "tensor", 1)
    normed_grad = own_sum + jnp.where(is_prompt, prompt_sum + arrived_prompt.astype(f32), 0.0)
    normed_grad = normed_grad.reshape(tiles, CONT, width)
    qkv_grad = jnp.concatenate(
        [
            scatter_grads(qkv_grads[0][:, :cut_qkv], qkv_grads[1][:, :cut_qkv], True),
            scatter_grads(qkv_grads[0][:, cut_qkv:], qkv_grads[1][:, cut_qkv:], False),
        ],
        1,
    )

    shift_one_grad = jnp.sum(normed_grad, 1)
    scale_one_grad = jnp.sum(normed_grad * unit_one, 1)
    input_grad = middle_grad + norm_back(unit_one, inverse_one, normed_grad, mods[1])

    sums = jnp.stack(
        [
            shift_one_grad,
            scale_one_grad,
            gate_one_grad,
            shift_two_grad,
            scale_two_grad,
            gate_two_grad,
        ],
        1,
    ).reshape(tiles, 6 * width)
    first_row = (jnp.arange(tiles) == 0)[:, None]
    prompt_sums = jnp.where(first_row, jnp.sum(sums, 0, keepdims=True), 0.0)
    segment_sums = jnp.where(is_prompt, prompt_sums, sums).astype(bf16)

    local = jnp.stack(
        [
            jnp.sum(valid * result * result),
            jnp.sum(valid * attn_part * attn_part),
            jnp.sum(valid * mlp_part * mlp_part),
            jnp.sum(valid) * width,
        ]
    )
    local = jnp.concatenate(split_three(local))
    local = jnp.pad(local, (0, col_width - 12)).astype(bf16)
    packet = segment_sums.reshape(tiles, devices, col_width).transpose(1, 0, 2)
    packet = jnp.concatenate(
        [packet, jnp.broadcast_to(local[None, None], (devices, 1, col_width))], 1
    )
    packet = jnp.pad(packet, ((0, 0), (0, 16 - packet.shape[1]), (0, 0)))
    packets = lax.all_to_all(packet, both, 0, 0, tiled=True)
    totals = jnp.sum(packets[:, tiles, :12].astype(f32), 0)
    totals = totals[:4] + totals[4:8] + totals[8:12]
    stats = jnp.sqrt(totals[:3] / totals[3])

    grads = packets[:, :tiles].reshape(devices * tiles, col_width)
    cond_groups = cond.reshape(dp_count, 16, width)
    own_steps = step_pad.reshape(dp_count, 16)
    cond_rows = jnp.stack([cond_groups[:, :tiles], cond_groups[:, 1 : 1 + tiles]], 1)
    step_slots = jnp.stack([own_steps[:, :tiles], own_steps[:, 1 : 1 + tiles]], 1).reshape(-1)
    mod_grad = dot(cond_rows.reshape(devices * tiles, width), grads, TN)
    condition_grad = dot(grads, w_mod, NT)
    slot_pick = (step_slots[:, None] == jnp.arange(STEPS, dtype=jnp.int32)[None, :]).astype(f32)
    table_part = lax.dot_general(
        slot_pick,
        condition_grad,
        TN,
        precision=lax.Precision.HIGHEST,
        preferred_element_type=f32,
    )
    table_pieces = lax.all_to_all(
        table_part.reshape(devices, table_rows, width), both, 0, 0, tiled=True
    )
    table_grad = jnp.sum(table_pieces, 0)
    return (
        result.reshape(count, width).astype(bf16),
        input_grad.reshape(count, width),
        qkv_grad.reshape(w_qkv.shape),
        out_grad.T,
        up_grad,
        down_grad.T,
        mod_grad,
        table_grad,
        stats,
    )


def solution(mesh):
    return jax.shard_map(
        body,
        mesh=mesh,
        in_specs=(
            P(("dp", "tensor"), None),
            P(("dp", "tensor"), None),
            P("dp", None, "tensor"),
            P("tensor", "dp"),
            P("dp", "tensor"),
            P("tensor", "dp"),
            P(None, ("dp", "tensor")),
            P(("dp", "tensor"), None),
            P("dp"),
            P("dp", None),
            P("dp", None),
        ),
        out_specs=(
            P(("dp", "tensor"), None),
            P(("dp", "tensor"), None),
            P("dp", None, "tensor"),
            P("tensor", "dp"),
            P("dp", "tensor"),
            P("tensor", "dp"),
            P(None, ("dp", "tensor")),
            P(("dp", "tensor"), None),
            P(),
        ),
        check_vma=False,
    )
```

time: 1700 us -> 613 us (0.36)
  waiting for transfers between devices: 648 us -> 154 us
  matrix products: 477 us -> 127 us
  blocking collectives: 180 us -> 0 us
  other arithmetic: 220 us -> 90.8 us
  starting transfers between devices: 13 us -> 109 us
  local copies, waits for them, and re-layouts: 129 us -> 46.3 us
  Pallas kernels: 0 us -> 75.9 us
    reduce_scatter x9 -> x0, waiting for transfers between devices: 405 us -> none  [the longest x1 99.8 us: body(): lax.psum_scatter(table_part, ('dp', 'tensor'), scatter_dimension=0, tiled...]
    dot_general x49 -> x43, matrix products: 477 us -> 127 us  [the longest x42 125 us: dot(): return lax.dot_general(left, right, dims, preferred_element_type=f32)]
    all_gather x7 -> x0, waiting for transfers between devices: 227 us -> none  [the longest x1 45.2 us: body(): normed_two_all = lax.all_gather(normed_two, 'tensor', axis=0, tiled=True)]
    all_gather x4 -> x0, blocking collectives: 141 us -> none  [the longest x1 67.2 us: body(): lax.all_gather(time_table, ('dp', 'tensor'), axis=0, tiled=True)]
    ppermute x0 -> x42, waiting for transfers between devices: none -> 132 us  [swap(): return lax.ppermute(x, axis, [(i, i ^ bit) for i in range(count)])]
    ppermute x0 -> x42, starting transfers between devices: none -> 88.8 us  [swap(): return lax.ppermute(x, axis, [(i, i ^ bit) for i in range(count)])]
    convert_element_type x9 -> x24, other arithmetic: 99.1 us -> 20.2 us  [the longest x4 5.56 us: scatter_grads(): cur = halve(cur, order[0], len(bits)).astype(bf16)]
    pallas_call x0 -> x8, Pallas kernels: none -> 75.9 us  [the longest x2 33.8 us: attend_back(): pl.pallas_call(backward_kernel, grid_spec=pltpu.PrefetchScalarGridSpec(nu...]
  transfers between devices with their start and end apart: 19 -> 46, of which waited for: 17 -> 18; matrix products, arithmetic and copies ran while one was open for 9% -> 19% of each run, Pallas kernels for 0% -> 7%
where the time goes in v1:
time: 613 us; the launch traced here: 607 us
  waiting for transfers between devices  154 us (25%)
  matrix products  127 us (21%)
  starting transfers between devices  109 us (18%)
  other arithmetic  90.8 us (15%)
  Pallas kernels  75.9 us (12%)
  local copies, waits for them, and re-layouts  46.3 us (8%)
    ppermute x42, waiting for transfers between devices, swap(): return lax.ppermute(x, axis, [(i, i ^ bit) for i in range(count)])  132 us
    dot_general x42, matrix products, dot(): return lax.dot_general(left, right, dims, preferred_element_type=f32)  125 us
    ppermute x42, starting transfers between devices, swap(): return lax.ppermute(x, axis, [(i, i ^ bit) for i in range(count)])  88.8 us
    pallas_call x2, Pallas kernels, attend_back(): pl.pallas_call(backward_kernel, grid_spec=pltpu.PrefetchScalarGridSpec(nu...  33.8 us
    pallas_call x2, Pallas kernels, attend(): pl.pallas_call(forward_kernel, grid_spec=pltpu.PrefetchScalarGridSpec(num...  24.8 us
    pallas_call x4, Pallas kernels, project(): pl.pallas_call(lambda *refs: project_kernel(turned, *refs), grid=(parts,)...  17.3 us
    unnamed x223, local copies, waits for them, and re-layouts  16.2 us
    another operation x28, other arithmetic, join_halves(): return jnp.stack([low, high], axis)  16.2 us
  transfers between devices with their start and end apart: 46, of which 18 were waited for; matrix products, arithmetic and copies ran while one was open for 19% of the time, Pallas kernels for 7%

profile of v1, /device:TPU:0, one launch (start us, length us, event | category | flops | bytes accessed | tf_op | source)
XLA Modules:
  0.0 607.4 jit_solution(5213647425264166779)
XLA Ops:
  13.3 6.2 %all-to-all-start = ((bf16[32,16,768]{2,1,0:T(8,128)(2,1)}), bf16[32,16,768]{2,1,0:T(8,128)(2,1)}, u32[]{:S(2)}, u32[]{:S(2)}) async-start(bf16[32,16,768]{2,1,0:T(8,128)(2,1)} %broadcast_in_dim.31), calls=%async_computation | async-start | bytes 1572864 | tf_op jit(solution)/shard_map/all_to_all | solution.py:484
  38.4 5.7 collective-permute-done.6
  51.2 19.0 %collective-permute-done.2 = bf16[2,2,48,640]{3,2,0,1:T(8,128)(2,1)S(1)} collective-permute-done((bf16[2,2,48,640]{3,2,0,1:T(8,128)(2,1)S(1)}, bf16[2,2,48,640]{3,2,0,1:T(8,128)(2,1)S(1)}, u32[]{:S(2)}, u32[]{:S(2)}) %collective-permute-start.2) | collective-permute-done | bytes 245792 | tf_op jit(solution)/shard_map/ppermute | solution.py:41
  72.9 5.6 collective-permute-done.8
  86.4 8.8 %collective-permute-done.18 = bf16[2,2,48,1536]{3,2,1,0:T(8,128)(2,1)S(1)} collective-permute-done((bf16[2,2,48,1536]{3,2,1,0:T(8,128)(2,1)S(1)}, bf16[2,2,48,1536]{3,2,1,0:T(8,128)(2,1)S(1)}, u32[]{:S(2)}, u32[]{:S(2)}) %collective-permute-start.18) | collective-permute-done | bytes 589856 | tf_op jit(solution)/shard_map/ppermute | solution.py:41
  121.3 16.1 %all-to-all-done.1 = f32[32,16,144]{2,1,0:T(8,128)} async-done(((f32[32,16,144]{2,1,0:T(8,128)}), f32[32,16,144]{2,1,0:T(8,128)}, u32[]{:S(2)}, u32[]{:S(2)}) %all-to-all-start.1) | async-done | bytes 294944 | tf_op jit(solution)/shard_map/all_to_all | solution.py:495
  160.1 12.6 %attend.3 = (bf16[1024,384]{1,0:T(8,128)(2,1)S(1)}, f32[3,2,1024]{2,1,0:T(2,128)S(1)}) custom-call(s32[10]{0:T(128)S(1)} %pad_add_fusion.1.info, bf16[1024,1152]{1,0:T(8,128)(2,1)S(1)} %project.6.q_ref.ko_ref.vo_ref, bf16[1024,768]{1,0:T(8,128)(2,1)S(1)} %project.7.kp_ref.vp_ref, bf16[1024,768]{1,0:T(8,128)(2,1)S(1)} %project.7.kp_ref.vp_ref, ...), custom_call_target="tpu_custom_call" | custom-call | flops 14495514624 | bytes 6291456 | tf_op jit(solution)/shard_map/attend/pallas_call | solution.py:258
  182.9 12.2 %attend.2 = (bf16[1024,384]{1,0:T(8,128)(2,1)S(1)}, f32[3,2,1024]{2,1,0:T(2,128)S(1)}) custom-call(s32[10]{0:T(128)S(1)} %pad_add_fusion.1.info, bf16[1024,1152]{1,0:T(8,128)(2,1)S(1)} %project.4.q_ref.ko_ref.vo_ref, bf16[1024,768]{1,0:T(8,128)(2,1)S(1)} %project.5.kp_ref.vp_ref, bf16[1024,768]{1,0:T(8,128)(2,1)S(1)} %project.5.kp_ref.vp_ref, ...), custom_call_target="tpu_custom_call" | custom-call | flops 14495514624 | bytes 6291456 | tf_op jit(solution)/shard_map/attend/pallas_call | solution.py:258
  207.4 5.9 multiply_convert_fusion.2
  221.6 6.0 multiply_convert_fusion
  245.6 6.2 %multiply_convert_fusion.1 = bf16[1024,1536]{1,0:T(8,128)(2,1)S(1)} fusion(bf16[1024,768]{1,0:T(8,128)(2,1)S(1)} %copy-done.83, bf16[768,1536]{1,0:T(8,128)(2,1)S(1)} %bitcast.489, f32[1024,1536]{1,0:T(8,128)} %get-tuple-element.180), kind=kOutput, calls=%fused_computation.17 | convolution fusion | flops 2434793472 | bytes 13369344 | tf_op jit(solution)/shard_map/dot_general | solution.py:28
  260.1 9.7 %fusion.36 = (f32[1024]{0:T(1024)S(1)}, f32[1024]{0:T(1024)S(1)}, f32[]{:T(128)}, f32[]{:T(128)}, f32[]{:T(128)}, /*index=5*/bf16[1024,768]{1,0:T(8,128)(2,1)}, f32[1024,768]{1,0:T(8,128)S(1)}) fusion(f32[8,768]{1,0:T(8,128)S(1)} %get-tuple-element.186, f32[1024]{0:T(1024)S(1)} %get-tuple-element.161, f32[1024,768]{1,0:T(8,128)S(1)} %get-tuple-element.79, ...), kind=kOutput, calls=%fused_computation.102 | convolution fusion | flops 2431645696 | bytes 22900748 | tf_op jit(solution)/shard_map/dot_general | solution.py:28
  281.7 16.7 %attend_back.3 = (bf16[1024,384]{1,0:T(8,128)(2,1)S(1)}, bf16[1024,384]{1,0:T(8,128)(2,1)S(1)}, bf16[1024,384]{1,0:T(8,128)(2,1)S(1)}, bf16[1024,384]{1,0:T(8,128)(2,1)S(1)}, bf16[1024,384]{1,0:T(8,128)(2,1)S(1)}) custom-call(s32[10]{0:T(128)S(1)} %pad_add_fusion.1.info, bf16[1024,1152]{1,0:T(8,128)(2,1)} %copy-done.8, ...), custom_call_target="tpu_custom_call" | custom-call | flops 32212254720 | bytes 11010048 | tf_op jit(solution)/shard_map/attend_back/pallas_call | solution.py:393
  308.1 17.1 %attend_back.2 = (bf16[1024,384]{1,0:T(8,128)(2,1)S(1)}, bf16[1024,384]{1,0:T(8,128)(2,1)S(1)}, bf16[1024,384]{1,0:T(8,128)(2,1)S(1)}, bf16[1024,384]{1,0:T(8,128)(2,1)S(1)}, bf16[1024,384]{1,0:T(8,128)(2,1)S(1)}) custom-call(s32[10]{0:T(128)S(1)} %pad_add_fusion.1.info, bf16[1024,1152]{1,0:T(8,128)(2,1)} %copy-done.9, ...), custom_call_target="tpu_custom_call" | custom-call | flops 32212254720 | bytes 11010048 | tf_op jit(solution)/shard_map/attend_back/pallas_call | solution.py:393
  376.2 39.3 %collective-permute-start.21 = (bf16[1024,768]{1,0:T(8,128)(2,1)S(1)}, bf16[1024,768]{1,0:T(8,128)(2,1)S(1)}, u32[]{:S(2)}, u32[]{:S(2)}) collective-permute-start(bf16[1024,768]{1,0:T(8,128)(2,1)S(1)} %get-tuple-element.182), channel_id=1, source_target_pairs={{0,1},{1,0},{2,3},{3,2},{4,5},{5,4},{6,7},{7,6},{8,9},{9,8},{10,11... | collective-permute-start | bytes 4718600 | tf_op jit(solution)/shard_map/ppermute | solution.py:41
  428.1 9.1 %collective-permute-done.28 = bf16[2,2,2,48,512]{4,3,1,2,0:T(8,128)(2,1)S(1)} collective-permute-done((bf16[2,2,2,48,512]{4,3,1,2,0:T(8,128)(2,1)S(1)}, bf16[2,2,2,48,512]{4,3,1,2,0:T(8,128)(2,1)S(1)}, u32[]{:S(2)}, u32[]{:S(2)}) %collective-permute-start.28) | collective-permute-done | bytes 393248 | tf_op jit(solution)/shard_map/ppermute | solution.py:41
  441.7 23.3 %collective-permute-done.29 = bf16[2,2,48,512]{3,2,0,1:T(8,128)(2,1)S(1)} collective-permute-done((bf16[2,2,48,512]{3,2,0,1:T(8,128)(2,1)S(1)}, bf16[2,2,48,512]{3,2,0,1:T(8,128)(2,1)S(1)}, u32[]{:S(2)}, u32[]{:S(2)}) %collective-permute-start.29) | collective-permute-done | bytes 196640 | tf_op jit(solution)/shard_map/ppermute | solution.py:41
  476.3 6.5 %fusion.35 = (f32[1024]{0:T(1024)S(1)}, f32[1024]{0:T(1024)S(1)}, f32[1024,768]{1,0:T(8,128)S(1)}) fusion(f32[8,768]{1,0:T(8,128)S(1)} %copy-done.91, f32[1024]{0:T(1024)S(1)} %copy-done.96, f32[1024]{0:T(1024)S(1)} %copy-done.94, bf16[1024,768]{1,0:T(8,128)(2,1)S(1)} %copy-done.31, f32[1024,768]{1,0:T(8,128)} %get-tuple-element.183, ...), kind=kOutput, calls=%fused_computation.101 | convolution fusion | flops 616560640 | bytes 26583040 | tf_op jit(solution)/shard_map/dot_general | solution.py:28
  491.6 5.7 all-to-all-start.2
  530.8 6.0 all-to-all-done.3
  538.6 15.2 %collective-permute-done.38 = bf16[2,2,2,48,1536]{4,3,1,2,0:T(8,128)(2,1)} collective-permute-done((bf16[2,2,2,48,1536]{4,3,1,2,0:T(8,128)(2,1)}, bf16[2,2,2,48,1536]{4,3,1,2,0:T(8,128)(2,1)}, u32[]{:S(2)}, u32[]{:S(2)}) %collective-permute-start.38) | collective-permute-done | bytes 1179680 | tf_op jit(solution)/shard_map/ppermute | solution.py:41
  567.6 8.5 %collective-permute-done.39 = bf16[2,2,48,1536]{3,2,0,1:T(8,128)(2,1)S(1)} collective-permute-done((bf16[2,2,48,1536]{3,2,0,1:T(8,128)(2,1)S(1)}, bf16[2,2,48,1536]{3,2,0,1:T(8,128)(2,1)S(1)}, u32[]{:S(2)}, u32[]{:S(2)}) %collective-permute-start.39) | collective-permute-done | bytes 589856 | tf_op jit(solution)/shard_map/ppermute | solution.py:41
  587.6 8.0 %collective-permute-done.35 = bf16[2,48,1920]{2,1,0:T(8,128)(2,1)S(1)} collective-permute-done((bf16[2,48,1920]{2,1,0:T(8,128)(2,1)S(1)}, bf16[2,48,1920]{2,1,0:T(8,128)(2,1)S(1)}, u32[]{:S(2)}, u32[]{:S(2)}) %collective-permute-start.35) | collective-permute-done | bytes 368672 | tf_op jit(solution)/shard_map/ppermute | solution.py:41
  597.7 8.0 %collective-permute-done.36 = bf16[48,1920]{1,0:T(8,128)(2,1)S(1)} collective-permute-done((bf16[48,1920]{1,0:T(8,128)(2,1)S(1)}, bf16[48,1920]{1,0:T(8,128)(2,1)S(1)}, u32[]{:S(2)}, u32[]{:S(2)}) %collective-permute-start.36) | collective-permute-done | bytes 184352 | tf_op jit(solution)/shard_map/ppermute | solution.py:41
  (521 shorter events, 325.8 us)
Async XLA Ops:
  2.3 33.0 %collective-permute-start.5 = (bf16[48,512]{1,0:T(8,128)(2,1)}, bf16[48,512]{1,0:T(8,128)(2,1)}, u32[]{:S(2)}, u32[]{:S(2)}) collective-permute-start(bf16[48,512]{1,0:T(8,128)(2,1)} %slice.266), channel_id=1, source_target_pairs={{0,16},{2,18},{4,20},{6,22},{8,24},{10,26},{12,28},{14,30},{16,0},... | collective-permute-start | bytes 147464 | tf_op jit(solution)/shard_map/ppermute | solution.py:41
  6.4 31.4 %collective-permute-start = (bf16[48,640]{1,0:T(8,128)(2,1)S(1)}, bf16[48,640]{1,0:T(8,128)(2,1)S(1)}, u32[]{:S(2)}, u32[]{:S(2)}) collective-permute-start(bf16[48,640]{1,0:T(8,128)(2,1)S(1)} %slice.263), channel_id=1, source_target_pairs={{0,16},{2,18},{4,20},{6,22},{8,24},{10,26},{12,28},{14,30},{16,0},... | collective-permute-start | bytes 184328 | tf_op jit(solution)/shard_map/ppermute | solution.py:41
  6.5 39.0 %collective-permute-start.16 = (bf16[48,1536]{1,0:T(8,128)(2,1)}, bf16[48,1536]{1,0:T(8,128)(2,1)}, u32[]{:S(2)}, u32[]{:S(2)}) collective-permute-start(bf16[48,1536]{1,0:T(8,128)(2,1)} %bitcast.509), channel_id=1, source_target_pairs={{0,16},{2,18},{4,20},{6,22},{8,24},{10,26},{12,28},{14,30},{16,0},... | collective-permute-start | bytes 442376 | tf_op jit(solution)/shard_map/ppermute | solution.py:41
  10.9 36.9 %collective-permute-start.11 = (bf16[48,1920]{1,0:T(8,128)(2,1)}, bf16[48,1920]{1,0:T(8,128)(2,1)S(1)}, u32[]{:S(2)}, u32[]{:S(2)}) collective-permute-start(bf16[48,1920]{1,0:T(8,128)(2,1)} %pad_maximum_fusion.28), channel_id=1, source_target_pairs={{0,16},{2,18},{4,20},{6,22},{8,24},{10,26},{12,28},{14,30},{16,0},... | collective-permute-start | bytes 552968 | tf_op jit(solution)/shard_map/ppermute | solution.py:41
  13.3 87.0 %all-to-all-start = ((bf16[32,16,768]{2,1,0:T(8,128)(2,1)}), bf16[32,16,768]{2,1,0:T(8,128)(2,1)}, u32[]{:S(2)}, u32[]{:S(2)}) async-start(bf16[32,16,768]{2,1,0:T(8,128)(2,1)} %broadcast_in_dim.31), calls=%async_computation | async-start | bytes 1572864 | tf_op jit(solution)/shard_map/all_to_all | solution.py:484
  19.5 94.7 %collective-permute-start.10 = (bf16[1024,768]{1,0:T(8,128)(2,1)S(1)}, bf16[1024,768]{1,0:T(8,128)(2,1)}, u32[]{:S(2)}, u32[]{:S(2)}) collective-permute-start(bf16[1024,768]{1,0:T(8,128)(2,1)S(1)} %copy-done.29), channel_id=1, source_target_pairs={{0,1},{1,0},{2,3},{3,2},{4,5},{5,4},{6,7},{7,6},{8,9},{9,8},{10,11... | collective-permute-start | bytes 4718600 | tf_op jit(solution)/shard_map/ppermute | solution.py:41
  46.5 25.2 %collective-permute-start.17 = (bf16[2,48,1536]{2,1,0:T(8,128)(2,1)S(1)}, bf16[2,48,1536]{2,1,0:T(8,128)(2,1)S(1)}, u32[]{:S(2)}, u32[]{:S(2)}) collective-permute-start(bf16[2,48,1536]{2,1,0:T(8,128)(2,1)S(1)} %pad_maximum_fusion.24), channel_id=1, source_target_pairs={{0,8},{2,10},{4,12},{6,14},{8,0},{10,2},{12,4},{14,6},{16,24},{18,... | collective-permute-start | bytes 884744 | tf_op jit(solution)/shard_map/ppermute | solution.py:41
  50.1 28.5 %collective-permute-start.8 = (bf16[2,2,2,48,512]{4,3,0,1,2:T(8,128)(2,1)S(1)}, bf16[2,2,2,48,512]{4,3,0,1,2:T(8,128)(2,1)S(1)}, u32[]{:S(2)}, u32[]{:S(2)}) collective-permute-start(bf16[2,2,2,48,512]{4,3,0,1,2:T(8,128)(2,1)S(1)} %get-tuple-element.123), channel_id=1, source_target_pairs={{0,1},{1,0},{2,3},{3,2},{4,5},{5,4},{6,7},{7,6},{8,9},{9,8},{10,11... | collective-permute-start | bytes 1179656 | tf_op jit(solution)/shard_map/ppermute | solution.py:41
  79.6 32.8 %collective-permute-start.9 = (bf16[2,2,2,2,48,512]{5,4,1,2,3,0:T(8,128)(2,1)}, bf16[2,2,2,2,48,512]{5,4,1,2,3,0:T(8,128)(2,1)}, u32[]{:S(2)}, u32[]{:S(2)}) collective-permute-start(bf16[2,2,2,2,48,512]{5,4,1,2,3,0:T(8,128)(2,1)} %pad_maximum_fusion.17), channel_id=1, source_target_pairs={{0,2},{2,0},{4,6},{6,4},{8,10},{10,8},{12,14},{14,12},{16,18},{18,... | collective-permute-start | bytes 2359304 | tf_op jit(solution)/shard_map/ppermute | solution.py:41
  86.4 31.1 %collective-permute-start.4 = (bf16[2,2,2,2,48,640]{5,4,1,2,0,3:T(8,128)(2,1)}, bf16[2,2,2,2,48,640]{5,4,1,2,0,3:T(8,128)(2,1)}, u32[]{:S(2)}, u32[]{:S(2)}) collective-permute-start(bf16[2,2,2,2,48,640]{5,4,1,2,0,3:T(8,128)(2,1)} %pad_maximum_fusion.13), channel_id=1, source_target_pairs={{0,2},{2,0},{4,6},{6,4},{8,10},{10,8},{12,14},{14,12},{16,18},{18,... | collective-permute-start | bytes 2949128 | tf_op jit(solution)/shard_map/ppermute | solution.py:41
  96.9 56.7 %collective-permute-start.19 = (bf16[2,2,2,48,1536]{4,3,2,1,0:T(8,128)(2,1)}, bf16[2,2,2,48,1536]{4,3,2,1,0:T(8,128)(2,1)}, u32[]{:S(2)}, u32[]{:S(2)}) collective-permute-start(bf16[2,2,2,48,1536]{4,3,2,1,0:T(8,128)(2,1)} %get-tuple-element.109), channel_id=1, source_target_pairs={{0,1},{1,0},{2,3},{3,2},{4,5},{5,4},{6,7},{7,6},{8,9},{9,8},{10,11... | collective-permute-start | bytes 3538952 | tf_op jit(solution)/shard_map/ppermute | solution.py:41
  98.9 57.1 %collective-permute-start.14 = (bf16[2,2,2,48,1920]{4,3,2,1,0:T(8,128)(2,1)}, bf16[2,2,2,48,1920]{4,3,2,1,0:T(8,128)(2,1)}, u32[]{:S(2)}, u32[]{:S(2)}) collective-permute-start(bf16[2,2,2,48,1920]{4,3,2,1,0:T(8,128)(2,1)} %pad_maximum_fusion.8), channel_id=1, source_target_pairs={{0,4},{2,6},{4,0},{6,2},{8,12},{10,14},{12,8},{14,10},{16,20},{18,... | collective-permute-start | bytes 4423688 | tf_op jit(solution)/shard_map/ppermute | solution.py:41
  105.4 32.0 %all-to-all-start.1 = ((f32[32,16,144]{2,1,0:T(8,128)}), f32[32,16,144]{2,1,0:T(8,128)}, u32[]{:S(2)}, u32[]{:S(2)}) async-start(f32[32,16,144]{2,1,0:T(8,128)} %bitcast.493), calls=%async_computation.1 | async-start | bytes 1048576 | tf_op jit(solution)/shard_map/all_to_all | solution.py:495
  155.9 39.2 %collective-permute-start.20 = (bf16[2,2,2,2,48,1536]{5,4,3,2,1,0:T(8,128)(2,1)S(1)}, bf16[2,2,2,2,48,1536]{5,4,3,2,1,0:T(8,128)(2,1)}, u32[]{:S(2)}, u32[]{:S(2)}) collective-permute-start(bf16[2,2,2,2,48,1536]{5,4,3,2,1,0:T(8,128)(2,1)S(1)} %pad_maximum_fusion.5), channel_id=1, source_target_pairs={{0,2},{2,0},{4,6},{6,4},{8,10},{10,8},{12,14},{14,12},{16,18},{18,... | collective-permute-start | bytes 7077896 | tf_op jit(solution)/shard_map/ppermute | solution.py:41
  159.7 38.5 %collective-permute-start.15 = (bf16[2,2,2,2,48,1920]{5,4,3,2,1,0:T(8,128)(2,1)}, bf16[2,2,2,2,48,1920]{5,4,3,2,1,0:T(8,128)(2,1)}, u32[]{:S(2)}, u32[]{:S(2)}) collective-permute-start(bf16[2,2,2,2,48,1920]{5,4,3,2,1,0:T(8,128)(2,1)} %pad_maximum_fusion.1), channel_id=1, source_target_pairs={{0,2},{2,0},{4,6},{6,4},{8,10},{10,8},{12,14},{14,12},{16,18},{18,... | collective-permute-start | bytes 8847368 | tf_op jit(solution)/shard_map/ppermute | solution.py:41
  369.5 56.3 %collective-permute-start.27 = (bf16[2,2,2,2,48,512]{5,4,1,2,0,3:T(8,128)(2,1)S(1)}, bf16[2,2,2,2,48,512]{5,4,1,2,0,3:T(8,128)(2,1)S(1)}, u32[]{:S(2)}, u32[]{:S(2)}) collective-permute-start(bf16[2,2,2,2,48,512]{5,4,1,2,0,3:T(8,128)(2,1)S(1)} %bitcast.505), channel_id=1, source_target_pairs={{0,2},{2,0},{4,6},{6,4},{8,10},{10,8},{12,14},{14,12},{16,18},{18,... | collective-permute-start | bytes 2359304 | tf_op jit(solution)/shard_map/ppermute | solution.py:41
  371.0 56.7 %collective-permute-start.22 = (bf16[2,2,2,2,48,640]{5,4,3,2,1,0:T(8,128)(2,1)S(1)}, bf16[2,2,2,2,48,640]{5,4,3,2,1,0:T(8,128)(2,1)S(1)}, u32[]{:S(2)}, u32[]{:S(2)}) collective-permute-start(bf16[2,2,2,2,48,640]{5,4,3,2,1,0:T(8,128)(2,1)S(1)} %fusion.63), channel_id=1, source_target_pairs={{0,2},{2,0},{4,6},{6,4},{8,10},{10,8},{12,14},{14,12},{16,18},{18,... | collective-permute-start | bytes 2949128 | tf_op jit(solution)/shard_map/ppermute | solution.py:41
  376.2 98.8 %collective-permute-start.21 = (bf16[1024,768]{1,0:T(8,128)(2,1)S(1)}, bf16[1024,768]{1,0:T(8,128)(2,1)S(1)}, u32[]{:S(2)}, u32[]{:S(2)}) collective-permute-start(bf16[1024,768]{1,0:T(8,128)(2,1)S(1)} %get-tuple-element.182), channel_id=1, source_target_pairs={{0,1},{1,0},{2,3},{3,2},{4,5},{5,4},{6,7},{7,6},{8,9},{9,8},{10,11... | collective-permute-start | bytes 4718600 | tf_op jit(solution)/shard_map/ppermute | solution.py:41
  418.8 99.7 %collective-permute-start.37 = (bf16[2,2,2,2,48,1536]{5,4,1,2,0,3:T(8,128)(2,1)}, bf16[2,2,2,2,48,1536]{5,4,1,2,0,3:T(8,128)(2,1)}, u32[]{:S(2)}, u32[]{:S(2)}) collective-permute-start(bf16[2,2,2,2,48,1536]{5,4,1,2,0,3:T(8,128)(2,1)} %bitcast.445), channel_id=1, source_target_pairs={{0,2},{2,0},{4,6},{6,4},{8,10},{10,8},{12,14},{14,12},{16,18},{18,... | collective-permute-start | bytes 7077896 | tf_op jit(solution)/shard_map/ppermute | solution.py:41
  428.0 39.2 %collective-permute-start.23 = (bf16[2,2,2,48,640]{4,3,2,1,0:T(8,128)(2,1)S(1)}, bf16[2,2,2,48,640]{4,3,2,1,0:T(8,128)(2,1)S(1)}, u32[]{:S(2)}, u32[]{:S(2)}) collective-permute-start(bf16[2,2,2,48,640]{4,3,2,1,0:T(8,128)(2,1)S(1)} %slice_bitcast_fusion.4), channel_id=1, source_target_pairs={{0,1},{1,0},{2,3},{3,2},{4,5},{5,4},{6,7},{7,6},{8,9},{9,8},{10,11... | collective-permute-start | bytes 1474568 | tf_op jit(solution)/shard_map/ppermute | solution.py:41
  437.3 27.7 %collective-permute-start.29 = (bf16[2,2,48,512]{3,2,0,1:T(8,128)(2,1)S(1)}, bf16[2,2,48,512]{3,2,0,1:T(8,128)(2,1)S(1)}, u32[]{:S(2)}, u32[]{:S(2)}) collective-permute-start(bf16[2,2,48,512]{3,2,0,1:T(8,128)(2,1)S(1)} %slice_bitcast_fusion.10), channel_id=1, source_target_pairs={{0,1},{1,0},{2,3},{3,2},{4,5},{5,4},{6,7},{7,6},{8,9},{9,8},{10,11... | collective-permute-start | bytes 589832 | tf_op jit(solution)/shard_map/ppermute | solution.py:41
  441.6 82.4 %collective-permute-start.32 = (bf16[2,2,2,2,48,1920]{5,4,1,2,3,0:T(8,128)(2,1)}, bf16[2,2,2,2,48,1920]{5,4,1,2,3,0:T(8,128)(2,1)}, u32[]{:S(2)}, u32[]{:S(2)}) collective-permute-start(bf16[2,2,2,2,48,1920]{5,4,1,2,3,0:T(8,128)(2,1)} %bitcast.444), channel_id=1, source_target_pairs={{0,2},{2,0},{4,6},{6,4},{8,10},{10,8},{12,14},{14,12},{16,18},{18,... | collective-permute-start | bytes 8847368 | tf_op jit(solution)/shard_map/ppermute | solution.py:41
  522.2 31.6 %collective-permute-start.38 = (bf16[2,2,2,48,1536]{4,3,1,2,0:T(8,128)(2,1)}, bf16[2,2,2,48,1536]{4,3,1,2,0:T(8,128)(2,1)}, u32[]{:S(2)}, u32[]{:S(2)}) collective-permute-start(bf16[2,2,2,48,1536]{4,3,1,2,0:T(8,128)(2,1)} %dynamic-slice_bitcast_fusion), channel_id=1, source_target_pairs={{0,4},{2,6},{4,0},{6,2},{8,12},{10,14},{12,8},{14,10},{16,20},{18,... | collective-permute-start | bytes 3538952 | tf_op jit(solution)/shard_map/ppermute | solution.py:41
  527.8 36.5 %collective-permute-start.33 = (bf16[2,2,2,48,1920]{4,3,0,1,2:T(8,128)(2,1)}, bf16[2,2,2,48,1920]{4,3,0,1,2:T(8,128)(2,1)}, u32[]{:S(2)}, u32[]{:S(2)}) collective-permute-start(bf16[2,2,2,48,1920]{4,3,0,1,2:T(8,128)(2,1)} %slice_bitcast_fusion), channel_id=1, source_target_pairs={{0,1},{1,0},{2,3},{3,2},{4,5},{5,4},{6,7},{7,6},{8,9},{9,8},{10,11... | collective-permute-start | bytes 4423688 | tf_op jit(solution)/shard_map/ppermute | solution.py:41
  (130 other events, 1853.7 us)

commit v2 on v1

v2 whole, which is shorter than its diff:
```python
import math

import jax
import jax.numpy as jnp
from jax import lax
from jax.experimental import pallas as pl
from jax.experimental.pallas import tpu as pltpu
from jax.sharding import PartitionSpec as P

HEAD_DIM = 64
PROMPT = 1024
CONT = 128
NCONT = 8
STEPS = 256
SEGS = 1 + NCONT

bf16 = jnp.bfloat16
f32 = jnp.float32
NN = (((1,), (0,)), ((), ()))
NT = (((1,), (1,)), ((), ()))
TN = (((0,), (0,)), ((), ()))
SCALE = HEAD_DIM ** (-0.5)
SCALE2 = SCALE * math.log2(math.e)
NEG = -1e30


def dot(left, right, dims=NN):
    return lax.dot_general(left, right, dims, preferred_element_type=f32)


def lanes(shape):
    return lax.broadcasted_iota(jnp.int32, shape, 1)


def rows(shape):
    return lax.broadcasted_iota(jnp.int32, shape, 0)


BOTH = ("dp", "tensor")
TENSOR, CORE, NEAR = 1, 2, 4
LONG = pl.CostEstimate(flops=10**11, bytes_accessed=1, transcendentals=0)


def swap(x, bits):
    count = lax.axis_size(BOTH)
    return lax.ppermute(x, BOTH, [(i, i ^ bits) for i in range(count)])


def tie(*arrays):
    return lax.optimization_barrier(arrays)


def after(array, *others):
    return lax.optimization_barrier((array,) + others)[0]


def far_count():
    return lax.axis_size("dp") // 4


def far_bits():
    return [1 << k for k in range(far_count().bit_length() - 1)]


def plus(left, right):
    return (left.astype(f32) + right.astype(f32)).astype(bf16)


def send_far(cur):
    cur = cur.reshape((-1, 2) + cur.shape[1:])
    return cur[:, 0], cur[:, 1]


def join_kernel(cuts, bit_ref, own_ref, came_ref, *out_refs):
    bit = bit_ref[0]
    start = 0
    for out_ref, cut in zip(out_refs, cuts):
        for n in range(own_ref.shape[0]):
            out_ref[n, bit] = own_ref[n, :, start : start + cut]
            out_ref[n, 1 - bit] = came_ref[n, :, start : start + cut]
        start += cut


def join(own, came, bit, cuts=None):
    count, rows_each, columns = own.shape
    sizes = cuts or (columns,)
    group = min(count, 2)
    spec = pl.BlockSpec((group, rows_each, columns), lambda n, s: (n, 0, 0))
    outs = pl.pallas_call(
        lambda *refs: join_kernel(sizes, *refs),
        grid_spec=pltpu.PrefetchScalarGridSpec(
            num_scalar_prefetch=1,
            grid=(count // group,),
            in_specs=[spec, spec],
            out_specs=[
                pl.BlockSpec((group, 2, rows_each, cut), lambda n, s: (n, 0, 0, 0)) for cut in sizes
            ],
        ),
        out_shape=[jax.ShapeDtypeStruct((count, 2, rows_each, cut), bf16) for cut in sizes],
        cost_estimate=pl.CostEstimate(flops=1, bytes_accessed=10**6, transcendentals=0),
        compiler_params=pltpu.CompilerParams(vmem_limit_bytes=16 * 2**20),
        name="join",
    )(bit.astype(jnp.int32).reshape(1), own, came)
    outs = [out.reshape(2 * count, rows_each, -1) for out in outs]
    return outs if cuts else outs[0]


def turn(x, cosine, sine):
    lane = lanes(x.shape) % 64
    swapped = jnp.where(lane < 32, -pltpu.roll(x, 96, 1), pltpu.roll(x, 32, 1))
    return x * cosine + swapped * sine


def turn_back(x, cosine, sine):
    lane = lanes(x.shape) % 64
    swapped = jnp.where(lane < 32, pltpu.roll(x, 96, 1), -pltpu.roll(x, 32, 1))
    return x * cosine + swapped * sine


def norm_parts(inputs):
    average = jnp.mean(inputs, -1, keepdims=True)
    centred = inputs - average
    spread = jnp.mean(centred * centred, -1, keepdims=True)
    inverse = lax.rsqrt(spread + 1e-05)
    return centred * inverse, inverse


def norm_back(unit, inverse, grad, scales):
    inner = grad * (1.0 + scales)
    first = jnp.mean(inner, -1, keepdims=True)
    second = jnp.mean(inner * unit, -1, keepdims=True)
    return inverse * (inner - first - unit * second)


def modulation(mods_ref, info, tile, part):
    segment = jnp.where(info[0] == 0, 0, 1 + tile)
    width = mods_ref.shape[1] // 6
    return mods_ref[pl.ds(segment, 1), part * width : (part + 1) * width]


def store_pieces(total, info, keep_ref, send_ref, lead):
    half, rows_each = keep_ref.shape[-3], keep_ref.shape[-2]
    fars = half // 2
    for k in range(half):
        low = total[2 * k * rows_each : (2 * k + 1) * rows_each]
        high = total[(2 * k + 1) * rows_each : (2 * k + 2) * rows_each]
        place = ((k % 2) ^ info[11]) * fars + ((k // 2) ^ info[12])
        keep_ref[lead + (place,)] = jnp.where(info[10] == 0, low, high).astype(bf16)
        send_ref[lead + (place,)] = jnp.where(info[10] == 0, high, low).astype(bf16)


def fill(source_ref, w_refs, out_ref, tables):
    for half, w_ref in enumerate(w_refs):
        pl.when(pl.program_id(0) == half)(lambda w_ref=w_ref: fill_half(source_ref, w_ref, out_ref, tables))


def fill_half(source_ref, w_ref, out_ref, tables):
    joined = dot(source_ref[...], w_ref[...])
    for c in range(joined.shape[1] // 128):
        cut = slice(c * 128, (c + 1) * 128)
        piece = joined[:, cut]
        if tables:
            piece = turn(piece, tables[0][...], tables[1][...])
        out_ref[0, :, cut] = piece.astype(bf16)


def project_own_kernel(info, x_ref, mods_ref, *refs):
    w_ref, (cos_ref, sin_ref, joined_ref, normed_ref) = refs[:2], refs[2:]
    half, part = pl.program_id(0), pl.program_id(1)

    @pl.when((half == 0) & (part == 0))
    def _():
        for i in range(x_ref.shape[0] // CONT):
            cut = slice(i * CONT, (i + 1) * CONT)
            unit, _ = norm_parts(x_ref[cut, :].astype(f32))
            shift, scale = (modulation(mods_ref, info, i, n) for n in range(2))
            normed_ref[cut, :] = (unit * (1.0 + scale) + shift).astype(bf16)

    pl.when(part < 2)(lambda: fill(normed_ref, w_ref, joined_ref, (cos_ref, sin_ref)))
    pl.when(part == 2)(lambda: fill(normed_ref, w_ref, joined_ref, None))


def project_prompt_kernel(info, x_ref, *refs):
    came_refs, (mods_ref, *w_ref, cos_ref, sin_ref, joined_ref, normed_ref) = refs[:-7], refs[-7:]
    half, part = pl.program_id(0), pl.program_id(1)
    width = x_ref.shape[1]

    @pl.when((half == 0) & (part == 0))
    def _():
        shift, scale = mods_ref[0:1, :width], mods_ref[0:1, width : 2 * width]
        for i in range(x_ref.shape[0] // CONT):
            cut = slice(i * CONT, (i + 1) * CONT)
            place = i * CONT
            for came_ref in came_refs:
                if 0 <= place < came_ref.shape[0]:
                    came = came_ref[place : place + CONT, :].astype(f32)
                place -= came_ref.shape[0]
            x = jnp.where(info[0] == 0, x_ref[cut, :].astype(f32), came)
            unit, _ = norm_parts(x)
            normed_ref[cut, :] = (unit * (1.0 + scale) + shift).astype(bf16)

    pl.when(part == 0)(lambda: fill(normed_ref, w_ref, joined_ref, (cos_ref, sin_ref)))
    pl.when(part == 1)(lambda: fill(normed_ref, w_ref, joined_ref, None))


def project(kernel, parts, estimate, info, inputs, mods, qkv, tables):
    count, width = inputs[0].shape
    head_width = qkv[0].shape[1] // 3

    def whole(array):
        return pl.BlockSpec(array.shape, lambda t, p, s: (0,) * array.ndim)

    def weight(half):
        def place(t, p, s):
            now = p + 3 - parts
            return (0, jnp.where(t == half, now, 2 if half == 0 else 3 - parts))

        return pl.BlockSpec((width, head_width), place)

    return pl.pallas_call(
        kernel,
        grid_spec=pltpu.PrefetchScalarGridSpec(
            num_scalar_prefetch=1,
            grid=(2, parts),
            in_specs=[whole(array) for array in inputs]
            + [whole(mods), weight(0), weight(1)]
            + [whole(table) for table in tables],
            out_specs=[
                pl.BlockSpec((1, count, head_width), lambda t, p, s: (t, 0, p)),
                whole(inputs[0]),
            ],
        ),
        out_shape=[
            jax.ShapeDtypeStruct((2, count, parts * head_width), bf16),
            jax.ShapeDtypeStruct((count, width), bf16),
        ],
        compiler_params=pltpu.CompilerParams(vmem_limit_bytes=32 * 2**20),
        cost_estimate=estimate,
        name="project",
    )(info, *inputs, mods, *qkv, *tables)


def middle_kernel(
    info, x_ref, a0_ref, a1_ref, mods_ref, o0_ref, o1_ref, branch_ref, middle_ref, n2_ref
):
    branch = dot(a0_ref[...], o0_ref[...], NT) + dot(a1_ref[...], o1_ref[...], NT)
    branch_ref[...] = branch
    per = x_ref.shape[0] // CONT
    for u in range(per):
        cut = slice(u * CONT, (u + 1) * CONT)
        gate, shift, scale = (
            modulation(mods_ref, info, pl.program_id(0) * per + u, n) for n in (2, 3, 4)
        )
        middle = x_ref[cut, :].astype(f32) + gate * branch[cut]
        middle_ref[cut, :] = middle
        unit, _ = norm_parts(middle)
        n2_ref[cut, :] = (unit * (1.0 + scale) + shift).astype(bf16)


def middle_norm(info, x, attended, mods, out_t):
    count, width = x.shape
    head_width = attended[0].shape[1]
    tile = 256
    by_row = pl.BlockSpec((tile, width), lambda i, s: (i, 0))
    by_head = pl.BlockSpec((tile, head_width), lambda i, s: (i, 0))
    return pl.pallas_call(
        middle_kernel,
        grid_spec=pltpu.PrefetchScalarGridSpec(
            num_scalar_prefetch=1,
            grid=(count // tile,),
            in_specs=[
                by_row,
                by_head,
                by_head,
                pl.BlockSpec(mods.shape, lambda i, s: (0, 0)),
                pl.BlockSpec((width, head_width), lambda i, s: (0, 0)),
                pl.BlockSpec((width, head_width), lambda i, s: (0, 0)),
            ],
            out_specs=[by_row] * 3,
        ),
        out_shape=[
            jax.ShapeDtypeStruct((count, width), f32),
            jax.ShapeDtypeStruct((count, width), f32),
            jax.ShapeDtypeStruct((count, width), bf16),
        ],
        compiler_params=pltpu.CompilerParams(vmem_limit_bytes=32 * 2**20),
        cost_estimate=LONG,
        name="middle_norm",
    )(info, x, *attended, mods, *out_t)


def mlp_kernel(first, info, n2_ref, *refs):
    if first:
        cot_ref, mods_ref = refs[:2]
        refs = refs[2:]
    else:
        n2_turned, out_grad, out_turned, branch_before, grad_before = refs[:5]
        refs = refs[5:]
    up_ref, down_ref, branch_ref, grad_ref = refs[:4]
    down_keep_ref, down_send_ref, up_keep_ref, up_send_ref = refs[4:8]
    if first:
        n2_turned, out_grad, out_turned = refs[8:11]
    hidden, pre_grad = refs[-2:]
    count = n2_ref.shape[0]

    @pl.when(pl.program_id(0) == 0)
    def _():
        if first:
            for i in range(count // CONT):
                cut = slice(i * CONT, (i + 1) * CONT)
                gate = modulation(mods_ref, info, i, 5)
                out_grad[cut, :] = (cot_ref[cut, :].astype(f32) * gate).astype(bf16)
            n2_turned[...] = jnp.transpose(n2_ref[...])
            out_turned[...] = jnp.transpose(out_grad[...])
            branch_ref[...] = jnp.zeros_like(branch_ref)
            grad_ref[...] = jnp.zeros_like(grad_ref)
        else:
            branch_ref[...] = branch_before[...]
            grad_ref[...] = grad_before[...]

    up, down = up_ref[...], down_ref[...]
    tile = 256
    for i in range(count // tile):
        cut = slice(i * tile, (i + 1) * tile)
        pre = dot(n2_ref[cut, :], up)
        cdf = 0.5 * (1.0 + lax.erf(pre * (2.0**-0.5)))
        pdf = jnp.exp(-0.5 * pre * pre) * ((2.0 * math.pi) ** -0.5)
        value = (pre * cdf).astype(bf16)
        hidden[cut, :] = value
        grad = (dot(out_grad[cut, :], down) * (cdf + pre * pdf)).astype(bf16)
        pre_grad[cut, :] = grad
        branch_ref[cut, :] += dot(value, down, NT)
        grad_ref[cut, :] += dot(grad, up, NT)
    store_pieces(dot(out_turned[...], hidden[...]), info, down_keep_ref, down_send_ref, ())
    store_pieces(dot(n2_turned[...], pre_grad[...]), info, up_keep_ref, up_send_ref, ())


def feed_forward(info, n2, sources, up, down):
    count, width = n2.shape
    hidden_width = up.shape[1]
    first = len(sources) == 2
    cols = 384
    dp_count = lax.axis_size("dp")
    pieces = (dp_count // 2, width // dp_count, hidden_width)

    def whole(array):
        return pl.BlockSpec(array.shape, lambda b, s: (0,) * array.ndim)

    piece_spec = pl.BlockSpec(pieces[:2] + (cols,), lambda b, s: (0, 0, b))
    weight_spec = pl.BlockSpec((width, cols), lambda b, s: (0, b))
    outs = [jax.ShapeDtypeStruct((count, width), f32)] * 2 + [
        jax.ShapeDtypeStruct(pieces, bf16)
    ] * 4
    out_specs = [whole(n2)] * 2 + [piece_spec] * 4
    if first:
        shapes = [(width, count), (count, width), (width, count)]
        outs += [jax.ShapeDtypeStruct(shape, bf16) for shape in shapes]
        out_specs += [pl.BlockSpec(shape, lambda b, s: (0, 0)) for shape in shapes]
    return pl.pallas_call(
        lambda *refs: mlp_kernel(first, *refs),
        grid_spec=pltpu.PrefetchScalarGridSpec(
            num_scalar_prefetch=1,
            grid=(hidden_width // cols,),
            in_specs=[whole(n2)] + [whole(array) for array in sources] + [weight_spec] * 2,
            out_specs=out_specs,
            scratch_shapes=[pltpu.VMEM((count, cols), bf16), pltpu.VMEM((count, cols), bf16)],
        ),
        out_shape=outs,
        compiler_params=pltpu.CompilerParams(vmem_limit_bytes=52 * 2**20),
        cost_estimate=LONG,
        name="feed_forward",
    )(info, n2, *sources, up, down)


def post_kernel(
    info,
    middle_ref,
    branch_ref,
    mlp_ref,
    n2_grad_ref,
    cot_ref,
    a0_ref,
    a1_ref,
    mods_ref,
    o0_ref,
    o1_ref,
    out_ref,
    middle_grad_ref,
    g0_ref,
    g1_ref,
    sums_ref,
    keep_ref,
    send_ref,
    total,
    attn_grad,
):
    step = pl.program_id(0)
    per = middle_ref.shape[0] // CONT
    for u in range(per):
        cut = slice(u * CONT, (u + 1) * CONT)
        tile = step * per + u
        gate1, scale2, gate2 = (modulation(mods_ref, info, tile, n) for n in (2, 4, 5))
        middle, branch, mlp = middle_ref[cut, :], branch_ref[cut, :], mlp_ref[cut, :]
        n2_grad, upstream = n2_grad_ref[cut, :], cot_ref[cut, :].astype(f32)
        mlp_part, attn_part = gate2 * mlp, gate1 * branch
        result = middle + mlp_part
        out_ref[cut, :] = result.astype(bf16)
        unit, inverse = norm_parts(middle)
        middle_grad = upstream + norm_back(unit, inverse, n2_grad, scale2)
        middle_grad_ref[cut, :] = middle_grad
        attn_grad[cut, :] = (middle_grad * gate1).astype(bf16)
        valid = (rows((CONT, 1)) < info[2 + tile]).astype(f32)
        for n, value in enumerate(
            (
                middle_grad * branch,
                n2_grad,
                n2_grad * unit,
                upstream * mlp,
                valid * result * result,
                valid * attn_part * attn_part,
                valid * mlp_part * mlp_part,
            )
        ):
            sums_ref[u, n : n + 1, :] = jnp.sum(value, 0, keepdims=True)
        sums_ref[u, 7:8, :] = jnp.zeros_like(gate1)
    halves = ((a0_ref, g0_ref, o0_ref), (a1_ref, g1_ref, o1_ref))
    for t, (a_ref, g_ref, o_ref) in enumerate(halves):
        g_ref[...] = dot(attn_grad[...], o_ref[...]).astype(bf16)
        part = dot(attn_grad[...], a_ref[...], TN)
        total[t] = jnp.where(step == 0, part, total[t] + part)

    @pl.when(step == pl.num_programs(0) - 1)
    def _():
        for t in range(2):
            store_pieces(total[t], info, keep_ref, send_ref, (t,))


def post(info, middle, branch, mlp, n2_grad, cotangent, attended, mods, out_t):
    count, width = middle.shape
    head_width = attended[0].shape[1]
    tile = 256
    tiles = count // CONT
    dp_count = lax.axis_size("dp")
    pieces = (2, dp_count // 2, width // dp_count, head_width)
    by_row = pl.BlockSpec((tile, width), lambda i, s: (i, 0))
    by_head = pl.BlockSpec((tile, head_width), lambda i, s: (i, 0))
    return pl.pallas_call(
        post_kernel,
        grid_spec=pltpu.PrefetchScalarGridSpec(
            num_scalar_prefetch=1,
            grid=(count // tile,),
            in_specs=[by_row] * 5
            + [
                by_head,
                by_head,
                pl.BlockSpec(mods.shape, lambda i, s: (0, 0)),
                pl.BlockSpec((width, head_width), lambda i, s: (0, 0)),
                pl.BlockSpec((width, head_width), lambda i, s: (0, 0)),
            ],
            out_specs=[
                by_row,
                by_row,
                by_head,
                by_head,
                pl.BlockSpec((tile // CONT, 8, width), lambda i, s: (i, 0, 0)),
                pl.BlockSpec(pieces, lambda i, s: (0, 0, 0, 0)),
                pl.BlockSpec(pieces, lambda i, s: (0, 0, 0, 0)),
            ],
            scratch_shapes=[
                pltpu.VMEM((2, width, head_width), f32),
                pltpu.VMEM((tile, width), bf16),
            ],
        ),
        out_shape=[
            jax.ShapeDtypeStruct((count, width), bf16),
            jax.ShapeDtypeStruct((count, width), f32),
            jax.ShapeDtypeStruct((count, head_width), bf16),
            jax.ShapeDtypeStruct((count, head_width), bf16),
            jax.ShapeDtypeStruct((tiles, 8, width), f32),
            jax.ShapeDtypeStruct(pieces, bf16),
            jax.ShapeDtypeStruct(pieces, bf16),
        ],
        compiler_params=pltpu.CompilerParams(vmem_limit_bytes=48 * 2**20),
        cost_estimate=LONG,
        name="post",
    )(info, middle, branch, mlp, n2_grad, cotangent, *attended, mods, *out_t)


def last_kernel(
    info, x_ref, own_ref, prompt_ref, came_ref, middle_grad_ref, mods_ref, out_ref, sums_ref
):
    step = pl.program_id(0)
    per = x_ref.shape[0] // CONT
    for u in range(per):
        cut = slice(u * CONT, (u + 1) * CONT)
        scale = modulation(mods_ref, info, step * per + u, 1)
        prompt = prompt_ref[cut, :] + came_ref[cut, :].astype(f32)
        grad = own_ref[cut, :] + jnp.where(info[0] == 0, prompt, 0.0)
        unit, inverse = norm_parts(x_ref[cut, :].astype(f32))
        sums_ref[u, 0:1, :] = jnp.sum(grad, 0, keepdims=True)
        sums_ref[u, 1:2, :] = jnp.sum(grad * unit, 0, keepdims=True)
        sums_ref[u, 2:, :] = jnp.zeros((6, x_ref.shape[1]), f32)
        out_ref[cut, :] = middle_grad_ref[cut, :] + norm_back(unit, inverse, grad, scale)


def last(info, x, own_sum, prompt_sum, came, middle_grad, mods):
    count, width = x.shape
    tile = 256
    by_row = pl.BlockSpec((tile, width), lambda i, s: (i, 0))
    return pl.pallas_call(
        last_kernel,
        grid_spec=pltpu.PrefetchScalarGridSpec(
            num_scalar_prefetch=1,
            grid=(count // tile,),
            in_specs=[by_row] * 5 + [pl.BlockSpec(mods.shape, lambda i, s: (0, 0))],
            out_specs=[by_row, pl.BlockSpec((tile // CONT, 8, width), lambda i, s: (i, 0, 0))],
        ),
        out_shape=[
            jax.ShapeDtypeStruct((count, width), f32),
            jax.ShapeDtypeStruct((count // CONT, 8, width), f32),
        ],
        compiler_params=pltpu.CompilerParams(vmem_limit_bytes=32 * 2**20),
        cost_estimate=LONG,
        name="last",
    )(info, x, own_sum, prompt_sum, came, middle_grad, mods)


def forward_kernel(info, *refs):
    q_ref, kp_ref, vp_ref, ko_ref, vo_ref = (ref.at[0] for ref in refs[:5])
    o_ref, lse_ref = refs[5:]
    role = info[0]
    prompt_count = info[1]
    count = q_ref.shape[0]
    lane = lanes((count, 128))
    row = rows((count, 128))
    tile = 256
    blocks = count // tile

    def prepare(h):
        sel = (lane // 64) == h
        extra = 64 * (1 - h)
        q = jnp.where(sel, q_ref[...], jnp.where(lane == extra, 1.0, 0.0).astype(bf16))
        bias = jnp.where((lane == extra) & (row >= prompt_count), NEG, 0.0).astype(bf16)
        k = jnp.where(sel, kp_ref[...], bias)
        v = jnp.where(sel, vp_ref[...], jnp.ones((), bf16))
        return sel, q, k, v

    def finish(h, i, o, top):
        extra = 64 * (1 - h)
        weight = o[:, extra : extra + 1]
        lse = top * SCALE2 + jnp.log2(weight)
        turned = jnp.transpose(jnp.broadcast_to(lse, (tile, 128)))
        lse_ref[0, h : h + 1, i * tile : (i + 1) * tile] = turned[0:1, :]
        return o * (1.0 / weight)

    def store(outs):
        for i in range(blocks):
            merged = jnp.where(lanes((tile, 128)) < 64, outs[0][i], outs[1][i])
            o_ref[i * tile : (i + 1) * tile, :] = merged.astype(bf16)

    @pl.when(role == 0)
    def _():
        outs = []
        for h in range(2):
            sel, q, k, v = prepare(h)
            heads = []
            for i in range(blocks):
                start, stop = i * tile, (i + 1) * tile
                s = dot(q[start:stop], k[:stop], NT)
                near = jnp.where(lanes((tile, tile)) <= rows((tile, tile)), s[:, start:], NEG)
                top = jnp.max(near, 1, keepdims=True)
                if i:
                    top = jnp.maximum(top, jnp.max(s[:, :start], 1, keepdims=True))
                o = dot(jnp.exp2(near * SCALE2 - top * SCALE2).astype(bf16), v[start:stop])
                if i:
                    o = o + dot(
                        jnp.exp2(s[:, :start] * SCALE2 - top * SCALE2).astype(bf16), v[:start]
                    )
                heads.append(finish(h, i, o, top))
            outs.append(heads)
        store(outs)

    @pl.when(role != 0)
    def _():
        outs = []
        for h in range(2):
            sel, q, k, v = prepare(h)
            own_k = jnp.where(sel, ko_ref[...], jnp.zeros((), bf16))
            own_v = jnp.where(sel, vo_ref[...], jnp.ones((), bf16))
            heads = []
            for i in range(blocks):
                start, stop = i * tile, (i + 1) * tile
                s = dot(q[start:stop], k, NT)
                cuts = [slice(r, r + CONT) for r in range(start, stop, CONT)]
                near = []
                for cut in cuts:
                    piece = dot(q[cut], own_k[cut], NT)
                    col, line = lanes((CONT, CONT)), rows((CONT, CONT))
                    fine = (col <= line) & (col < info[2 + cut.start // CONT])
                    near.append(jnp.where(fine, piece, NEG))
                near = jnp.concatenate(near, 0)
                top = jnp.maximum(
                    jnp.max(s, 1, keepdims=True), jnp.max(near, 1, keepdims=True)
                )
                far_weight = jnp.exp2(s * SCALE2 - top * SCALE2).astype(bf16)
                near_weight = jnp.exp2(near * SCALE2 - top * SCALE2).astype(bf16)
                own = [
                    dot(near_weight[n * CONT : (n + 1) * CONT], own_v[cut])
                    for n, cut in enumerate(cuts)
                ]
                heads.append(finish(h, i, dot(far_weight, v) + jnp.concatenate(own, 0), top))
            outs.append(heads)
        store(outs)


def attend(info, joined, prompts, t):
    count = joined.shape[1]
    head_width = joined.shape[2] // 3
    pairs = head_width // 128

    def spec(offset):
        return pl.BlockSpec((1, count, 128), lambda h, s: (t, 0, offset + h))

    return pl.pallas_call(
        forward_kernel,
        grid_spec=pltpu.PrefetchScalarGridSpec(
            num_scalar_prefetch=1,
            grid=(pairs,),
            in_specs=[spec(0), spec(0), spec(pairs), spec(pairs), spec(2 * pairs)],
            out_specs=[
                pl.BlockSpec((count, 128), lambda h, s: (0, h)),
                pl.BlockSpec((1, 2, count), lambda h, s: (h, 0, 0)),
            ],
        ),
        out_shape=[
            jax.ShapeDtypeStruct((count, head_width), bf16),
            jax.ShapeDtypeStruct((pairs, 2, count), f32),
        ],
        compiler_params=pltpu.CompilerParams(vmem_limit_bytes=40 * 2**20),
        cost_estimate=LONG,
        name="attend",
    )(info, joined, prompts, prompts, joined, joined)


def backward_kernel(first, last, tiles, own, info, *refs):
    refs = list(refs)
    q_ref, do_ref, o_ref, lse_ref = refs[0].at[0], *refs[1:4]
    del refs[:4]
    if tiles:
        kp_ref, vp_ref, cp_ref, sp_ref = refs[0].at[0], refs[1].at[0], *refs[2:4]
        del refs[:4]
    if own:
        ko_ref, vo_ref = refs[0].at[0], refs[1].at[0]
        del refs[:2]
    if own or last:
        co_ref, so_ref = refs[:2]
        del refs[:2]
    before_ref = None if first else refs.pop(0)
    dq_ref = refs.pop(0)
    if tiles:
        dkp_ref, dvp_ref = refs[:2]
        del refs[:2]
    if own:
        dko_ref, dvo_ref = refs[:2]
        del refs[:2]
    (dq_acc,) = refs
    role = info[0]
    prompt_count = info[1]
    count = q_ref.shape[0]
    tile = 256
    lane = lanes((count, 128))
    none = jnp.zeros((), bf16)
    products = jnp.transpose(do_ref[...].astype(f32) * o_ref[...].astype(f32))
    deltas = [jnp.sum(products[64 * h : 64 * h + 64], 0, keepdims=True) for h in range(2)]
    dq_acc[...] = jnp.zeros_like(dq_acc) if first else before_ref[...]

    def far_block(j, prompt):
        start, stop = j * tile, (j + 1) * tile
        cut = slice(start - tiles[0] * tile, stop - tiles[0] * tile)
        q_from = start if prompt else 0
        lane_k = lanes((tile, 128))
        row_k = rows((tile, 128)) + start
        key_parts, value_parts = [], []
        for h in range(2):
            extra = 64 * (1 - h)
            sel = (lane_k // 64) == h
            bias = jnp.where((lane_k == extra) & (row_k >= prompt_count), NEG, 0.0).astype(bf16)
            k = jnp.where(sel, kp_ref[cut, :], bias)
            k_plain = jnp.where(sel, kp_ref[cut, :], none)
            v = jnp.where(sel, vp_ref[cut, :], none)
            lane_q = lane[q_from:]
            ones = jnp.where(lane_q == extra, 1.0, 0.0).astype(bf16)
            q = jnp.where((lane_q // 64) == h, q_ref[q_from:, :], ones)
            s = dot(k, q, NT)
            if prompt:
                near = jnp.where(rows((tile, tile)) <= lanes((tile, tile)), s[:, :tile], NEG)
                s = jnp.concatenate([near, s[:, tile:]], 1) if stop < count else near
            weight = jnp.exp2(s * SCALE2 - lse_ref[0, h : h + 1, q_from:])
            grad = dot(v, do_ref[q_from:, :], NT)
            score = (weight * (grad - deltas[h][:, q_from:])).astype(bf16)
            value_parts.append(dot(weight.astype(bf16), do_ref[q_from:, :]))
            key_parts.append(dot(score, q_ref[q_from:, :]))
            dq_acc[q_from:, :] += dot(score, k_plain, TN)
        key_grad = jnp.where(lane_k < 64, key_parts[0], key_parts[1]) * SCALE
        value_grad = jnp.where(lane_k < 64, value_parts[0], value_parts[1])
        dkp_ref[cut, :] = turn_back(key_grad, cp_ref[cut, :], sp_ref[cut, :]).astype(bf16)
        dvp_ref[cut, :] = value_grad.astype(bf16)

    @pl.when(role == 0)
    def _():
        for j in tiles:
            far_block(j, True)
        if own:
            dko_ref[...] = jnp.zeros_like(dko_ref)
            dvo_ref[...] = jnp.zeros_like(dvo_ref)

    @pl.when(role != 0)
    def _():
        for j in tiles:
            far_block(j, False)
        lane_k = lanes((CONT, CONT))
        row_k = rows((CONT, CONT))
        for i in range(count // CONT if own else 0):
            cut = slice(i * CONT, (i + 1) * CONT)
            key_parts, value_parts, query_part = [], [], None
            for h in range(2):
                sel = (lane_k // 64) == h
                k = jnp.where(sel, ko_ref[cut, :], none)
                v = jnp.where(sel, vo_ref[cut, :], none)
                fine = (row_k <= lane_k) & (row_k < info[2 + i])
                s = jnp.where(fine, dot(k, q_ref[cut, :], NT), NEG)
                weight = jnp.exp2(s * SCALE2 - lse_ref[0, h : h + 1, cut])
                grad = dot(v, do_ref[cut, :], NT)
                score = (weight * (grad - deltas[h][:, cut])).astype(bf16)
                value_parts.append(dot(weight.astype(bf16), do_ref[cut, :]))
                key_parts.append(dot(score, q_ref[cut, :]))
                part = dot(score, k, TN)
                query_part = part if query_part is None else query_part + part
            dq_acc[cut, :] += query_part
            key_grad = jnp.where(lane_k < 64, key_parts[0], key_parts[1]) * SCALE
            value_grad = jnp.where(lane_k < 64, value_parts[0], value_parts[1])
            dko_ref[cut, :] = turn_back(key_grad, co_ref[cut, :], so_ref[cut, :]).astype(bf16)
            dvo_ref[cut, :] = value_grad.astype(bf16)

    if last:
        dq_ref[...] = turn_back(dq_acc[...] * SCALE, co_ref[...], so_ref[...]).astype(bf16)
    else:
        dq_ref[...] = dq_acc[...]


def attend_back(info, joined, prompts, t, grad, out, lse, tables, tiles, own, before=None, last=True):
    count = joined.shape[1]
    head_width = joined.shape[2] // 3
    pairs = head_width // 128
    first = before is None
    part = 256 * len(tiles)

    def half_spec(offset):
        return pl.BlockSpec((1, count, 128), lambda h, s: (t, 0, offset + h))

    def part_spec(offset):
        return pl.BlockSpec((1, part, 128), lambda h, s: (t, tiles[0] * 256 // part, offset + h))

    rows_spec = pl.BlockSpec((count, 128), lambda h, s: (0, h))
    whole = pl.BlockSpec((count, 128), lambda h, s: (0, 0))
    args = [joined, grad, out, lse]
    specs = [
        half_spec(0),
        rows_spec,
        rows_spec,
        pl.BlockSpec((1, 2, count), lambda h, s: (h, 0, 0)),
    ]
    outs = [jax.ShapeDtypeStruct((count, head_width), bf16 if last else f32)]
    out_specs = [rows_spec]
    if tiles:
        args += [prompts, prompts, tables[2], tables[3]]
        part_table = pl.BlockSpec((part, 128), lambda h, s: (tiles[0] * 256 // part, 0))
        specs += [part_spec(0), part_spec(pairs), part_table, part_table]
        outs += [jax.ShapeDtypeStruct((part, head_width), bf16)] * 2
        out_specs += [pl.BlockSpec((part, 128), lambda h, s: (0, h))] * 2
    if own:
        args += [joined, joined]
        specs += [half_spec(pairs), half_spec(2 * pairs)]
        outs += [jax.ShapeDtypeStruct((count, head_width), bf16)] * 2
        out_specs += [rows_spec] * 2
    if own or last:
        args += [tables[0], tables[1]]
        specs += [whole, whole]
    if not first:
        args += [before]
        specs += [rows_spec]
    return pl.pallas_call(
        lambda *refs: backward_kernel(first, last, tiles, own, *refs),
        grid_spec=pltpu.PrefetchScalarGridSpec(
            num_scalar_prefetch=1,
            grid=(pairs,),
            in_specs=specs,
            out_specs=out_specs,
            scratch_shapes=[pltpu.VMEM((count, 128), f32)],
        ),
        out_shape=outs,
        compiler_params=pltpu.CompilerParams(vmem_limit_bytes=48 * 2**20),
        cost_estimate=LONG,
        name="attend_back",
    )(info, *args)


def split_three(values):
    high = lax.reduce_precision(values, 8, 7)
    rest = values - high
    mid = lax.reduce_precision(rest, 8, 7)
    return high, mid, rest - mid


def pick(x, index, axis):
    return lax.dynamic_index_in_dim(x, index, axis, keepdims=False)


def body(
    block_input,
    cotangent,
    w_qkv,
    w_out,
    w_up,
    w_down,
    w_mod,
    time_table,
    prompt_len,
    cont_len,
    timestep,
):
    count, width = block_input.shape
    tiles = count // CONT
    dp_count = lax.axis_size("dp")
    tensor_count = lax.axis_size("tensor")
    devices = dp_count * tensor_count
    role = lax.axis_index("tensor")
    is_prompt = role == 0
    me = lax.axis_index("dp")
    core, near, far = me % 2, (me // 2) % 2, me // 4
    fars = far_count()
    low_bits = far_bits()
    high_bits = list(reversed(low_bits))
    head_width = w_qkv.shape[2]
    half = count // 2

    def far_bit(bit):
        return (far // bit) % 2

    far_top, far_rest = high_bits[0], high_bits[1:]
    cuts = (head_width, w_up.shape[1], w_down.shape[0])
    table_rows, rows_each = time_table.shape[0], w_qkv.shape[0]
    steps = jnp.pad(timestep.reshape(1, -1), ((0, rows_each - 1), (0, 128 - SEGS))).astype(bf16)
    table_width = table_rows * width // rows_each
    table_width += -table_width % 128
    table_part = time_table.reshape(-1)
    table_part = jnp.pad(table_part, (0, rows_each * table_width - table_part.shape[0]))
    table_part = table_part.reshape(rows_each, table_width)
    first = [w_qkv.reshape(rows_each, -1), table_part, steps]
    first_cuts = (first[0].shape[1], table_width + 128)
    first = jnp.concatenate(first, 1)[None]
    bounds = [0, count // 4, count * 5 // 8, count]
    x_parts = [block_input[bounds[n] : bounds[n + 1]] for n in range(3)]
    rest = jnp.concatenate([w_out.T, w_up, w_down.T], 1)[None]
    came_first = swap(first, 8 * far_top)
    first, came_first, x_parts, rest = tie(first, came_first, x_parts, rest)
    came = [swap(x_parts[0], TENSOR)]
    for bit in far_rest:
        first = join(first, came_first, far_bit(2 * bit))
        came_first = swap(first, 8 * bit)
    came_first, first, came, rest = tie(came_first, first, came, rest)
    qkv_far, table_far = join(first, came_first, far_bit(1), first_cuts)

    table_near = [swap(table_far, bits) for bits in (NEAR, TENSOR, NEAR + TENSOR)]
    qkv_near = [swap(qkv_far, bits) for bits in (NEAR, TENSOR)]
    table_own = join(table_far, table_near[0], near)
    table_other = join(table_near[1], table_near[2], near)
    table_came = [swap(table_own, CORE), swap(table_other, CORE)]
    table_cuts = (table_width, 128)
    packets = [
        join(table_own, table_came[0], core, table_cuts),
        join(table_other, table_came[1], core, table_cuts),
    ]
    rest_came = swap(rest, 8 * far_top)

    turns = HEAD_DIM // 2
    freqs = 10000.0 ** (-(jnp.arange(128, dtype=jnp.int32) % turns).astype(f32) / turns)
    inside = jnp.arange(count, dtype=jnp.int32)
    prompt_count = prompt_len[0]
    own_places = jnp.where(is_prompt, inside, prompt_count + inside % CONT).astype(f32)
    own_angles = own_places[:, None] * freqs[None, :]
    prompt_angles = inside.astype(f32)[:, None] * freqs[None, :]
    tables = (jnp.cos(own_angles), jnp.sin(own_angles), jnp.cos(prompt_angles), jnp.sin(prompt_angles))
    own_len = jnp.where(
        is_prompt,
        jnp.clip(prompt_count - CONT * jnp.arange(NCONT, dtype=jnp.int32), 0, CONT),
        cont_len[0],
    )
    info = jnp.concatenate(
        [jnp.stack([role, prompt_count]), own_len, jnp.stack([core, near, far])]
    ).astype(jnp.int32)

    table_full = jnp.concatenate([packets[0][0], packets[1][0]], 0)
    table_full = table_full.reshape(2 * dp_count, -1)[:, : table_rows * width]
    table_full = table_full.reshape(STEPS, width)
    step_rows = packets[0][1][:, 0, :SEGS].astype(jnp.int32)
    row_ids = (jnp.arange(2)[:, None, None] + role) % 2 * table_rows + (
        jnp.arange(dp_count)[None, :, None] * 2 * table_rows + jnp.arange(table_rows)
    )
    row_ids = row_ids.reshape(-1).astype(jnp.int32)
    step_pad = jnp.pad(step_rows, ((0, 0), (0, 16 - SEGS))).reshape(-1)
    chosen = (step_pad[:, None] == row_ids[None, :]).astype(bf16)
    cond = dot(chosen, table_full).astype(bf16)
    col_width = w_mod.shape[1]
    col_part = dot(cond, w_mod).reshape(dp_count, 1, 16, col_width)
    col_part = jnp.broadcast_to(col_part, (dp_count, tensor_count, 16, col_width))
    col_part = col_part.reshape(devices, 16, col_width).astype(f32)
    arrived = lax.all_to_all(col_part, BOTH, 0, 0, tiled=True)
    qkv_far, qkv_near, rest, rest_came, tables, info, _ = tie(
        qkv_far, qkv_near, rest, rest_came, tables, info, col_part
    )
    qkv_near.append(swap(qkv_far, NEAR + TENSOR))
    rest = join(rest, rest_came, far_bit(far_top), None if far_rest else cuts)
    if far_rest:
        rest_came = swap(rest, 8 * far_rest[0])

    qkv_far, qkv_near, arrived, came, x_parts = tie(qkv_far, qkv_near, arrived, came, x_parts)
    came.append(swap(x_parts[1], TENSOR))
    mods = jnp.transpose(arrived, (1, 0, 2)).reshape(16, 6 * width).astype(f32)
    qkv_own = join(qkv_far, qkv_near[0], near)
    qkv_other = join(qkv_near[1], qkv_near[2], near)
    qkv_came = [swap(qkv_own, CORE), swap(qkv_other, CORE)]
    for bit in far_rest[1:]:
        rest = join(rest, rest_came, far_bit(bit * 2))
        rest_came = swap(rest, 8 * bit)
    qkv = [
        join(own, other, core).reshape(width, -1)
        for own, other in zip((qkv_own, qkv_other), qkv_came)
    ]
    rest, rest_came, mods, qkv, came, x_parts = tie(rest, rest_came, mods, qkv, came, x_parts)

    came.append(swap(x_parts[2], TENSOR))
    o_own, u_own, d_own = join(rest, rest_came, far_bit(1), cuts) if far_rest else rest
    u_near, o_near, o_other = swap(u_own, NEAR), swap(o_own, NEAR), swap(o_own, TENSOR)
    joined, normed = project(
        project_own_kernel, 3, LONG, info, [block_input], mods, qkv, tables[:2]
    )
    came, joined, u_near = tie(came, joined, u_near)
    prompts, prompt_normed = project(
        project_prompt_kernel, 2, LONG, info, [block_input, *came], mods, qkv, tables[2:]
    )
    u_near, o_near, o_other, u_own, o_own, d_own, prompts = tie(
        u_near, o_near, o_other, u_own, o_own, d_own, prompts
    )
    d_near, u_other, oo_near = swap(d_own, NEAR), swap(u_own, TENSOR), swap(o_other, NEAR)
    u_own, o_own = join(u_own, u_near, near), join(o_own, o_near, near)
    u_core = swap(u_own, CORE)
    out_0, lse_0 = attend(info, *tie(joined, prompts, u_own, o_own)[:2], 0)
    d_near, u_other, oo_near, u_core, d_own, u_own, o_own, o_other, out_0, joined = tie(
        d_near, u_other, oo_near, u_core, d_own, u_own, o_own, o_other, out_0, joined
    )
    d_other, uu_near = swap(d_own, TENSOR), swap(u_other, NEAR)
    d_own, o_other = join(d_own, d_near, near), join(o_other, oo_near, near)
    d_core, o_core, oo_core = swap(d_own, CORE), swap(o_own, CORE), swap(o_other, CORE)
    up_0 = join(u_own, u_core, core).reshape(width, -1)
    out_1, lse_1 = attend(info, *tie(joined, prompts, d_own, o_other, up_0)[:2], 1)
    d_other, uu_near, d_core, o_core, oo_core, d_own, o_own, o_other, u_other, out_1 = tie(
        d_other, uu_near, d_core, o_core, oo_core, d_own, o_own, o_other, u_other, out_1
    )
    attended, lses = [out_0, out_1], [lse_0, lse_1]
    out_t = [
        join(o_own, o_core, core).reshape(width, -1),
        join(o_other, oo_core, core).reshape(width, -1),
    ]
    branch, middle, normed_two = middle_norm(info, block_input, attended, mods, out_t)

    dd_near = swap(d_other, NEAR)
    u_other = join(u_other, uu_near, near)
    uu_core = swap(u_other, CORE)
    down_0 = join(d_own, d_core, core).reshape(width, -1)
    d_other, u_other, normed_two, down_0 = tie(d_other, u_other, normed_two, down_0)
    mlp, n2_grad, d_keep_0, d_send_0, u_keep_0, u_send_0, *shared = feed_forward(
        info, normed_two, (cotangent, mods), up_0, down_0
    )
    dd_near, uu_core, d_other, u_other, mlp, d_send_0, u_send_0 = tie(
        dd_near, uu_core, d_other, u_other, mlp, d_send_0, u_send_0
    )
    d_other = join(d_other, dd_near, near)
    dd_core = swap(d_other, CORE)
    up_1 = join(u_other, uu_core, core).reshape(width, -1)
    down_1 = join(d_other, dd_core, core).reshape(width, -1)
    up_1, down_1, mlp, d_send_0, u_send_0 = tie(up_1, down_1, mlp, d_send_0, u_send_0)
    d_came_0, u_came_0 = swap(d_send_0, CORE), swap(u_send_0, CORE)
    mlp, n2_grad, d_keep_1, d_send_1, u_keep_1, u_send_1 = feed_forward(
        info, normed_two, (*shared, mlp, n2_grad), up_1, down_1
    )
    d_came_0, u_came_0, mlp, d_send_1, u_send_1 = tie(d_came_0, u_came_0, mlp, d_send_1, u_send_1)
    d_came_1, u_came_1 = swap(d_send_1, CORE), swap(u_send_1, CORE)
    block_output, middle_grad, grad_0, grad_1, post_sums, o_keep, o_send = post(
        info, middle, branch, mlp, n2_grad, cotangent, attended, mods, out_t
    )
    d_came_1, u_came_1, o_keep, o_send, grad_0, grad_1 = tie(
        d_came_1, u_came_1, o_keep, o_send, grad_0, grad_1
    )

    def by_near(x):
        return x.reshape((2, 2, fars) + x.shape[2:])

    def near_part(keep, came, part):
        half_of = slice(part * fars, (part + 1) * fars)
        return plus(keep[half_of], came[half_of])

    o_came = swap(o_send, CORE)
    d_send = [near_part(d_keep_0, d_came_0, 1), near_part(d_keep_1, d_came_1, 1)]
    d_keep = [near_part(d_keep_0, d_came_0, 0), near_part(d_keep_1, d_came_1, 0)]
    u_send, u_keep = plus(u_keep_1, u_came_1), plus(u_keep_0, u_came_0)
    d_came, u_came = swap(jnp.stack(d_send), NEAR), swap(u_send, TENSOR)
    d_keep, u_keep, grad_1 = tie(d_keep, u_keep, grad_1)

    def back(t, grad, blocks, own, before=None, last=True):
        return attend_back(
            info, joined, prompts, t, grad, attended[t], lses[t], tables, blocks, own, before, last
        )

    wq, wk, wv = (
        [qkv[t][:, n * head_width : (n + 1) * head_width] for t in range(2)] for n in range(3)
    )

    def prompt_part(t, dk, dv):
        return dot(dk, wk[t], NT) + dot(dv, wv[t], NT)

    def own_part(t, dq, dk, dv):
        return dot(dq, wq[t], NT) + dot(dk, wk[t], NT) + dot(dv, wv[t], NT)

    def weight_part(dq, dk, dv, dk_prompt, dv_prompt):
        parts = [
            dot(normed, dq, TN),
            dot(normed, dk, TN) + dot(prompt_normed, dk_prompt, TN),
            dot(normed, dv, TN) + dot(prompt_normed, dv_prompt, TN),
        ]
        whole = jnp.concatenate(parts, 1).astype(bf16)
        return whole.reshape(fars, 2, 2, -1, whole.shape[1])

    dq_1, dkp_1, dvp_1, dk_1, dv_1 = back(1, grad_1, (0, 1, 2, 3), True)
    d_came, u_came, o_came, d_keep, u_keep, o_keep, grad_0, dq_1, dkp_1, dvp_1, dk_1, dv_1 = tie(
        d_came, u_came, o_came, d_keep, u_keep, o_keep, grad_0, dq_1, dkp_1, dvp_1, dk_1, dv_1
    )
    o_cur = by_near(plus(o_keep, o_came))
    d_keep, d_send = plus(d_keep[0], d_came[0]), plus(d_keep[1], d_came[1])
    u_keep, u_send = near_part(u_keep, u_came, 0), near_part(u_keep, u_came, 1)
    d_came, u_came = swap(d_send, TENSOR), swap(u_send, NEAR)
    o_came = swap(o_cur[:, 1], NEAR)
    o_keep = o_cur[:, 0]
    q_cur = weight_part(dq_1, dk_1, dv_1, dkp_1, dvp_1)
    q_came = swap(pick(q_cur, 1 - core, 2), CORE)
    q_keep = pick(q_cur, core, 2)
    own_sum = own_part(1, dq_1, dk_1, dv_1)
    prompt_sum = prompt_part(1, dkp_1, dvp_1)
    q_keep, own_sum, prompt_sum, grad_0, d_keep, u_keep, o_keep = tie(
        q_keep, own_sum, prompt_sum, grad_0, d_keep, u_keep, o_keep
    )

    dq_0, dkp_a, dvp_a = back(0, grad_0, (0, 1), False, None, False)
    q_came, d_came, u_came, o_came, q_keep, d_keep, u_keep, o_keep, dq_0, dkp_a, dvp_a = tie(
        q_came, d_came, u_came, o_came, q_keep, d_keep, u_keep, o_keep, dq_0, dkp_a, dvp_a
    )
    sum_a = prompt_sum[:half] + prompt_part(0, dkp_a, dvp_a)
    came_a = swap(sum_a.astype(bf16), TENSOR)
    d_keep, d_send = send_far(plus(d_keep, d_came))
    u_keep, u_send = send_far(plus(u_keep, u_came))
    o_cur = plus(o_keep, o_came)
    q_cur = plus(q_keep, q_came)
    d_came, u_came = swap(d_send, 8), swap(u_send, 8)
    o_came, o_keep = swap(o_cur[1], TENSOR), o_cur[0]
    q_came, q_keep = swap(pick(q_cur, 1 - near, 1), NEAR), pick(q_cur, near, 1)
    sum_a, d_keep, u_keep, o_keep, q_keep, dq_0 = tie(sum_a, d_keep, u_keep, o_keep, q_keep, dq_0)

    dq_0, dkp_b, dvp_b, dk_0, dv_0 = back(0, grad_0, (2, 3), True, dq_0, True)
    came, keep, grads = tie(
        (came_a, d_came, u_came, o_came, q_came),
        (d_keep, u_keep, o_keep, q_keep),
        (dkp_b, dvp_b, dk_0, dv_0, dq_0),
    )
    came_a, d_came, u_came, o_came, q_came = came
    d_keep, u_keep, o_keep, q_keep = keep
    dkp_b, dvp_b, dk_0, dv_0, dq_0 = grads
    sum_b = prompt_sum[half:] + prompt_part(0, dkp_b, dvp_b)
    came_b = swap(sum_b.astype(bf16), TENSOR)
    sum_b, dq_0, dk_0, dv_0 = tie(sum_b, dq_0, dk_0, dv_0)

    def far_end(keep, came):
        for bit in low_bits[1:]:
            keep, send = send_far(plus(keep, came))
            came = swap(send, 8 * bit)
        return keep, came

    d_keep, d_came = far_end(d_keep, d_came)
    u_keep, u_came = far_end(u_keep, u_came)
    o_keep, o_send = send_far(plus(o_keep, o_came))
    o_came = swap(o_send, 8)
    q_other = swap(plus(q_keep, q_came), TENSOR)
    dkp_0, dvp_0 = jnp.concatenate([dkp_a, dkp_b], 0), jnp.concatenate([dvp_a, dvp_b], 0)
    q_cur = weight_part(dq_0, dk_0, dv_0, dkp_0, dvp_0)
    q_came, q_keep = swap(pick(q_cur, 1 - core, 2), CORE), pick(q_cur, core, 2)
    own_sum = own_sum + own_part(0, dq_0, dk_0, dv_0)
    q_came, q_keep, own_sum = tie(q_came, q_keep, own_sum)
    q_cur = plus(q_keep, q_came)
    q_came, q_keep = swap(pick(q_cur, 1 - near, 1), NEAR), pick(q_cur, near, 1)
    d_came, u_came, o_came, q_other, own_sum, o_keep, d_keep, u_keep, came_b = tie(
        d_came, u_came, o_came, q_other, own_sum, o_keep, d_keep, u_keep, came_b
    )
    input_grad, last_sums = last(
        info,
        block_input,
        own_sum,
        jnp.concatenate([sum_a, sum_b], 0),
        jnp.concatenate([came_a, came_b], 0),
        middle_grad,
        mods,
    )
    q_came, q_keep, last_sums, d_keep, u_keep = tie(q_came, q_keep, last_sums, d_keep, u_keep)
    down_grad = (d_keep.astype(f32) + d_came.astype(f32))[0]
    up_grad = (u_keep.astype(f32) + u_came.astype(f32))[0]
    o_keep, o_came = far_end(o_keep, o_came)
    out_grad = (o_keep.astype(f32) + o_came.astype(f32))[0]
    q_cur = q_keep.astype(f32) + q_came.astype(f32) + q_other.astype(f32)
    q_cur = q_cur.reshape((2,) * len(low_bits) + q_cur.shape[1:])
    for bit in low_bits:
        axis = q_cur.ndim - 3
        mine = (far // bit) % 2
        q_cur = q_cur.astype(bf16)
        came = swap(pick(q_cur, 1 - mine, axis), 8 * bit)
        q_cur = pick(q_cur, mine, axis).astype(f32) + came.astype(f32)

    order = [last_sums[:, 0], last_sums[:, 1]] + [post_sums[:, n] for n in range(4)]
    sums = jnp.stack(order, 1).reshape(tiles, 6 * width)
    first_row = (jnp.arange(tiles) == 0)[:, None]
    prompt_sums = jnp.where(first_row, jnp.sum(sums, 0, keepdims=True), 0.0)
    segment_sums = jnp.where(is_prompt, prompt_sums, sums).astype(bf16)

    local = jnp.concatenate(
        [
            jnp.sum(post_sums[:, 4:7], (0, 2)),
            (jnp.sum(own_len) * width).astype(f32).reshape(1),
        ]
    )
    local = jnp.concatenate(split_three(local))
    local = jnp.pad(local, (0, col_width - 12)).astype(bf16)
    packet = segment_sums.reshape(tiles, devices, col_width).transpose(1, 0, 2)
    packet = jnp.concatenate(
        [packet, jnp.broadcast_to(local[None, None], (devices, 1, col_width))], 1
    )
    packet = jnp.pad(packet, ((0, 0), (0, 16 - packet.shape[1]), (0, 0)))
    packets = lax.all_to_all(packet, BOTH, 0, 0, tiled=True)
    totals = jnp.sum(packets[:, tiles, :12].astype(f32), 0)
    totals = totals[:4] + totals[4:8] + totals[8:12]
    stats = jnp.sqrt(totals[:3] / totals[3])

    grads = packets[:, :tiles].reshape(devices * tiles, col_width)
    cond_groups = cond.reshape(dp_count, 16, width)
    own_steps = step_pad.reshape(dp_count, 16)
    cond_rows = jnp.stack([cond_groups[:, :tiles], cond_groups[:, 1 : 1 + tiles]], 1)
    step_slots = jnp.stack([own_steps[:, :tiles], own_steps[:, 1 : 1 + tiles]], 1).reshape(-1)
    mod_grad = dot(cond_rows.reshape(devices * tiles, width), grads, TN)
    condition_grad = dot(grads, w_mod, NT)
    slot_pick = (step_slots[:, None] == jnp.arange(STEPS, dtype=jnp.int32)[None, :]).astype(f32)
    table_part = lax.dot_general(
        slot_pick,
        condition_grad,
        TN,
        precision=lax.Precision.HIGHEST,
        preferred_element_type=f32,
    )
    table_pieces = lax.all_to_all(
        table_part.astype(bf16).reshape(devices, table_rows, width), BOTH, 0, 0, tiled=True
    )
    table_grad = jnp.sum(table_pieces.astype(f32), 0)
    return (
        block_output,
        input_grad,
        q_cur.reshape(w_qkv.shape),
        out_grad.T,
        up_grad,
        down_grad.T,
        mod_grad,
        table_grad,
        stats,
    )


def solution(mesh):
    return jax.shard_map(
        body,
        mesh=mesh,
        in_specs=(
            P(("dp", "tensor"), None),
            P(("dp", "tensor"), None),
            P("dp", None, "tensor"),
            P("tensor", "dp"),
            P("dp", "tensor"),
            P("tensor", "dp"),
            P(None, ("dp", "tensor")),
            P(("dp", "tensor"), None),
            P("dp"),
            P("dp", None),
            P("dp", None),
        ),
        out_specs=(
            P(("dp", "tensor"), None),
            P(("dp", "tensor"), None),
            P("dp", None, "tensor"),
            P("tensor", "dp"),
            P("dp", "tensor"),
            P("tensor", "dp"),
            P(None, ("dp", "tensor")),
            P(("dp", "tensor"), None),
            P(),
        ),
        check_vma=False,
    )
```

time: 613 us -> 460 us (0.75)
  Pallas kernels: 75.9 us -> 181 us
  matrix products: 127 us -> 30.1 us
  other arithmetic: 90.8 us -> 21.6 us
  waiting for transfers between devices: 154 us -> 89.6 us
  starting transfers between devices: 109 us -> 87 us
    pallas_call x6 -> x34, Pallas kernels: 51.1 us -> 156 us  [the longest x2 59.5 us: feed_forward(): pl.pallas_call(lambda *refs: mlp_kernel(first, *refs), grid_spec=pltpu.Pr...]
    dot_general x42 -> x26, matrix products: 125 us -> 28.7 us  [dot(): return lax.dot_general(left, right, dims, preferred_element_type=f32)]
    ppermute x42 -> x58, waiting for transfers between devices: 132 us -> 74.1 us  [swap(): return lax.ppermute(x, BOTH, [(i, i ^ bits) for i in range(count)])]
    another operation x42 -> x5, other arithmetic: 30.8 us -> 1.96 us  [the longest x1 1.12 us: body(): d_came, u_came = (swap(jnp.stack(d_send), NEAR), swap(u_send, TENSOR))]
    convert_element_type x24 -> x18, other arithmetic: 20.2 us -> 6.17 us  [the longest x14 5.92 us: plus(): return (left.astype(f32) + right.astype(f32)).astype(bf16)]
    ppermute x42 -> x58, starting transfers between devices: 88.8 us -> 75.6 us  [swap(): return lax.ppermute(x, BOTH, [(i, i ^ bits) for i in range(count)])]
    slice x18 -> x5, local copies, waits for them, and re-layouts: 14.5 us -> 4.13 us  [the longest x2 3.35 us: body(): x_parts = [block_input[bounds[n]:bounds[n + 1]] for n in range(3)]]
    all_to_all x4 -> x3, starting transfers between devices: 20.6 us -> 11.4 us  [the longest x1 4.32 us: body(): arrived = lax.all_to_all(col_part, BOTH, 0, 0, tiled=True)]
  transfers between devices with their start and end apart: 46 -> 61, of which waited for: 18 -> 24; matrix products, arithmetic and copies ran while one was open for 19% -> 12% of each run, Pallas kernels for 7% -> 36%
where the time goes in v2:
time: 460 us; the launch traced here: 456 us
  Pallas kernels  181 us (39%)
  waiting for transfers between devices  89.6 us (19%)
  starting transfers between devices  87 us (19%)
  local copies, waits for them, and re-layouts  43 us (9%)
  matrix products  30.1 us (7%)
  other arithmetic  21.6 us (5%)
    ppermute x58, starting transfers between devices, swap(): return lax.ppermute(x, BOTH, [(i, i ^ bits) for i in range(count)])  75.6 us
    ppermute x58, waiting for transfers between devices, swap(): return lax.ppermute(x, BOTH, [(i, i ^ bits) for i in range(count)])  74.1 us
    pallas_call x2, Pallas kernels, feed_forward(): pl.pallas_call(lambda *refs: mlp_kernel(first, *refs), grid_spec=pltpu.Pr...  59.5 us
    pallas_call x3, Pallas kernels, attend_back(): pl.pallas_call(lambda *refs: backward_kernel(first, last, tiles, own, *re...  38.5 us
    dot_general x26, matrix products, dot(): return lax.dot_general(left, right, dims, preferred_element_type=f32)  28.7 us
    pallas_call x2, Pallas kernels, attend(): pl.pallas_call(forward_kernel, grid_spec=pltpu.PrefetchScalarGridSpec(num...  24.3 us
    unnamed x199, local copies, waits for them, and re-layouts  23.2 us
    pallas_call x2, Pallas kernels, project(): pl.pallas_call(kernel, grid_spec=pltpu.PrefetchScalarGridSpec(num_scalar_...  19.9 us
  transfers between devices with their start and end apart: 61, of which 24 were waited for; matrix products, arithmetic and copies ran while one was open for 12% of the time, Pallas kernels for 36%

profile of v2, /device:TPU:0, one launch (start us, length us, event | category | flops | bytes accessed | tf_op | source)
XLA Modules:
  0.0 456.0 jit_solution(7981002334882047310)
XLA Ops:
  16.7 5.4 %multiply_sine_fusion = (f32[1024,128]{1,0:T(8,128)}, f32[1024,128]{1,0:T(8,128)}, f32[1024,128]{1,0:T(8,128)}, f32[1024,128]{1,0:T(8,128)}) fusion(f32[1024]{0:T(1024)S(1)} %get-tuple-element.560, f32[128]{0:T(128)S(1)} %fusion.68, f32[1024]{0:T(1024)S(1)} %get-tuple-element.559), kind=kLoop, calls=%fused_computation.53 | loop fusion | flops 262144 | bytes 2105856 | tf_op jit(solution)/shard_map/sin | solution.py:893
  44.5 9.5 %collective-permute-done.5.refs_2_ = bf16[1,48,3456]{2,1,0:T(8,128)(2,1)S(1)} collective-permute-done((bf16[1,48,3456]{2,1,0:T(8,128)(2,1)S(1)}, bf16[1,48,3456]{2,1,0:T(8,128)(2,1)S(1)}, u32[]{:S(2)}, u32[]{:S(2)}) %collective-permute-start.5) | collective-permute-done | bytes 331808 | tf_op jit(solution)/shard_map/ppermute | solution.py:46
  54.8 6.4 %all-to-all-done = f32[32,16,144]{2,1,0:T(8,128)} async-done(((f32[32,16,144]{2,1,0:T(8,128)}), f32[32,16,144]{2,1,0:T(8,128)}, u32[]{:S(2)}, u32[]{:S(2)}) %all-to-all-start) | async-done | bytes 294944 | tf_op jit(solution)/shard_map/all_to_all | solution.py:918
  61.1 5.0 %collective-permute-done.12.refs_2_ = bf16[4,48,1152]{2,1,0:T(8,128)(2,1)S(1)} collective-permute-done((bf16[4,48,1152]{2,1,0:T(8,128)(2,1)S(1)}, bf16[4,48,1152]{2,1,0:T(8,128)(2,1)S(1)}, u32[]{:S(2)}, u32[]{:S(2)}) %collective-permute-start.12) | collective-permute-done | bytes 442400 | tf_op jit(solution)/shard_map/ppermute | solution.py:46
  82.7 4.6 %collective-permute-done.11.refs_2_ = bf16[2,48,3456]{2,1,0:T(8,128)(2,1)S(1)} collective-permute-done((bf16[2,48,3456]{2,1,0:T(8,128)(2,1)S(1)}, bf16[2,48,3456]{2,1,0:T(8,128)(2,1)S(1)}, u32[]{:S(2)}, u32[]{:S(2)}) %collective-permute-start.11) | collective-permute-done | bytes 663584 | tf_op jit(solution)/shard_map/ppermute | solution.py:46
  92.4 11.2 %project.2 = (bf16[2,1024,1152]{2,1,0:T(8,128)(2,1)S(1)}, bf16[1024,768]{1,0:T(8,128)(2,1)S(1)}) custom-call(s32[13]{0:T(128)S(1)} %concatenate.58.info.refs_0_, bf16[1024,768]{1,0:T(8,128)(2,1)S(1)} %copy-done.9, f32[16,4608]{1,0:T(8,128)S(1)} %copy-done.28, bf16[768,1152]{1,0:T(8,128)(2,1)S(1)} %bitcast.236, bf16[768,1152]{1,0:T(8,128)(2,1)S(1)} %bitcast.245, ...), custom_call_target="tpu_custom_call" | custom-call | flops 99999997952 | bytes 1 | tf_op jit(solution)/shard_map/project/pallas_call | solution.py:220
  107.3 8.7 %project.3 = (bf16[2,1024,768]{2,1,0:T(8,128)(2,1)S(1)}, bf16[1024,768]{1,0:T(8,128)(2,1)S(1)}) custom-call(s32[13]{0:T(128)S(1)} %concatenate.58.info.refs_0_, bf16[1024,768]{1,0:T(8,128)(2,1)S(1)} %copy-done.9, bf16[256,768]{1,0:T(8,128)(2,1)S(1)} %copy-done.32, bf16[384,768]{1,0:T(8,128)(2,1)} %collective-permute-done.15.refs_1_, ...), custom_call_target="tpu_custom_call" | custom-call | flops 99999997952 | bytes 1 | tf_op jit(solution)/shard_map/project/pallas_call | solution.py:220
  122.9 12.1 %attend.2 = (bf16[1024,384]{1,0:T(8,128)(2,1)S(1)}, f32[3,2,1024]{2,1,0:T(2,128)S(1)}) custom-call(s32[13]{0:T(128)S(1)} %concatenate.58.info.refs_0_, bf16[2,1024,1152]{2,1,0:T(8,128)(2,1)S(1)} %copy-done.40, bf16[2,1024,768]{2,1,0:T(8,128)(2,1)S(1)} %get-tuple-element.312.refs_1_.refs_2_.refs_5_.refs_6_, ...), custom_call_target="tpu_custom_call" | custom-call | flops 99999997952 | bytes 1 | tf_op jit(solution)/shard_map/attend/pallas_call | solution.py:624
  136.8 4.8 %collective-permute-start.24 = (bf16[4,48,1536]{2,1,0:T(8,128)(2,1)S(1)}, bf16[4,48,1536]{2,1,0:T(8,128)(2,1)}, u32[]{:S(2)}, u32[]{:S(2)}) collective-permute-start(bf16[4,48,1536]{2,1,0:T(8,128)(2,1)S(1)} %bitcast.279), channel_id=1, source_target_pairs={{0,1},{1,0},{2,3},{3,2},{4,5},{5,4},{6,7},{7,6},{8,9},{9,8},{10,11... | collective-permute-start | bytes 1769480 | tf_op jit(solution)/shard_map/ppermute | solution.py:46
  142.9 12.3 %attend.3 = (bf16[1024,384]{1,0:T(8,128)(2,1)S(1)}, f32[3,2,1024]{2,1,0:T(2,128)S(1)}) custom-call(s32[13]{0:T(128)S(1)} %concatenate.58.info.refs_0_, bf16[2,1024,1152]{2,1,0:T(8,128)(2,1)S(1)} %copy-done.40, bf16[2,1024,768]{2,1,0:T(8,128)(2,1)S(1)} %get-tuple-element.312.refs_1_.refs_2_.refs_5_.refs_6_, ...), custom_call_target="tpu_custom_call" | custom-call | flops 99999997952 | bytes 1 | tf_op jit(solution)/shard_map/attend/pallas_call | solution.py:624
  170.1 29.7 %feed_forward.2 = (f32[1024,768]{1,0:T(8,128)}, f32[1024,768]{1,0:T(8,128)}, bf16[8,48,1536]{2,1,0:T(8,128)(2,1)S(1)}, bf16[8,48,1536]{2,1,0:T(8,128)(2,1)}, bf1...) custom-call(s32[13]{0:T(128)S(1)} %concatenate.58.info.refs_0_, ...), custom_call_target="tpu_custom_call" | custom-call | flops 99999997952 | bytes 1 | tf_op jit(solution)/shard_map/feed_forward/pallas_call | solution.py:359
  212.5 29.8 %feed_forward.3 = (f32[1024,768]{1,0:T(8,128)}, f32[1024,768]{1,0:T(8,128)}, bf16[8,48,1536]{2,1,0:T(8,128)(2,1)S(1)}, bf16[8,48,1536]{2,1,0:T(8,128)(2,1)}, bf1...) custom-call(s32[13]{0:T(128)S(1)} %concatenate.58.info.refs_0_, bf16[1024,768]{1,0:T(8,128)(2,1)} %copy-done.46, ...), custom_call_target="tpu_custom_call" | custom-call | flops 99999997952 | bytes 1 | tf_op jit(solution)/shard_map/feed_forward/pallas_call | solution.py:359
  243.4 12.2 %post.1 = (bf16[1024,768]{1,0:T(8,128)(2,1)}, f32[1024,768]{1,0:T(8,128)}, bf16[1024,384]{1,0:T(8,128)(2,1)S(1)}, bf16[1024,384]{1,0:T(8,128)(2,1)S(1)}, f32[8,8...) custom-call(s32[13]{0:T(128)S(1)} %concatenate.58.info.refs_0_, ...), custom_call_target="tpu_custom_call" | custom-call | flops 99999997952 | bytes 1 | tf_op jit(solution)/shard_map/post/pallas_call | solution.py:447
  267.4 17.1 %attend_back.3 = (bf16[1024,384]{1,0:T(8,128)(2,1)S(1)}, bf16[1024,384]{1,0:T(8,128)(2,1)S(1)}, bf16[1024,384]{1,0:T(8,128)(2,1)S(1)}, bf16[1024,384]{1,0:T(8,128)(2,1)S(1)}, bf16[1024,384]{1,0:T(8,128)(2,1)S(1)}) custom-call(s32[13]{0:T(128)S(1)} %concatenate.58.info.refs_0_, bf16[2,1024,1152]{2,1,0:T(8,128)(2,1)} %copy-done.39, ...), custom_call_target="tpu_custom_call" | custom-call | flops 99999997952 | bytes 1 | tf_op jit(solution)/shard_map/attend_back/pallas_call | solution.py:792
  284.5 7.6 %collective-permute-done.36 = bf16[2,4,48,1536]{3,2,1,0:T(8,128)(2,1)S(1)} collective-permute-done((bf16[2,4,48,1536]{3,2,1,0:T(8,128)(2,1)}, bf16[2,4,48,1536]{3,2,1,0:T(8,128)(2,1)S(1)}, u32[]{:S(2)}, u32[]{:S(2)}) %collective-permute-start.36) | collective-permute-done | bytes 1179680 | tf_op jit(solution)/shard_map/ppermute | solution.py:46
  307.2 8.0 %collective-permute-start.40 = (bf16[4,48,1536]{2,1,0:T(8,128)(2,1)S(1)}, bf16[4,48,1536]{2,1,0:T(8,128)(2,1)S(1)}, u32[]{:S(2)}, u32[]{:S(2)}) collective-permute-start(bf16[4,48,1536]{2,1,0:T(8,128)(2,1)S(1)} %get-tuple-element.524), channel_id=1, source_target_pairs={{0,1},{1,0},{2,3},{3,2},{4,5},{5,4},{6,7},{7,6},{8,9},{9,8},{10,11... | collective-permute-start | bytes 1769480 | tf_op jit(solution)/shard_map/ppermute | solution.py:46
  321.8 11.6 %attend_back.4 = (f32[1024,384]{1,0:T(8,128)S(1)}, bf16[512,384]{1,0:T(8,128)(2,1)S(1)}, bf16[512,384]{1,0:T(8,128)(2,1)S(1)}) custom-call(s32[13]{0:T(128)S(1)} %concatenate.58.info.refs_0_, bf16[2,1024,1152]{2,1,0:T(8,128)(2,1)} %copy-done.39, bf16[1024,384]{1,0:T(8,128)(2,1)S(1)} %get-tuple-element.404.refs_2_, bf16[1024,384]{1,0:T(8,128)(2,1)S(1)} %copy-done.48, ...), custom_call_target="tpu_custom_call" | custom-call | flops 99999997952 | bytes 1 | tf_op jit(solution)/shard_map/attend_back/pallas_call | solution.py:792
  345.9 9.9 %attend_back.5 = (bf16[1024,384]{1,0:T(8,128)(2,1)S(1)}, bf16[512,384]{1,0:T(8,128)(2,1)S(1)}, bf16[512,384]{1,0:T(8,128)(2,1)S(1)}, bf16[1024,384]{1,0:T(8,128)(2,1)S(1)}, bf16[1024,384]{1,0:T(8,128)(2,1)S(1)}) custom-call(s32[13]{0:T(128)S(1)} %concatenate.58.info.refs_0_, bf16[2,1024,1152]{2,1,0:T(8,128)(2,1)} %copy-done.39, ...), custom_call_target="tpu_custom_call" | custom-call | flops 99999997952 | bytes 1 | tf_op jit(solution)/shard_map/attend_back/pallas_call | solution.py:792
  355.9 6.6 %collective-permute-done.43 = bf16[512,768]{1,0:T(8,128)(2,1)S(1)} collective-permute-done((bf16[512,768]{1,0:T(8,128)(2,1)S(1)}, bf16[512,768]{1,0:T(8,128)(2,1)S(1)}, u32[]{:S(2)}, u32[]{:S(2)}) %collective-permute-start.43) | collective-permute-done | bytes 786464 | tf_op jit(solution)/shard_map/ppermute | solution.py:46
  375.0 8.2 %collective-permute-start.51 = (bf16[4,48,1152]{2,1,0:T(8,128)(2,1)S(1)}, bf16[4,48,1152]{2,1,0:T(8,128)(2,1)S(1)}, u32[]{:S(2)}, u32[]{:S(2)}) collective-permute-start(bf16[4,48,1152]{2,1,0:T(8,128)(2,1)S(1)} %add_convert_fusion.14), channel_id=1, source_target_pairs={{0,1},{1,0},{2,3},{3,2},{4,5},{5,4},{6,7},{7,6},{8,9},{9,8},{10,11... | collective-permute-start | bytes 1327112 | tf_op jit(solution)/shard_map/ppermute | solution.py:46
  390.2 9.0 %collective-permute-done.49 = bf16[1,48,1536]{2,1,0:T(8,128)(2,1)S(1)} collective-permute-done((bf16[1,48,1536]{2,1,0:T(8,128)(2,1)S(1)}, bf16[1,48,1536]{2,1,0:T(8,128)(2,1)S(1)}, u32[]{:S(2)}, u32[]{:S(2)}) %collective-permute-start.49) | collective-permute-done | bytes 147488 | tf_op jit(solution)/shard_map/ppermute | solution.py:46
  399.2 8.7 %collective-permute-done.53 = bf16[512,768]{1,0:T(8,128)(2,1)S(1)} collective-permute-done((bf16[512,768]{1,0:T(8,128)(2,1)S(1)}, bf16[512,768]{1,0:T(8,128)(2,1)S(1)}, u32[]{:S(2)}, u32[]{:S(2)}) %collective-permute-start.53) | collective-permute-done | bytes 786464 | tf_op jit(solution)/shard_map/ppermute | solution.py:46
  427.0 8.3 %collective-permute-done.55 = bf16[2,48,1152]{2,1,0:T(8,128)(2,1)S(1)} collective-permute-done((bf16[2,48,1152]{2,1,0:T(8,128)(2,1)S(1)}, bf16[2,48,1152]{2,1,0:T(8,128)(2,1)S(1)}, u32[]{:S(2)}, u32[]{:S(2)}) %collective-permute-start.55) | collective-permute-done | bytes 221216 | tf_op jit(solution)/shard_map/ppermute | solution.py:46
  446.0 9.1 %all-to-all-done.2 = bf16[32,8,768]{2,1,0:T(8,128)(2,1)S(1)} async-done(((bf16[32,8,768]{2,1,0:T(8,128)(2,1)}), bf16[32,8,768]{2,1,0:T(8,128)(2,1)S(1)}, u32[]{:S(2)}, u32[]{:S(2)}) %all-to-all-start.2) | async-done | bytes 393248 | tf_op jit(solution)/shard_map/all_to_all | solution.py:1174
  (455 shorter events, 196.4 us)
Async XLA Ops:
  29.1 25.6 %collective-permute-start.4 = (bf16[4,48,1152]{2,1,0:T(8,128)(2,1)S(1)}, bf16[4,48,1152]{2,1,0:T(8,128)(2,1)S(1)}, u32[]{:S(2)}, u32[]{:S(2)}) collective-permute-start(bf16[4,48,1152]{2,1,0:T(8,128)(2,1)S(1)} %bitcast.288), channel_id=1, source_target_pairs={{0,1},{1,0},{2,3},{3,2},{4,5},{5,4},{6,7},{7,6},{8,9},{9,8},{10,11... | collective-permute-start | bytes 1327112 | tf_op jit(solution)/shard_map/ppermute | solution.py:46
  30.7 24.1 %collective-permute-start.3 = (bf16[4,48,1152]{2,1,0:T(8,128)(2,1)S(1)}, bf16[4,48,1152]{2,1,0:T(8,128)(2,1)S(1)}, u32[]{:S(2)}, u32[]{:S(2)}) collective-permute-start(bf16[4,48,1152]{2,1,0:T(8,128)(2,1)S(1)} %bitcast.289), channel_id=1, source_target_pairs={{0,4},{1,5},{2,6},{3,7},{4,0},{5,1},{6,2},{7,3},{8,12},{9,13},{10,... | collective-permute-start | bytes 1327112 | tf_op jit(solution)/shard_map/ppermute | solution.py:46
  31.8 22.2 %collective-permute-start.5 = (bf16[1,48,3456]{2,1,0:T(8,128)(2,1)S(1)}, bf16[1,48,3456]{2,1,0:T(8,128)(2,1)S(1)}, u32[]{:S(2)}, u32[]{:S(2)}) collective-permute-start(bf16[1,48,3456]{2,1,0:T(8,128)(2,1)S(1)} %maximum_bitcast_fusion.refs_1_), channel_id=1, source_target_pairs={{0,16},{1,17},{2,18},{3,19},{4,20},{5,21},{6,22},{7,23},{8,24},{9,... | collective-permute-start | bytes 995336 | tf_op jit(solution)/shard_map/ppermute | solution.py:46
  39.5 21.6 %all-to-all-start = ((f32[32,16,144]{2,1,0:T(8,128)}), f32[32,16,144]{2,1,0:T(8,128)}, u32[]{:S(2)}, u32[]{:S(2)}) async-start(f32[32,16,144]{2,1,0:T(8,128)} %bitcast.303), calls=%async_computation | async-start | bytes 1048576 | tf_op jit(solution)/shard_map/all_to_all | solution.py:918
  68.0 19.3 %collective-permute-start.11 = (bf16[2,48,3456]{2,1,0:T(8,128)(2,1)S(1)}, bf16[2,48,3456]{2,1,0:T(8,128)(2,1)S(1)}, u32[]{:S(2)}, u32[]{:S(2)}) collective-permute-start(bf16[2,48,3456]{2,1,0:T(8,128)(2,1)S(1)} %bitcast.262), channel_id=1, source_target_pairs={{0,8},{1,9},{2,10},{3,11},{4,12},{5,13},{6,14},{7,15},{8,0},{9,1},... | collective-permute-start | bytes 1990664 | tf_op jit(solution)/shard_map/ppermute | solution.py:46
  88.3 27.7 %collective-permute-start.19 = (bf16[4,48,384]{2,1,0:T(8,128)(2,1)}, bf16[4,48,384]{2,1,0:T(8,128)(2,1)}, u32[]{:S(2)}, u32[]{:S(2)}) collective-permute-start(bf16[4,48,384]{2,1,0:T(8,128)(2,1)} %bitcast.30.refs_1_), channel_id=1, source_target_pairs={{0,1},{1,0},{2,3},{3,2},{4,5},{5,4},{6,7},{7,6},{8,9},{9,8},{10,11... | collective-permute-start | bytes 442376 | tf_op jit(solution)/shard_map/ppermute | solution.py:46
  89.5 26.6 %collective-permute-start.18 = (bf16[4,48,384]{2,1,0:T(8,128)(2,1)}, bf16[4,48,384]{2,1,0:T(8,128)(2,1)}, u32[]{:S(2)}, u32[]{:S(2)}) collective-permute-start(bf16[4,48,384]{2,1,0:T(8,128)(2,1)} %bitcast.30.refs_1_), channel_id=1, source_target_pairs={{0,4},{1,5},{2,6},{3,7},{4,0},{5,1},{6,2},{7,3},{8,12},{9,13},{10,... | collective-permute-start | bytes 442376 | tf_op jit(solution)/shard_map/ppermute | solution.py:46
  116.1 18.9 %collective-permute-start.22 = (bf16[4,48,384]{2,1,0:T(8,128)(2,1)}, bf16[4,48,384]{2,1,0:T(8,128)(2,1)S(1)}, u32[]{:S(2)}, u32[]{:S(2)}) collective-permute-start(bf16[4,48,384]{2,1,0:T(8,128)(2,1)} %collective-permute-done.19.refs_1_), channel_id=1, source_target_pairs={{0,4},{1,5},{2,6},{3,7},{4,0},{5,1},{6,2},{7,3},{8,12},{9,13},{10,... | collective-permute-start | bytes 442376 | tf_op jit(solution)/shard_map/ppermute | solution.py:46
  136.2 19.0 %collective-permute-start.28 = (bf16[8,48,384]{2,1,0:T(8,128)(2,1)S(1)}, bf16[8,48,384]{2,1,0:T(8,128)(2,1)S(1)}, u32[]{:S(2)}, u32[]{:S(2)}) collective-permute-start(bf16[8,48,384]{2,1,0:T(8,128)(2,1)S(1)} %bitcast.270), channel_id=1, source_target_pairs={{0,2},{1,3},{2,0},{3,1},{4,6},{5,7},{6,4},{7,5},{8,10},{9,11},{10,... | collective-permute-start | bytes 884744 | tf_op jit(solution)/shard_map/ppermute | solution.py:46
  136.4 18.8 %collective-permute-start.27 = (bf16[8,48,384]{2,1,0:T(8,128)(2,1)S(1)}, bf16[8,48,384]{2,1,0:T(8,128)(2,1)S(1)}, u32[]{:S(2)}, u32[]{:S(2)}) collective-permute-start(bf16[8,48,384]{2,1,0:T(8,128)(2,1)S(1)} %bitcast.268), channel_id=1, source_target_pairs={{0,2},{1,3},{2,0},{3,1},{4,6},{5,7},{6,4},{7,5},{8,10},{9,11},{10,... | collective-permute-start | bytes 884744 | tf_op jit(solution)/shard_map/ppermute | solution.py:46
  156.9 42.9 %collective-permute-start.29 = (bf16[4,48,1536]{2,1,0:T(8,128)(2,1)}, bf16[4,48,1536]{2,1,0:T(8,128)(2,1)}, u32[]{:S(2)}, u32[]{:S(2)}) collective-permute-start(bf16[4,48,1536]{2,1,0:T(8,128)(2,1)} %collective-permute-done.24.refs_1_), channel_id=1, source_target_pairs={{0,4},{1,5},{2,6},{3,7},{4,0},{5,1},{6,2},{7,3},{8,12},{9,13},{10,... | collective-permute-start | bytes 1769480 | tf_op jit(solution)/shard_map/ppermute | solution.py:46
  159.0 40.9 %collective-permute-start.30 = (bf16[8,48,1536]{2,1,0:T(8,128)(2,1)}, bf16[8,48,1536]{2,1,0:T(8,128)(2,1)}, u32[]{:S(2)}, u32[]{:S(2)}) collective-permute-start(bf16[8,48,1536]{2,1,0:T(8,128)(2,1)} %bitcast.39.refs_1_), channel_id=1, source_target_pairs={{0,2},{1,3},{2,0},{3,1},{4,6},{5,7},{6,4},{7,5},{8,10},{9,11},{10,... | collective-permute-start | bytes 3538952 | tf_op jit(solution)/shard_map/ppermute | solution.py:46
  212.0 30.3 %collective-permute-start.32 = (bf16[8,48,1536]{2,1,0:T(8,128)(2,1)}, bf16[8,48,1536]{2,1,0:T(8,128)(2,1)S(1)}, u32[]{:S(2)}, u32[]{:S(2)}) collective-permute-start(bf16[8,48,1536]{2,1,0:T(8,128)(2,1)} %get-tuple-element.341), channel_id=1, source_target_pairs={{0,2},{1,3},{2,0},{3,1},{4,6},{5,7},{6,4},{7,5},{8,10},{9,11},{10,... | collective-permute-start | bytes 3538952 | tf_op jit(solution)/shard_map/ppermute | solution.py:46
  212.1 30.3 %collective-permute-start.33 = (bf16[8,48,1536]{2,1,0:T(8,128)(2,1)}, bf16[8,48,1536]{2,1,0:T(8,128)(2,1)S(1)}, u32[]{:S(2)}, u32[]{:S(2)}) collective-permute-start(bf16[8,48,1536]{2,1,0:T(8,128)(2,1)} %get-tuple-element.342), channel_id=1, source_target_pairs={{0,2},{1,3},{2,0},{3,1},{4,6},{5,7},{6,4},{7,5},{8,10},{9,11},{10,... | collective-permute-start | bytes 3538952 | tf_op jit(solution)/shard_map/ppermute | solution.py:46
  262.4 22.1 %collective-permute-start.38 = (bf16[2,8,48,384]{3,2,1,0:T(8,128)(2,1)S(1)}, bf16[2,8,48,384]{3,2,1,0:T(8,128)(2,1)}, u32[]{:S(2)}, u32[]{:S(2)}) collective-permute-start(bf16[2,8,48,384]{3,2,1,0:T(8,128)(2,1)S(1)} %get-tuple-element.369), channel_id=1, source_target_pairs={{0,2},{1,3},{2,0},{3,1},{4,6},{5,7},{6,4},{7,5},{8,10},{9,11},{10,... | collective-permute-start | bytes 1769480 | tf_op jit(solution)/shard_map/ppermute | solution.py:46
  263.6 28.5 %collective-permute-start.36 = (bf16[2,4,48,1536]{3,2,1,0:T(8,128)(2,1)}, bf16[2,4,48,1536]{3,2,1,0:T(8,128)(2,1)S(1)}, u32[]{:S(2)}, u32[]{:S(2)}) collective-permute-start(bf16[2,4,48,1536]{3,2,1,0:T(8,128)(2,1)} %pad_maximum_fusion.4), channel_id=1, source_target_pairs={{0,4},{1,5},{2,6},{3,7},{4,0},{5,1},{6,2},{7,3},{8,12},{9,13},{10,... | collective-permute-start | bytes 3538952 | tf_op jit(solution)/shard_map/ppermute | solution.py:46
  265.1 28.5 %collective-permute-start.37 = (bf16[8,48,1536]{2,1,0:T(8,128)(2,1)S(1)}, bf16[8,48,1536]{2,1,0:T(8,128)(2,1)S(1)}, u32[]{:S(2)}, u32[]{:S(2)}) collective-permute-start(bf16[8,48,1536]{2,1,0:T(8,128)(2,1)S(1)} %add_convert_fusion.1), channel_id=1, source_target_pairs={{0,1},{1,0},{2,3},{3,2},{4,5},{5,4},{6,7},{7,6},{8,9},{9,8},{10,11... | collective-permute-start | bytes 3538952 | tf_op jit(solution)/shard_map/ppermute | solution.py:46
  295.6 37.9 %collective-permute-start.42 = (bf16[2,4,48,384]{3,2,1,0:T(8,128)(2,1)}, bf16[2,4,48,384]{3,2,1,0:T(8,128)(2,1)}, u32[]{:S(2)}, u32[]{:S(2)}) collective-permute-start(bf16[2,4,48,384]{3,2,1,0:T(8,128)(2,1)} %get-tuple-element.534), channel_id=1, source_target_pairs={{0,4},{1,5},{2,6},{3,7},{4,0},{5,1},{6,2},{7,3},{8,12},{9,13},{10,... | collective-permute-start | bytes 884744 | tf_op jit(solution)/shard_map/ppermute | solution.py:46
  305.6 27.9 %collective-permute-start.39 = (bf16[4,2,48,1152]{3,2,1,0:T(8,128)(2,1)S(1)}, bf16[4,2,48,1152]{3,2,1,0:T(8,128)(2,1)S(1)}, u32[]{:S(2)}, u32[]{:S(2)}) collective-permute-start(bf16[4,2,48,1152]{3,2,1,0:T(8,128)(2,1)S(1)} %get-tuple-element.520), channel_id=1, source_target_pairs={{0,2},{1,3},{2,0},{3,1},{4,6},{5,7},{6,4},{7,5},{8,10},{9,11},{10,... | collective-permute-start | bytes 2654216 | tf_op jit(solution)/shard_map/ppermute | solution.py:46
  307.2 26.2 %collective-permute-start.40 = (bf16[4,48,1536]{2,1,0:T(8,128)(2,1)S(1)}, bf16[4,48,1536]{2,1,0:T(8,128)(2,1)S(1)}, u32[]{:S(2)}, u32[]{:S(2)}) collective-permute-start(bf16[4,48,1536]{2,1,0:T(8,128)(2,1)S(1)} %get-tuple-element.524), channel_id=1, source_target_pairs={{0,1},{1,0},{2,3},{3,2},{4,5},{5,4},{6,7},{7,6},{8,9},{9,8},{10,11... | collective-permute-start | bytes 1769480 | tf_op jit(solution)/shard_map/ppermute | solution.py:46
  336.3 19.5 %collective-permute-start.46 = (bf16[4,48,384]{2,1,0:T(8,128)(2,1)S(1)}, bf16[4,48,384]{2,1,0:T(8,128)(2,1)S(1)}, u32[]{:S(2)}, u32[]{:S(2)}) collective-permute-start(bf16[4,48,384]{2,1,0:T(8,128)(2,1)S(1)} %get-tuple-element.542), channel_id=1, source_target_pairs={{0,1},{1,0},{2,3},{3,2},{4,5},{5,4},{6,7},{7,6},{8,9},{9,8},{10,11... | collective-permute-start | bytes 442376 | tf_op jit(solution)/shard_map/ppermute | solution.py:46
  370.2 19.9 %collective-permute-start.50 = (bf16[2,48,384]{2,1,0:T(8,128)(2,1)S(1)}, bf16[2,48,384]{2,1,0:T(8,128)(2,1)S(1)}, u32[]{:S(2)}, u32[]{:S(2)}) collective-permute-start(bf16[2,48,384]{2,1,0:T(8,128)(2,1)S(1)} %get-tuple-element.544), channel_id=1, source_target_pairs={{0,8},{1,9},{2,10},{3,11},{4,12},{5,13},{6,14},{7,15},{8,0},{9,1},... | collective-permute-start | bytes 221192 | tf_op jit(solution)/shard_map/ppermute | solution.py:46
  375.0 24.2 %collective-permute-start.51 = (bf16[4,48,1152]{2,1,0:T(8,128)(2,1)S(1)}, bf16[4,48,1152]{2,1,0:T(8,128)(2,1)S(1)}, u32[]{:S(2)}, u32[]{:S(2)}) collective-permute-start(bf16[4,48,1152]{2,1,0:T(8,128)(2,1)S(1)} %add_convert_fusion.14), channel_id=1, source_target_pairs={{0,1},{1,0},{2,3},{3,2},{4,5},{5,4},{6,7},{7,6},{8,9},{9,8},{10,11... | collective-permute-start | bytes 1327112 | tf_op jit(solution)/shard_map/ppermute | solution.py:46
  383.2 24.7 %collective-permute-start.53 = (bf16[512,768]{1,0:T(8,128)(2,1)S(1)}, bf16[512,768]{1,0:T(8,128)(2,1)S(1)}, u32[]{:S(2)}, u32[]{:S(2)}) collective-permute-start(bf16[512,768]{1,0:T(8,128)(2,1)S(1)} %get-tuple-element.557), channel_id=1, source_target_pairs={{0,1},{1,0},{2,3},{3,2},{4,5},{5,4},{6,7},{7,6},{8,9},{9,8},{10,11... | collective-permute-start | bytes 2359304 | tf_op jit(solution)/shard_map/ppermute | solution.py:46
  (135 other events, 1270.4 us)

commit v3 on v2

--- a/solution.py
+++ b/solution.py
@@ -234,7 +234,7 @@
             jax.ShapeDtypeStruct((2, count, parts * head_width), bf16),
             jax.ShapeDtypeStruct((count, width), bf16),
         ],
-        compiler_params=pltpu.CompilerParams(vmem_limit_bytes=32 * 2**20),
+        compiler_params=pltpu.CompilerParams(vmem_limit_bytes=20 * 2**20),
         cost_estimate=estimate,
         name="project",
     )(info, *inputs, mods, *qkv, *tables)
@@ -283,7 +283,7 @@
             jax.ShapeDtypeStruct((count, width), f32),
             jax.ShapeDtypeStruct((count, width), bf16),
         ],
-        compiler_params=pltpu.CompilerParams(vmem_limit_bytes=32 * 2**20),
+        compiler_params=pltpu.CompilerParams(vmem_limit_bytes=16 * 2**20),
         cost_estimate=LONG,
         name="middle_norm",
     )(info, x, *attended, mods, *out_t)
@@ -344,7 +344,9 @@
     pieces = (dp_count // 2, width // dp_count, hidden_width)
 
     def whole(array):
-        return pl.BlockSpec(array.shape, lambda b, s: (0,) * array.ndim)
+        return pl.BlockSpec(
+            array.shape, lambda b, s: (0,) * array.ndim, pipeline_mode=pl.Buffered(1)
+        )
 
     piece_spec = pl.BlockSpec(pieces[:2] + (cols,), lambda b, s: (0, 0, b))
     weight_spec = pl.BlockSpec((width, cols), lambda b, s: (0, b))
@@ -366,7 +368,7 @@
             scratch_shapes=[pltpu.VMEM((count, cols), bf16), pltpu.VMEM((count, cols), bf16)],
         ),
         out_shape=outs,
-        compiler_params=pltpu.CompilerParams(vmem_limit_bytes=52 * 2**20),
+        compiler_params=pltpu.CompilerParams(vmem_limit_bytes=32 * 2**20),
         cost_estimate=LONG,
         name="feed_forward",
     )(info, n2, *sources, up, down)
@@ -480,7 +482,7 @@
             jax.ShapeDtypeStruct(pieces, bf16),
             jax.ShapeDtypeStruct(pieces, bf16),
         ],
-        compiler_params=pltpu.CompilerParams(vmem_limit_bytes=48 * 2**20),
+        compiler_params=pltpu.CompilerParams(vmem_limit_bytes=32 * 2**20),
         cost_estimate=LONG,
         name="post",
     )(info, middle, branch, mlp, n2_grad, cotangent, *attended, mods, *out_t)
@@ -519,7 +521,7 @@
             jax.ShapeDtypeStruct((count, width), f32),
             jax.ShapeDtypeStruct((count // CONT, 8, width), f32),
         ],
-        compiler_params=pltpu.CompilerParams(vmem_limit_bytes=32 * 2**20),
+        compiler_params=pltpu.CompilerParams(vmem_limit_bytes=16 * 2**20),
         cost_estimate=LONG,
         name="last",
     )(info, x, own_sum, prompt_sum, came, middle_grad, mods)
@@ -587,28 +589,23 @@
             sel, q, k, v = prepare(h)
             own_k = jnp.where(sel, ko_ref[...], jnp.zeros((), bf16))
             own_v = jnp.where(sel, vo_ref[...], jnp.ones((), bf16))
-            heads = []
+            heads, far, near, tops = [], [], [], []
+            col, line = lanes((CONT, CONT)), rows((CONT, CONT))
+            cuts = [slice(r, r + CONT) for r in range(0, count, CONT)]
+            for n, cut in enumerate(cuts):
+                fine = (col <= line) & (col < info[2 + n])
+                near.append(jnp.where(fine, dot(q[cut], own_k[cut], NT), NEG))
+            near = jnp.concatenate(near, 0)
+            near_tops = jnp.max(near, 1, keepdims=True)
             for i in range(blocks):
-                start, stop = i * tile, (i + 1) * tile
-                s = dot(q[start:stop], k, NT)
-                cuts = [slice(r, r + CONT) for r in range(start, stop, CONT)]
-                near = []
-                for cut in cuts:
-                    piece = dot(q[cut], own_k[cut], NT)
-                    col, line = lanes((CONT, CONT)), rows((CONT, CONT))
-                    fine = (col <= line) & (col < info[2 + cut.start // CONT])
-                    near.append(jnp.where(fine, piece, NEG))
-                near = jnp.concatenate(near, 0)
-                top = jnp.maximum(
-                    jnp.max(s, 1, keepdims=True), jnp.max(near, 1, keepdims=True)
-                )
-                far_weight = jnp.exp2(s * SCALE2 - top * SCALE2).astype(bf16)
-                near_weight = jnp.exp2(near * SCALE2 - top * SCALE2).astype(bf16)
-                own = [
-                    dot(near_weight[n * CONT : (n + 1) * CONT], own_v[cut])
-                    for n, cut in enumerate(cuts)
-                ]
-                heads.append(finish(h, i, dot(far_weight, v) + jnp.concatenate(own, 0), top))
+                cut = slice(i * tile, (i + 1) * tile)
+                s = dot(q[cut], k, NT)
+                tops.append(jnp.maximum(jnp.max(s, 1, keepdims=True), near_tops[cut]))
+                far.append(dot(jnp.exp2(s * SCALE2 - tops[i] * SCALE2).astype(bf16), v))
+            weight = jnp.exp2(near * SCALE2 - jnp.concatenate(tops, 0) * SCALE2).astype(bf16)
+            own = jnp.concatenate([dot(weight[cut], own_v[cut]) for cut in cuts], 0)
+            for i in range(blocks):
+                heads.append(finish(h, i, far[i] + own[i * tile : (i + 1) * tile], tops[i]))
             outs.append(heads)
         store(outs)
 
@@ -636,7 +633,7 @@
             jax.ShapeDtypeStruct((count, head_width), bf16),
             jax.ShapeDtypeStruct((pairs, 2, count), f32),
         ],
-        compiler_params=pltpu.CompilerParams(vmem_limit_bytes=40 * 2**20),
+        compiler_params=pltpu.CompilerParams(vmem_limit_bytes=20 * 2**20),
         cost_estimate=LONG,
         name="attend",
     )(info, joined, prompts, prompts, joined, joined)
@@ -720,25 +717,28 @@
             far_block(j, False)
         lane_k = lanes((CONT, CONT))
         row_k = rows((CONT, CONT))
-        for i in range(count // CONT if own else 0):
-            cut = slice(i * CONT, (i + 1) * CONT)
-            key_parts, value_parts, query_part = [], [], None
-            for h in range(2):
-                sel = (lane_k // 64) == h
-                k = jnp.where(sel, ko_ref[cut, :], none)
-                v = jnp.where(sel, vo_ref[cut, :], none)
+        every = range(count // CONT if own else 0)
+        cuts = [slice(i * CONT, (i + 1) * CONT) for i in every]
+        key_parts, value_parts = [], []
+        for h in range(2 if own else 0):
+            sel = (lane // 64) == h
+            k = jnp.where(sel, ko_ref[...], none)
+            v = jnp.where(sel, vo_ref[...], none)
+            scores, weights = [], []
+            for i, cut in enumerate(cuts):
                 fine = (row_k <= lane_k) & (row_k < info[2 + i])
-                s = jnp.where(fine, dot(k, q_ref[cut, :], NT), NEG)
-                weight = jnp.exp2(s * SCALE2 - lse_ref[0, h : h + 1, cut])
-                grad = dot(v, do_ref[cut, :], NT)
-                score = (weight * (grad - deltas[h][:, cut])).astype(bf16)
-                value_parts.append(dot(weight.astype(bf16), do_ref[cut, :]))
-                key_parts.append(dot(score, q_ref[cut, :]))
-                part = dot(score, k, TN)
-                query_part = part if query_part is None else query_part + part
-            dq_acc[cut, :] += query_part
-            key_grad = jnp.where(lane_k < 64, key_parts[0], key_parts[1]) * SCALE
-            value_grad = jnp.where(lane_k < 64, value_parts[0], value_parts[1])
+                scores.append(jnp.where(fine, dot(k[cut], q_ref[cut, :], NT), NEG) * SCALE2 - lse_ref[0, h : h + 1, cut])
+            weight = jnp.exp2(jnp.concatenate(scores, 0))
+            grad = jnp.concatenate([dot(v[cut], do_ref[cut, :], NT) - deltas[h][:, cut] for cut in cuts], 0)
+            score = (weight * grad).astype(bf16)
+            weight = weight.astype(bf16)
+            value_parts.append([dot(weight[cut], do_ref[cut, :]) for cut in cuts])
+            key_parts.append([dot(score[cut], q_ref[cut, :]) for cut in cuts])
+            for cut in cuts:
+                dq_acc[cut, :] += dot(score[cut], k[cut], TN)
+        for i, cut in enumerate(cuts):
+            key_grad = jnp.where(lane_k < 64, key_parts[0][i], key_parts[1][i]) * SCALE
+            value_grad = jnp.where(lane_k < 64, value_parts[0][i], value_parts[1][i])
             dko_ref[cut, :] = turn_back(key_grad, co_ref[cut, :], so_ref[cut, :]).astype(bf16)
             dvo_ref[cut, :] = value_grad.astype(bf16)
 
@@ -799,7 +799,7 @@
             scratch_shapes=[pltpu.VMEM((count, 128), f32)],
         ),
         out_shape=outs,
-        compiler_params=pltpu.CompilerParams(vmem_limit_bytes=48 * 2**20),
+        compiler_params=pltpu.CompilerParams(vmem_limit_bytes=20 * 2**20),
         cost_estimate=LONG,
         name="attend_back",
     )(info, *args)
@@ -1075,18 +1075,17 @@
     q_came, q_keep = swap(pick(q_cur, 1 - near, 1), NEAR), pick(q_cur, near, 1)
     sum_a, d_keep, u_keep, o_keep, q_keep, dq_0 = tie(sum_a, d_keep, u_keep, o_keep, q_keep, dq_0)
 
-    dq_0, dkp_b, dvp_b, dk_0, dv_0 = back(0, grad_0, (2, 3), True, dq_0, True)
+    dq_0, dkp_b, dvp_b = back(0, grad_0, (2, 3), False, dq_0, False)
     came, keep, grads = tie(
         (came_a, d_came, u_came, o_came, q_came),
         (d_keep, u_keep, o_keep, q_keep),
-        (dkp_b, dvp_b, dk_0, dv_0, dq_0),
+        (dkp_b, dvp_b, dq_0),
     )
     came_a, d_came, u_came, o_came, q_came = came
     d_keep, u_keep, o_keep, q_keep = keep
-    dkp_b, dvp_b, dk_0, dv_0, dq_0 = grads
+    dkp_b, dvp_b, dq_0 = grads
     sum_b = prompt_sum[half:] + prompt_part(0, dkp_b, dvp_b)
     came_b = swap(sum_b.astype(bf16), TENSOR)
-    sum_b, dq_0, dk_0, dv_0 = tie(sum_b, dq_0, dk_0, dv_0)
 
     def far_end(keep, came):
         for bit in low_bits[1:]:
@@ -1098,17 +1097,24 @@
     u_keep, u_came = far_end(u_keep, u_came)
     o_keep, o_send = send_far(plus(o_keep, o_came))
     o_came = swap(o_send, 8)
-    q_other = swap(plus(q_keep, q_came), TENSOR)
+    q_send = plus(q_keep, q_came)
+    q_send, sum_b, dq_0 = tie(q_send, sum_b, dq_0)
+    dq_0, dk_0, dv_0 = back(0, grad_0, (), True, dq_0, True)
+    came, keep, grads = tie(
+        (d_came, u_came, o_came), (d_keep, u_keep, o_keep), (dq_0, dk_0, dv_0, q_send)
+    )
+    d_came, u_came, o_came = came
+    d_keep, u_keep, o_keep = keep
+    dq_0, dk_0, dv_0, q_send = grads
     dkp_0, dvp_0 = jnp.concatenate([dkp_a, dkp_b], 0), jnp.concatenate([dvp_a, dvp_b], 0)
     q_cur = weight_part(dq_0, dk_0, dv_0, dkp_0, dvp_0)
     q_came, q_keep = swap(pick(q_cur, 1 - core, 2), CORE), pick(q_cur, core, 2)
     own_sum = own_sum + own_part(0, dq_0, dk_0, dv_0)
-    q_came, q_keep, own_sum = tie(q_came, q_keep, own_sum)
+    q_came, q_keep, own_sum, q_send = tie(q_came, q_keep, own_sum, q_send)
     q_cur = plus(q_keep, q_came)
     q_came, q_keep = swap(pick(q_cur, 1 - near, 1), NEAR), pick(q_cur, near, 1)
-    d_came, u_came, o_came, q_other, own_sum, o_keep, d_keep, u_keep, came_b = tie(
-        d_came, u_came, o_came, q_other, own_sum, o_keep, d_keep, u_keep, came_b
-    )
+    q_keep, own_sum, came_b, q_send = tie(q_keep, own_sum, came_b, q_send)
+    q_other = swap(q_send, TENSOR)
     input_grad, last_sums = last(
         info,
         block_input,
@@ -1118,20 +1124,11 @@
         middle_grad,
         mods,
     )
-    q_came, q_keep, last_sums, d_keep, u_keep = tie(q_came, q_keep, last_sums, d_keep, u_keep)
+    last_sums, d_keep, u_keep = tie(last_sums, d_keep, u_keep)
     down_grad = (d_keep.astype(f32) + d_came.astype(f32))[0]
     up_grad = (u_keep.astype(f32) + u_came.astype(f32))[0]
     o_keep, o_came = far_end(o_keep, o_came)
     out_grad = (o_keep.astype(f32) + o_came.astype(f32))[0]
-    q_cur = q_keep.astype(f32) + q_came.astype(f32) + q_other.astype(f32)
-    q_cur = q_cur.reshape((2,) * len(low_bits) + q_cur.shape[1:])
-    for bit in low_bits:
-        axis = q_cur.ndim - 3
-        mine = (far // bit) % 2
-        q_cur = q_cur.astype(bf16)
-        came = swap(pick(q_cur, 1 - mine, axis), 8 * bit)
-        q_cur = pick(q_cur, mine, axis).astype(f32) + came.astype(f32)
-
     order = [last_sums[:, 0], last_sums[:, 1]] + [post_sums[:, n] for n in range(4)]
     sums = jnp.stack(order, 1).reshape(tiles, 6 * width)
     first_row = (jnp.arange(tiles) == 0)[:, None]
@@ -1152,6 +1149,16 @@
     )
     packet = jnp.pad(packet, ((0, 0), (0, 16 - packet.shape[1]), (0, 0)))
     packets = lax.all_to_all(packet, BOTH, 0, 0, tiled=True)
+    q_keep = after(q_keep, packet)
+    q_cur = q_keep.astype(f32) + q_came.astype(f32) + q_other.astype(f32)
+    q_cur = q_cur.reshape((2,) * len(low_bits) + q_cur.shape[1:])
+
+    def q_step(cur, bit):
+        mine = (far // bit) % 2
+        cur = cur.astype(bf16)
+        return pick(cur, mine, cur.ndim - 3), swap(pick(cur, 1 - mine, cur.ndim - 3), 8 * bit)
+
+    q_keep, q_came = q_step(q_cur, low_bits[0])
     totals = jnp.sum(packets[:, tiles, :12].astype(f32), 0)
     totals = totals[:4] + totals[4:8] + totals[8:12]
     stats = jnp.sqrt(totals[:3] / totals[3])
@@ -1175,6 +1182,11 @@
         table_part.astype(bf16).reshape(devices, table_rows, width), BOTH, 0, 0, tiled=True
     )
     table_grad = jnp.sum(table_pieces.astype(f32), 0)
+    q_keep = after(q_keep, table_part)
+    q_cur = q_keep.astype(f32) + q_came.astype(f32)
+    for bit in low_bits[1:]:
+        q_keep, q_came = q_step(q_cur, bit)
+        q_cur = q_keep.astype(f32) + q_came.astype(f32)
     return (
         block_output,
         input_grad,

time: 460 us -> 440 us (0.957)
  starting transfers between devices: 87 us -> 78 us
  Pallas kernels: 181 us -> 173 us
    all_to_all x1, waiting for transfers between devices: 0.01 us -> 9.17 us  [body(): packets = lax.all_to_all(packet, BOTH, 0, 0, tiled=True)]
    all_to_all x1, waiting for transfers between devices: 9.11 us -> 0.01 us  [body(): lax.all_to_all(table_part.astype(bf16).reshape(devices, table_rows, width...]
    ppermute x58, starting transfers between devices: 75.6 us -> 67.4 us  [swap(): return lax.ppermute(x, BOTH, [(i, i ^ bits) for i in range(count)])]
    pallas_call x2, Pallas kernels: 59.5 us -> 51.5 us  [feed_forward(): pl.pallas_call(lambda *refs: mlp_kernel(first, *refs), grid_spec=pltpu.Pr...]
    unnamed x199 -> x194, local copies, waits for them, and re-layouts: 23.2 us -> 29.3 us
    pallas_call x3 -> x4, Pallas kernels: 38.5 us -> 38.5 us  [attend_back(): pl.pallas_call(lambda *refs: backward_kernel(first, last, tiles, own, *re...]
  transfers between devices with their start and end apart: 61 -> 61, of which waited for: 24 -> 26; matrix products, arithmetic and copies ran while one was open for 12% -> 13% of each run, Pallas kernels for 36% -> 35%
where the time goes in v3:
time: 440 us; the launch traced here: 436 us
  Pallas kernels  173 us (39%)
  waiting for transfers between devices  88.5 us (20%)
  starting transfers between devices  78 us (18%)
  local copies, waits for them, and re-layouts  46.8 us (11%)
  matrix products  27 us (6%)
  other arithmetic  18.6 us (4%)
    ppermute x58, waiting for transfers between devices, swap(): return lax.ppermute(x, BOTH, [(i, i ^ bits) for i in range(count)])  73 us
    ppermute x58, starting transfers between devices, swap(): return lax.ppermute(x, BOTH, [(i, i ^ bits) for i in range(count)])  67.4 us
    pallas_call x2, Pallas kernels, feed_forward(): pl.pallas_call(lambda *refs: mlp_kernel(first, *refs), grid_spec=pltpu.Pr...  51.5 us
    pallas_call x4, Pallas kernels, attend_back(): pl.pallas_call(lambda *refs: backward_kernel(first, last, tiles, own, *re...  38.5 us
    unnamed x194, local copies, waits for them, and re-layouts  29.3 us
    dot_general x26, matrix products, dot(): return lax.dot_general(left, right, dims, preferred_element_type=f32)  25.6 us
    pallas_call x2, Pallas kernels, attend(): pl.pallas_call(forward_kernel, grid_spec=pltpu.PrefetchScalarGridSpec(num...  24.3 us
    pallas_call x2, Pallas kernels, project(): pl.pallas_call(kernel, grid_spec=pltpu.PrefetchScalarGridSpec(num_scalar_...  19.9 us
  transfers between devices with their start and end apart: 61, of which 26 were waited for; matrix products, arithmetic and copies ran while one was open for 13% of the time, Pallas kernels for 35%

profile of v3, /device:TPU:0, one launch (start us, length us, event | category | flops | bytes accessed | tf_op | source)
XLA Modules:
  0.0 435.9 jit_solution(3552623080557479809)
XLA Ops:
  3.1 4.1 collective-permute-start
  16.7 5.4 %multiply_sine_fusion = (f32[1024,128]{1,0:T(8,128)}, f32[1024,128]{1,0:T(8,128)}, f32[1024,128]{1,0:T(8,128)}, f32[1024,128]{1,0:T(8,128)}) fusion(f32[1024]{0:T(1024)S(1)} %get-tuple-element.570, f32[128]{0:T(128)S(1)} %fusion.75, f32[1024]{0:T(1024)S(1)} %get-tuple-element.569), kind=kLoop, calls=%fused_computation.53 | loop fusion | flops 262144 | bytes 2105856 | tf_op jit(solution)/shard_map/sin | solution.py:893
  39.5 4.3 all-to-all-start
  44.6 9.5 %collective-permute-done.5.refs_2_ = bf16[1,48,3456]{2,1,0:T(8,128)(2,1)S(1)} collective-permute-done((bf16[1,48,3456]{2,1,0:T(8,128)(2,1)S(1)}, bf16[1,48,3456]{2,1,0:T(8,128)(2,1)S(1)}, u32[]{:S(2)}, u32[]{:S(2)}) %collective-permute-start.5) | collective-permute-done | bytes 331808 | tf_op jit(solution)/shard_map/ppermute | solution.py:46
  54.8 6.3 %all-to-all-done = f32[32,16,144]{2,1,0:T(8,128)} async-done(((f32[32,16,144]{2,1,0:T(8,128)}), f32[32,16,144]{2,1,0:T(8,128)}, u32[]{:S(2)}, u32[]{:S(2)}) %all-to-all-start) | async-done | bytes 294944 | tf_op jit(solution)/shard_map/all_to_all | solution.py:918
  61.1 5.0 %collective-permute-done.12.refs_2_ = bf16[4,48,1152]{2,1,0:T(8,128)(2,1)S(1)} collective-permute-done((bf16[4,48,1152]{2,1,0:T(8,128)(2,1)S(1)}, bf16[4,48,1152]{2,1,0:T(8,128)(2,1)S(1)}, u32[]{:S(2)}, u32[]{:S(2)}) %collective-permute-start.12) | collective-permute-done | bytes 442400 | tf_op jit(solution)/shard_map/ppermute | solution.py:46
  68.0 4.2 collective-permute-start.11
  82.8 4.6 %collective-permute-done.11.refs_2_ = bf16[2,48,3456]{2,1,0:T(8,128)(2,1)S(1)} collective-permute-done((bf16[2,48,3456]{2,1,0:T(8,128)(2,1)S(1)}, bf16[2,48,3456]{2,1,0:T(8,128)(2,1)S(1)}, u32[]{:S(2)}, u32[]{:S(2)}) %collective-permute-start.11) | collective-permute-done | bytes 663584 | tf_op jit(solution)/shard_map/ppermute | solution.py:46
  92.4 11.2 %project.2 = (bf16[2,1024,1152]{2,1,0:T(8,128)(2,1)S(1)}, bf16[1024,768]{1,0:T(8,128)(2,1)S(1)}) custom-call(s32[13]{0:T(128)S(1)} %concatenate.58.info.refs_0_, bf16[1024,768]{1,0:T(8,128)(2,1)S(1)} %copy-done.5, f32[16,4608]{1,0:T(8,128)S(1)} %copy-done.28, bf16[768,1152]{1,0:T(8,128)(2,1)S(1)} %bitcast.236, bf16[768,1152]{1,0:T(8,128)(2,1)S(1)} %bitcast.245, ...), custom_call_target="tpu_custom_call" | custom-call | flops 99999997952 | bytes 1 | tf_op jit(solution)/shard_map/project/pallas_call | solution.py:220
  107.3 8.7 %project.3 = (bf16[2,1024,768]{2,1,0:T(8,128)(2,1)S(1)}, bf16[1024,768]{1,0:T(8,128)(2,1)S(1)}) custom-call(s32[13]{0:T(128)S(1)} %concatenate.58.info.refs_0_, bf16[1024,768]{1,0:T(8,128)(2,1)S(1)} %copy-done.5, bf16[256,768]{1,0:T(8,128)(2,1)S(1)} %copy-done.37, bf16[384,768]{1,0:T(8,128)(2,1)} %collective-permute-done.15.refs_1_, ...), custom_call_target="tpu_custom_call" | custom-call | flops 99999997952 | bytes 1 | tf_op jit(solution)/shard_map/project/pallas_call | solution.py:220
  120.5 12.0 %attend.2 = (bf16[1024,384]{1,0:T(8,128)(2,1)S(1)}, f32[3,2,1024]{2,1,0:T(2,128)S(1)}) custom-call(s32[13]{0:T(128)S(1)} %concatenate.58.info.refs_0_, bf16[2,1024,1152]{2,1,0:T(8,128)(2,1)S(1)} %get-tuple-element.315.refs_0_.refs_3_.refs_4_.refs_1_.refs_9_.refs_10_.refs_5_.refs_6_, ...), custom_call_target="tpu_custom_call" | custom-call | flops 99999997952 | bytes 1 | tf_op jit(solution)/shard_map/attend/pallas_call | solution.py:621
  139.4 12.3 %attend.3 = (bf16[1024,384]{1,0:T(8,128)(2,1)S(1)}, f32[3,2,1024]{2,1,0:T(2,128)S(1)}) custom-call(s32[13]{0:T(128)S(1)} %concatenate.58.info.refs_0_, bf16[2,1024,1152]{2,1,0:T(8,128)(2,1)S(1)} %get-tuple-element.315.refs_0_.refs_3_.refs_4_.refs_1_.refs_9_.refs_10_.refs_5_.refs_6_, ...), custom_call_target="tpu_custom_call" | custom-call | flops 99999997952 | bytes 1 | tf_op jit(solution)/shard_map/attend/pallas_call | solution.py:621
  164.6 25.5 %feed_forward.2 = (f32[1024,768]{1,0:T(8,128)S(1)}, f32[1024,768]{1,0:T(8,128)}, bf16[8,48,1536]{2,1,0:T(8,128)(2,1)S(1)}, bf16[8,48,1536]{2,1,0:T(8,128)(2,1)S(...) custom-call(s32[13]{0:T(128)S(1)} %concatenate.58.info.refs_0_, ...), custom_call_target="tpu_custom_call" | custom-call | flops 99999997952 | bytes 1 | tf_op jit(solution)/shard_map/feed_forward/pallas_call | solution.py:361
  208.2 26.0 %feed_forward.3 = (f32[1024,768]{1,0:T(8,128)S(1)}, f32[1024,768]{1,0:T(8,128)S(1)}, bf16[8,48,1536]{2,1,0:T(8,128)(2,1)S(1)}, bf16[8,48,1536]{2,1,0:T(8,128)(2,...) custom-call(s32[13]{0:T(128)S(1)} %concatenate.58.info.refs_0_, ...), custom_call_target="tpu_custom_call" | custom-call | flops 99999997952 | bytes 1 | tf_op jit(solution)/shard_map/feed_forward/pallas_call | solution.py:361
  246.8 11.1 %post.1 = (bf16[1024,768]{1,0:T(8,128)(2,1)}, f32[1024,768]{1,0:T(8,128)S(1)}, bf16[1024,384]{1,0:T(8,128)(2,1)S(1)}, bf16[1024,384]{1,0:T(8,128)(2,1)S(1)}, f32...) custom-call(s32[13]{0:T(128)S(1)} %concatenate.58.info.refs_0_, ...), custom_call_target="tpu_custom_call" | custom-call | flops 99999997952 | bytes 1 | tf_op jit(solution)/shard_map/post/pallas_call | solution.py:449
  267.5 16.5 %attend_back.4 = (bf16[1024,384]{1,0:T(8,128)(2,1)S(1)}, bf16[1024,384]{1,0:T(8,128)(2,1)S(1)}, bf16[1024,384]{1,0:T(8,128)(2,1)S(1)}, bf16[1024,384]{1,0:T(8,128)(2,1)S(1)}, bf16[1024,384]{1,0:T(8,128)(2,1)S(1)}) custom-call(s32[13]{0:T(128)S(1)} %concatenate.58.info.refs_0_, bf16[2,1024,1152]{2,1,0:T(8,128)(2,1)S(1)} %copy-done.45, ...), custom_call_target="tpu_custom_call" | custom-call | flops 99999997952 | bytes 1 | tf_op jit(solution)/shard_map/attend_back/pallas_call | solution.py:792
  284.0 8.2 %collective-permute-done.36 = bf16[2,4,48,1536]{3,2,1,0:T(8,128)(2,1)S(1)} collective-permute-done((bf16[2,4,48,1536]{3,2,1,0:T(8,128)(2,1)S(1)}, bf16[2,4,48,1536]{3,2,1,0:T(8,128)(2,1)S(1)}, u32[]{:S(2)}, u32[]{:S(2)}) %collective-permute-start.36) | collective-permute-done | bytes 1179680 | tf_op jit(solution)/shard_map/ppermute | solution.py:46
  311.3 10.9 %attend_back.5 = (f32[1024,384]{1,0:T(8,128)S(1)}, bf16[512,384]{1,0:T(8,128)(2,1)S(1)}, bf16[512,384]{1,0:T(8,128)(2,1)S(1)}) custom-call(s32[13]{0:T(128)S(1)} %concatenate.58.info.refs_0_, bf16[2,1024,1152]{2,1,0:T(8,128)(2,1)S(1)} %copy-done.45, bf16[1024,384]{1,0:T(8,128)(2,1)S(1)} %get-tuple-element.408.refs_2_, bf16[1024,384]{1,0:T(8,128)(2,1)S(1)} %copy-done.69, ...), custom_call_target="tpu_custom_call" | custom-call | flops 99999997952 | bytes 1 | tf_op jit(solution)/shard_map/attend_back/pallas_call | solution.py:792
  330.4 7.0 %attend_back.6 = (f32[1024,384]{1,0:T(8,128)S(1)}, bf16[512,384]{1,0:T(8,128)(2,1)S(1)}, bf16[512,384]{1,0:T(8,128)(2,1)S(1)}) custom-call(s32[13]{0:T(128)S(1)} %concatenate.58.info.refs_0_, bf16[2,1024,1152]{2,1,0:T(8,128)(2,1)S(1)} %copy-done.45, bf16[1024,384]{1,0:T(8,128)(2,1)S(1)} %get-tuple-element.408.refs_2_, bf16[1024,384]{1,0:T(8,128)(2,1)S(1)} %copy-done.69, ...), custom_call_target="tpu_custom_call" | custom-call | flops 99999997952 | bytes 1 | tf_op jit(solution)/shard_map/attend_back/pallas_call | solution.py:792
  338.5 9.3 %collective-permute-done.43 = bf16[512,768]{1,0:T(8,128)(2,1)S(1)} collective-permute-done((bf16[512,768]{1,0:T(8,128)(2,1)S(1)}, bf16[512,768]{1,0:T(8,128)(2,1)S(1)}, u32[]{:S(2)}, u32[]{:S(2)}) %collective-permute-start.43) | collective-permute-done | bytes 786464 | tf_op jit(solution)/shard_map/ppermute | solution.py:46
  362.5 5.5 %collective-permute-start.52 = (bf16[512,768]{1,0:T(8,128)(2,1)S(1)}, bf16[512,768]{1,0:T(8,128)(2,1)S(1)}, u32[]{:S(2)}, u32[]{:S(2)}) collective-permute-start(bf16[512,768]{1,0:T(8,128)(2,1)S(1)} %get-tuple-element.567), channel_id=1, source_target_pairs={{0,1},{1,0},{2,3},{3,2},{4,5},{5,4},{6,7},{7,6},{8,9},{9,8},{10,11... | collective-permute-start | bytes 2359304 | tf_op jit(solution)/shard_map/ppermute | solution.py:46
  384.4 4.5 %last.1 = (f32[1024,768]{1,0:T(8,128)}, f32[8,8,768]{2,1,0:T(8,128)S(1)}) custom-call(s32[13]{0:T(128)S(1)} %concatenate.58.info.refs_0_, bf16[1024,768]{1,0:T(8,128)(2,1)S(1)} %copy-done.7, f32[1024,768]{1,0:T(8,128)S(1)} %add_add_fusion.own_ref, f32[1024,768]{1,0:T(8,128)S(1)} %pad_maximum_fusion.prompt_ref, ...), custom_call_target="tpu_custom_call" | custom-call | flops 99999997952 | bytes 1 | tf_op jit(solution)/shard_map/last/pallas_call | solution.py:512
  398.3 9.2 %all-to-all-done.1 = bf16[32,16,144]{2,1,0:T(8,128)(2,1)S(1)} async-done(((bf16[32,16,144]{2,1,0:T(8,128)(2,1)}), bf16[32,16,144]{2,1,0:T(8,128)(2,1)S(1)}, u32[]{:S(2)}, u32[]{:S(2)}) %all-to-all-start.1) | async-done | bytes 147488 | tf_op jit(solution)/shard_map/all_to_all | solution.py:1151
  415.6 10.8 %collective-permute-done.55 = bf16[2,48,1152]{2,1,0:T(8,128)(2,1)S(1)} collective-permute-done((bf16[2,48,1152]{2,1,0:T(8,128)(2,1)S(1)}, bf16[2,48,1152]{2,1,0:T(8,128)(2,1)S(1)}, u32[]{:S(2)}, u32[]{:S(2)}) %collective-permute-start.55) | collective-permute-done | bytes 221216 | tf_op jit(solution)/shard_map/ppermute | solution.py:46
  (451 shorter events, 199.8 us)
Async XLA Ops:
  29.1 25.7 %collective-permute-start.4 = (bf16[4,48,1152]{2,1,0:T(8,128)(2,1)S(1)}, bf16[4,48,1152]{2,1,0:T(8,128)(2,1)S(1)}, u32[]{:S(2)}, u32[]{:S(2)}) collective-permute-start(bf16[4,48,1152]{2,1,0:T(8,128)(2,1)S(1)} %bitcast.288), channel_id=1, source_target_pairs={{0,1},{1,0},{2,3},{3,2},{4,5},{5,4},{6,7},{7,6},{8,9},{9,8},{10,11... | collective-permute-start | bytes 1327112 | tf_op jit(solution)/shard_map/ppermute | solution.py:46
  30.7 24.1 %collective-permute-start.3 = (bf16[4,48,1152]{2,1,0:T(8,128)(2,1)S(1)}, bf16[4,48,1152]{2,1,0:T(8,128)(2,1)S(1)}, u32[]{:S(2)}, u32[]{:S(2)}) collective-permute-start(bf16[4,48,1152]{2,1,0:T(8,128)(2,1)S(1)} %bitcast.289), channel_id=1, source_target_pairs={{0,4},{1,5},{2,6},{3,7},{4,0},{5,1},{6,2},{7,3},{8,12},{9,13},{10,... | collective-permute-start | bytes 1327112 | tf_op jit(solution)/shard_map/ppermute | solution.py:46
  31.8 22.2 %collective-permute-start.5 = (bf16[1,48,3456]{2,1,0:T(8,128)(2,1)S(1)}, bf16[1,48,3456]{2,1,0:T(8,128)(2,1)S(1)}, u32[]{:S(2)}, u32[]{:S(2)}) collective-permute-start(bf16[1,48,3456]{2,1,0:T(8,128)(2,1)S(1)} %maximum_bitcast_fusion.refs_1_), channel_id=1, source_target_pairs={{0,16},{1,17},{2,18},{3,19},{4,20},{5,21},{6,22},{7,23},{8,24},{9,... | collective-permute-start | bytes 995336 | tf_op jit(solution)/shard_map/ppermute | solution.py:46
  39.5 21.6 %all-to-all-start = ((f32[32,16,144]{2,1,0:T(8,128)}), f32[32,16,144]{2,1,0:T(8,128)}, u32[]{:S(2)}, u32[]{:S(2)}) async-start(f32[32,16,144]{2,1,0:T(8,128)} %bitcast.303), calls=%async_computation | async-start | bytes 1048576 | tf_op jit(solution)/shard_map/all_to_all | solution.py:918
  68.0 19.4 %collective-permute-start.11 = (bf16[2,48,3456]{2,1,0:T(8,128)(2,1)S(1)}, bf16[2,48,3456]{2,1,0:T(8,128)(2,1)S(1)}, u32[]{:S(2)}, u32[]{:S(2)}) collective-permute-start(bf16[2,48,3456]{2,1,0:T(8,128)(2,1)S(1)} %bitcast.262), channel_id=1, source_target_pairs={{0,8},{1,9},{2,10},{3,11},{4,12},{5,13},{6,14},{7,15},{8,0},{9,1},... | collective-permute-start | bytes 1990664 | tf_op jit(solution)/shard_map/ppermute | solution.py:46
  88.3 27.7 %collective-permute-start.19 = (bf16[4,48,384]{2,1,0:T(8,128)(2,1)}, bf16[4,48,384]{2,1,0:T(8,128)(2,1)}, u32[]{:S(2)}, u32[]{:S(2)}) collective-permute-start(bf16[4,48,384]{2,1,0:T(8,128)(2,1)} %bitcast.30.refs_1_), channel_id=1, source_target_pairs={{0,1},{1,0},{2,3},{3,2},{4,5},{5,4},{6,7},{7,6},{8,9},{9,8},{10,11... | collective-permute-start | bytes 442376 | tf_op jit(solution)/shard_map/ppermute | solution.py:46
  89.5 26.6 %collective-permute-start.18 = (bf16[4,48,384]{2,1,0:T(8,128)(2,1)}, bf16[4,48,384]{2,1,0:T(8,128)(2,1)}, u32[]{:S(2)}, u32[]{:S(2)}) collective-permute-start(bf16[4,48,384]{2,1,0:T(8,128)(2,1)} %bitcast.30.refs_1_), channel_id=1, source_target_pairs={{0,4},{1,5},{2,6},{3,7},{4,0},{5,1},{6,2},{7,3},{8,12},{9,13},{10,... | collective-permute-start | bytes 442376 | tf_op jit(solution)/shard_map/ppermute | solution.py:46
  117.0 17.9 %collective-permute-start.21 = (bf16[4,48,1536]{2,1,0:T(8,128)(2,1)S(1)}, bf16[4,48,1536]{2,1,0:T(8,128)(2,1)S(1)}, u32[]{:S(2)}, u32[]{:S(2)}) collective-permute-start(bf16[4,48,1536]{2,1,0:T(8,128)(2,1)S(1)} %bitcast.282), channel_id=1, source_target_pairs={{0,1},{1,0},{2,3},{3,2},{4,5},{5,4},{6,7},{7,6},{8,9},{9,8},{10,11... | collective-permute-start | bytes 1769480 | tf_op jit(solution)/shard_map/ppermute | solution.py:46
  153.3 43.0 %collective-permute-start.29 = (bf16[4,48,1536]{2,1,0:T(8,128)(2,1)}, bf16[4,48,1536]{2,1,0:T(8,128)(2,1)}, u32[]{:S(2)}, u32[]{:S(2)}) collective-permute-start(bf16[4,48,1536]{2,1,0:T(8,128)(2,1)} %collective-permute-done.24.refs_1_), channel_id=1, source_target_pairs={{0,4},{1,5},{2,6},{3,7},{4,0},{5,1},{6,2},{7,3},{8,12},{9,13},{10,... | collective-permute-start | bytes 1769480 | tf_op jit(solution)/shard_map/ppermute | solution.py:46
  155.3 41.0 %collective-permute-start.30 = (bf16[8,48,1536]{2,1,0:T(8,128)(2,1)}, bf16[8,48,1536]{2,1,0:T(8,128)(2,1)}, u32[]{:S(2)}, u32[]{:S(2)}) collective-permute-start(bf16[8,48,1536]{2,1,0:T(8,128)(2,1)} %bitcast.39.refs_1_), channel_id=1, source_target_pairs={{0,2},{1,3},{2,0},{3,1},{4,6},{5,7},{6,4},{7,5},{8,10},{9,11},{10,... | collective-permute-start | bytes 3538952 | tf_op jit(solution)/shard_map/ppermute | solution.py:46
  207.5 29.9 %collective-permute-start.32 = (bf16[8,48,1536]{2,1,0:T(8,128)(2,1)S(1)}, bf16[8,48,1536]{2,1,0:T(8,128)(2,1)S(1)}, u32[]{:S(2)}, u32[]{:S(2)}) collective-permute-start(bf16[8,48,1536]{2,1,0:T(8,128)(2,1)S(1)} %copy-done.35), channel_id=1, source_target_pairs={{0,2},{1,3},{2,0},{3,1},{4,6},{5,7},{6,4},{7,5},{8,10},{9,11},{10,... | collective-permute-start | bytes 3538952 | tf_op jit(solution)/shard_map/ppermute | solution.py:46
  207.7 29.8 %collective-permute-start.33 = (bf16[8,48,1536]{2,1,0:T(8,128)(2,1)S(1)}, bf16[8,48,1536]{2,1,0:T(8,128)(2,1)S(1)}, u32[]{:S(2)}, u32[]{:S(2)}) collective-permute-start(bf16[8,48,1536]{2,1,0:T(8,128)(2,1)S(1)} %copy-done.33), channel_id=1, source_target_pairs={{0,2},{1,3},{2,0},{3,1},{4,6},{5,7},{6,4},{7,5},{8,10},{9,11},{10,... | collective-permute-start | bytes 3538952 | tf_op jit(solution)/shard_map/ppermute | solution.py:46
  263.7 20.4 %collective-permute-start.38 = (bf16[2,8,48,384]{3,2,1,0:T(8,128)(2,1)S(1)}, bf16[2,8,48,384]{3,2,1,0:T(8,128)(2,1)S(1)}, u32[]{:S(2)}, u32[]{:S(2)}) collective-permute-start(bf16[2,8,48,384]{3,2,1,0:T(8,128)(2,1)S(1)} %get-tuple-element.373), channel_id=1, source_target_pairs={{0,2},{1,3},{2,0},{3,1},{4,6},{5,7},{6,4},{7,5},{8,10},{9,11},{10,... | collective-permute-start | bytes 1769480 | tf_op jit(solution)/shard_map/ppermute | solution.py:46
  264.0 28.3 %collective-permute-start.36 = (bf16[2,4,48,1536]{3,2,1,0:T(8,128)(2,1)S(1)}, bf16[2,4,48,1536]{3,2,1,0:T(8,128)(2,1)S(1)}, u32[]{:S(2)}, u32[]{:S(2)}) collective-permute-start(bf16[2,4,48,1536]{3,2,1,0:T(8,128)(2,1)S(1)} %pad_maximum_fusion.4), channel_id=1, source_target_pairs={{0,4},{1,5},{2,6},{3,7},{4,0},{5,1},{6,2},{7,3},{8,12},{9,13},{10,... | collective-permute-start | bytes 3538952 | tf_op jit(solution)/shard_map/ppermute | solution.py:46
  265.6 28.0 %collective-permute-start.37 = (bf16[8,48,1536]{2,1,0:T(8,128)(2,1)S(1)}, bf16[8,48,1536]{2,1,0:T(8,128)(2,1)S(1)}, u32[]{:S(2)}, u32[]{:S(2)}) collective-permute-start(bf16[8,48,1536]{2,1,0:T(8,128)(2,1)S(1)} %add_convert_fusion.1), channel_id=1, source_target_pairs={{0,1},{1,0},{2,3},{3,2},{4,5},{5,4},{6,7},{7,6},{8,9},{9,8},{10,11... | collective-permute-start | bytes 3538952 | tf_op jit(solution)/shard_map/ppermute | solution.py:46
  293.9 28.3 %collective-permute-start.42 = (bf16[2,4,48,384]{3,2,1,0:T(8,128)(2,1)S(1)}, bf16[2,4,48,384]{3,2,1,0:T(8,128)(2,1)S(1)}, u32[]{:S(2)}, u32[]{:S(2)}) collective-permute-start(bf16[2,4,48,384]{3,2,1,0:T(8,128)(2,1)S(1)} %get-tuple-element.542), channel_id=1, source_target_pairs={{0,4},{1,5},{2,6},{3,7},{4,0},{5,1},{6,2},{7,3},{8,12},{9,13},{10,... | collective-permute-start | bytes 884744 | tf_op jit(solution)/shard_map/ppermute | solution.py:46
  303.7 18.5 %collective-permute-start.39 = (bf16[4,2,48,1152]{3,2,1,0:T(8,128)(2,1)S(1)}, bf16[4,2,48,1152]{3,2,1,0:T(8,128)(2,1)S(1)}, u32[]{:S(2)}, u32[]{:S(2)}) collective-permute-start(bf16[4,2,48,1152]{3,2,1,0:T(8,128)(2,1)S(1)} %get-tuple-element.528), channel_id=1, source_target_pairs={{0,2},{1,3},{2,0},{3,1},{4,6},{5,7},{6,4},{7,5},{8,10},{9,11},{10,... | collective-permute-start | bytes 2654216 | tf_op jit(solution)/shard_map/ppermute | solution.py:46
  304.1 18.1 %collective-permute-start.40 = (bf16[4,48,1536]{2,1,0:T(8,128)(2,1)S(1)}, bf16[4,48,1536]{2,1,0:T(8,128)(2,1)S(1)}, u32[]{:S(2)}, u32[]{:S(2)}) collective-permute-start(bf16[4,48,1536]{2,1,0:T(8,128)(2,1)S(1)} %get-tuple-element.532), channel_id=1, source_target_pairs={{0,1},{1,0},{2,3},{3,2},{4,5},{5,4},{6,7},{7,6},{8,9},{9,8},{10,11... | collective-permute-start | bytes 1769480 | tf_op jit(solution)/shard_map/ppermute | solution.py:46
  329.5 18.3 %collective-permute-start.43 = (bf16[512,768]{1,0:T(8,128)(2,1)S(1)}, bf16[512,768]{1,0:T(8,128)(2,1)S(1)}, u32[]{:S(2)}, u32[]{:S(2)}) collective-permute-start(bf16[512,768]{1,0:T(8,128)(2,1)S(1)} %get-tuple-element.565), channel_id=1, source_target_pairs={{0,1},{1,0},{2,3},{3,2},{4,5},{5,4},{6,7},{7,6},{8,9},{9,8},{10,11... | collective-permute-start | bytes 2359304 | tf_op jit(solution)/shard_map/ppermute | solution.py:46
  350.3 17.9 %collective-permute-start.50 = (bf16[2,48,384]{2,1,0:T(8,128)(2,1)S(1)}, bf16[2,48,384]{2,1,0:T(8,128)(2,1)S(1)}, u32[]{:S(2)}, u32[]{:S(2)}) collective-permute-start(bf16[2,48,384]{2,1,0:T(8,128)(2,1)S(1)} %get-tuple-element.554), channel_id=1, source_target_pairs={{0,8},{1,9},{2,10},{3,11},{4,12},{5,13},{6,14},{7,15},{8,0},{9,1},... | collective-permute-start | bytes 221192 | tf_op jit(solution)/shard_map/ppermute | solution.py:46
  362.5 20.5 %collective-permute-start.52 = (bf16[512,768]{1,0:T(8,128)(2,1)S(1)}, bf16[512,768]{1,0:T(8,128)(2,1)S(1)}, u32[]{:S(2)}, u32[]{:S(2)}) collective-permute-start(bf16[512,768]{1,0:T(8,128)(2,1)S(1)} %get-tuple-element.567), channel_id=1, source_target_pairs={{0,1},{1,0},{2,3},{3,2},{4,5},{5,4},{6,7},{7,6},{8,9},{9,8},{10,11... | collective-permute-start | bytes 2359304 | tf_op jit(solution)/shard_map/ppermute | solution.py:46
  389.0 23.6 %collective-permute-start.54 = (bf16[4,48,1152]{2,1,0:T(8,128)(2,1)}, bf16[4,48,1152]{2,1,0:T(8,128)(2,1)S(1)}, u32[]{:S(2)}, u32[]{:S(2)}) collective-permute-start(bf16[4,48,1152]{2,1,0:T(8,128)(2,1)} %add_convert_fusion.14), channel_id=1, source_target_pairs={{0,1},{1,0},{2,3},{3,2},{4,5},{5,4},{6,7},{7,6},{8,9},{9,8},{10,11... | collective-permute-start | bytes 1327112 | tf_op jit(solution)/shard_map/ppermute | solution.py:46
  390.8 21.8 %collective-permute-start.53 = (bf16[4,48,1152]{2,1,0:T(8,128)(2,1)}, bf16[4,48,1152]{2,1,0:T(8,128)(2,1)S(1)}, u32[]{:S(2)}, u32[]{:S(2)}) collective-permute-start(bf16[4,48,1152]{2,1,0:T(8,128)(2,1)} %get-tuple-element.533), channel_id=1, source_target_pairs={{0,4},{1,5},{2,6},{3,7},{4,0},{5,1},{6,2},{7,3},{8,12},{9,13},{10,... | collective-permute-start | bytes 1327112 | tf_op jit(solution)/shard_map/ppermute | solution.py:46
  409.9 25.2 %all-to-all-start.2 = ((bf16[32,8,768]{2,1,0:T(8,128)(2,1)}), bf16[32,8,768]{2,1,0:T(8,128)(2,1)S(1)}, u32[]{:S(2)}, u32[]{:S(2)}) async-start(bf16[32,8,768]{2,1,0:T(8,128)(2,1)} %bitcast.195), calls=%async_computation.2 | async-start | bytes 786432 | tf_op jit(solution)/shard_map/all_to_all | solution.py:1181
  (133 other events, 1194.6 us)

commit v4 on v3

--- a/solution.py
+++ b/solution.py
@@ -283,24 +283,25 @@
             jax.ShapeDtypeStruct((count, width), f32),
             jax.ShapeDtypeStruct((count, width), bf16),
         ],
-        compiler_params=pltpu.CompilerParams(vmem_limit_bytes=16 * 2**20),
+        compiler_params=pltpu.CompilerParams(vmem_limit_bytes=32 * 2**20),
         cost_estimate=LONG,
         name="middle_norm",
     )(info, x, *attended, mods, *out_t)
 
 
-def mlp_kernel(first, info, n2_ref, *refs):
+def mlp_kernel(first, whole_weights, info, n2_ref, *refs):
     if first:
         cot_ref, mods_ref = refs[:2]
         refs = refs[2:]
     else:
         n2_turned, out_grad, out_turned, branch_before, grad_before = refs[:5]
         refs = refs[5:]
-    up_ref, down_ref, branch_ref, grad_ref = refs[:4]
-    down_keep_ref, down_send_ref, up_keep_ref, up_send_ref = refs[4:8]
+    weight_refs, refs = refs[:whole_weights], refs[whole_weights:]
+    branch_ref, grad_ref = refs[:2]
+    down_keep_ref, down_send_ref, up_keep_ref, up_send_ref = refs[2:6]
     if first:
-        n2_turned, out_grad, out_turned = refs[8:11]
-    hidden, pre_grad = refs[-2:]
+        n2_turned, out_grad, out_turned = refs[6:9]
+    hidden, pre_grad, *joined = refs[-4:] if whole_weights == 4 else refs[-2:]
     count = n2_ref.shape[0]
 
     @pl.when(pl.program_id(0) == 0)
@@ -318,7 +319,19 @@
             branch_ref[...] = branch_before[...]
             grad_ref[...] = grad_before[...]
 
-    up, down = up_ref[...], down_ref[...]
+    if joined:
+        for n, out_ref in enumerate(joined):
+            own_ref, came_ref = weight_refs[2 * n : 2 * n + 2]
+            rows_each = own_ref.shape[1]
+            for k in range(own_ref.shape[0]):
+                own, came = own_ref[k], came_ref[k]
+                start = 2 * k * rows_each
+                out_ref[start : start + rows_each, :] = jnp.where(info[10] == 0, own, came)
+                start += rows_each
+                out_ref[start : start + rows_each, :] = jnp.where(info[10] == 0, came, own)
+        up, down = joined[0][...], joined[1][...]
+    else:
+        up, down = weight_refs[0][...], weight_refs[1][...]
     tile = 256
     for i in range(count // tile):
         cut = slice(i * tile, (i + 1) * tile)
@@ -335,9 +348,9 @@
     store_pieces(dot(n2_turned[...], pre_grad[...]), info, up_keep_ref, up_send_ref, ())
 
 
-def feed_forward(info, n2, sources, up, down):
+def feed_forward(info, n2, sources, weights):
     count, width = n2.shape
-    hidden_width = up.shape[1]
+    hidden_width = weights[0].shape[-1]
     first = len(sources) == 2
     cols = 384
     dp_count = lax.axis_size("dp")
@@ -349,7 +362,13 @@
         )
 
     piece_spec = pl.BlockSpec(pieces[:2] + (cols,), lambda b, s: (0, 0, b))
-    weight_spec = pl.BlockSpec((width, cols), lambda b, s: (0, b))
+    weight_specs = [
+        pl.BlockSpec(w.shape[:-1] + (cols,), lambda b, s, lead=w.ndim - 1: (0,) * lead + (b,))
+        for w in weights
+    ]
+    scratch = [pltpu.VMEM((count, cols), bf16)] * 2
+    if len(weights) == 4:
+        scratch += [pltpu.VMEM((width, cols), bf16)] * 2
     outs = [jax.ShapeDtypeStruct((count, width), f32)] * 2 + [
         jax.ShapeDtypeStruct(pieces, bf16)
     ] * 4
@@ -359,19 +378,19 @@
         outs += [jax.ShapeDtypeStruct(shape, bf16) for shape in shapes]
         out_specs += [pl.BlockSpec(shape, lambda b, s: (0, 0)) for shape in shapes]
     return pl.pallas_call(
-        lambda *refs: mlp_kernel(first, *refs),
+        lambda *refs: mlp_kernel(first, len(weights), *refs),
         grid_spec=pltpu.PrefetchScalarGridSpec(
             num_scalar_prefetch=1,
             grid=(hidden_width // cols,),
-            in_specs=[whole(n2)] + [whole(array) for array in sources] + [weight_spec] * 2,
+            in_specs=[whole(n2)] + [whole(array) for array in sources] + weight_specs,
             out_specs=out_specs,
-            scratch_shapes=[pltpu.VMEM((count, cols), bf16), pltpu.VMEM((count, cols), bf16)],
+            scratch_shapes=scratch,
         ),
         out_shape=outs,
-        compiler_params=pltpu.CompilerParams(vmem_limit_bytes=32 * 2**20),
+        compiler_params=pltpu.CompilerParams(vmem_limit_bytes=52 * 2**20),
         cost_estimate=LONG,
         name="feed_forward",
-    )(info, n2, *sources, up, down)
+    )(info, n2, *sources, *weights)
 
 
 def post_kernel(
@@ -482,7 +501,7 @@
             jax.ShapeDtypeStruct(pieces, bf16),
             jax.ShapeDtypeStruct(pieces, bf16),
         ],
-        compiler_params=pltpu.CompilerParams(vmem_limit_bytes=32 * 2**20),
+        compiler_params=pltpu.CompilerParams(vmem_limit_bytes=48 * 2**20),
         cost_estimate=LONG,
         name="post",
     )(info, middle, branch, mlp, n2_grad, cotangent, *attended, mods, *out_t)
@@ -925,8 +944,8 @@
         rest_came = swap(rest, 8 * far_rest[0])
 
     qkv_far, qkv_near, arrived, came, x_parts = tie(qkv_far, qkv_near, arrived, came, x_parts)
+    mods = jnp.transpose(arrived, (1, 0, 2)).reshape(16, 6 * width)
     came.append(swap(x_parts[1], TENSOR))
-    mods = jnp.transpose(arrived, (1, 0, 2)).reshape(16, 6 * width).astype(f32)
     qkv_own = join(qkv_far, qkv_near[0], near)
     qkv_other = join(qkv_near[1], qkv_near[2], near)
     qkv_came = [swap(qkv_own, CORE), swap(qkv_other, CORE)]
@@ -939,6 +958,9 @@
     ]
     rest, rest_came, mods, qkv, came, x_parts = tie(rest, rest_came, mods, qkv, came, x_parts)
 
+    def both_cores(own, came):
+        return [own, came] if rows_each % 16 == 0 else [join(own, came, core).reshape(width, -1)]
+
     came.append(swap(x_parts[2], TENSOR))
     o_own, u_own, d_own = join(rest, rest_came, far_bit(1), cuts) if far_rest else rest
     u_near, o_near, o_other = swap(u_own, NEAR), swap(o_own, NEAR), swap(o_own, TENSOR)
@@ -962,7 +984,7 @@
     d_other, uu_near = swap(d_own, TENSOR), swap(u_other, NEAR)
     d_own, o_other = join(d_own, d_near, near), join(o_other, oo_near, near)
     d_core, o_core, oo_core = swap(d_own, CORE), swap(o_own, CORE), swap(o_other, CORE)
-    up_0 = join(u_own, u_core, core).reshape(width, -1)
+    up_0 = both_cores(u_own, u_core)
     out_1, lse_1 = attend(info, *tie(joined, prompts, d_own, o_other, up_0)[:2], 1)
     d_other, uu_near, d_core, o_core, oo_core, d_own, o_own, o_other, u_other, out_1 = tie(
         d_other, uu_near, d_core, o_core, oo_core, d_own, o_own, o_other, u_other, out_1
@@ -977,22 +999,22 @@
     dd_near = swap(d_other, NEAR)
     u_other = join(u_other, uu_near, near)
     uu_core = swap(u_other, CORE)
-    down_0 = join(d_own, d_core, core).reshape(width, -1)
+    down_0 = both_cores(d_own, d_core)
     d_other, u_other, normed_two, down_0 = tie(d_other, u_other, normed_two, down_0)
     mlp, n2_grad, d_keep_0, d_send_0, u_keep_0, u_send_0, *shared = feed_forward(
-        info, normed_two, (cotangent, mods), up_0, down_0
+        info, normed_two, (cotangent, mods), up_0 + down_0
     )
     dd_near, uu_core, d_other, u_other, mlp, d_send_0, u_send_0 = tie(
         dd_near, uu_core, d_other, u_other, mlp, d_send_0, u_send_0
     )
     d_other = join(d_other, dd_near, near)
     dd_core = swap(d_other, CORE)
-    up_1 = join(u_other, uu_core, core).reshape(width, -1)
-    down_1 = join(d_other, dd_core, core).reshape(width, -1)
+    up_1 = both_cores(u_other, uu_core)
+    down_1 = both_cores(d_other, dd_core)
     up_1, down_1, mlp, d_send_0, u_send_0 = tie(up_1, down_1, mlp, d_send_0, u_send_0)
     d_came_0, u_came_0 = swap(d_send_0, CORE), swap(u_send_0, CORE)
     mlp, n2_grad, d_keep_1, d_send_1, u_keep_1, u_send_1 = feed_forward(
-        info, normed_two, (*shared, mlp, n2_grad), up_1, down_1
+        info, normed_two, (*shared, mlp, n2_grad), up_1 + down_1
     )
     d_came_0, u_came_0, mlp, d_send_1, u_send_1 = tie(d_came_0, u_came_0, mlp, d_send_1, u_send_1)
     d_came_1, u_came_1 = swap(d_send_1, CORE), swap(u_send_1, CORE)
@@ -1022,23 +1044,13 @@
             info, joined, prompts, t, grad, attended[t], lses[t], tables, blocks, own, before, last
         )
 
-    wq, wk, wv = (
-        [qkv[t][:, n * head_width : (n + 1) * head_width] for t in range(2)] for n in range(3)
-    )
-
-    def prompt_part(t, dk, dv):
-        return dot(dk, wk[t], NT) + dot(dv, wv[t], NT)
-
-    def own_part(t, dq, dk, dv):
-        return dot(dq, wq[t], NT) + dot(dk, wk[t], NT) + dot(dv, wv[t], NT)
-
-    def weight_part(dq, dk, dv, dk_prompt, dv_prompt):
-        parts = [
-            dot(normed, dq, TN),
-            dot(normed, dk, TN) + dot(prompt_normed, dk_prompt, TN),
-            dot(normed, dv, TN) + dot(prompt_normed, dv_prompt, TN),
-        ]
-        whole = jnp.concatenate(parts, 1).astype(bf16)
+    def prompt_part(t, dkv):
+        return dot(dkv, qkv[t][:, head_width:], NT)
+
+    def weight_part(dqkv, dkv_prompt):
+        whole = dot(normed, dqkv, TN)
+        parts = [whole[:, :head_width], whole[:, head_width:] + dot(prompt_normed, dkv_prompt, TN)]
+        whole = jnp.concatenate([part.astype(bf16) for part in parts], 1)
         return whole.reshape(fars, 2, 2, -1, whole.shape[1])
 
     dq_1, dkp_1, dvp_1, dk_1, dv_1 = back(1, grad_1, (0, 1, 2, 3), True)
@@ -1051,11 +1063,13 @@
     d_came, u_came = swap(d_send, TENSOR), swap(u_send, NEAR)
     o_came = swap(o_cur[:, 1], NEAR)
     o_keep = o_cur[:, 0]
-    q_cur = weight_part(dq_1, dk_1, dv_1, dkp_1, dvp_1)
+    dqkv_1 = jnp.concatenate([dq_1, dk_1, dv_1], 1)
+    dkvp_1 = jnp.concatenate([dkp_1, dvp_1], 1)
+    q_cur = weight_part(dqkv_1, dkvp_1)
     q_came = swap(pick(q_cur, 1 - core, 2), CORE)
     q_keep = pick(q_cur, core, 2)
-    own_sum = own_part(1, dq_1, dk_1, dv_1)
-    prompt_sum = prompt_part(1, dkp_1, dvp_1)
+    own_sum = dot(dqkv_1, qkv[1], NT)
+    prompt_sum = prompt_part(1, dkvp_1)
     q_keep, own_sum, prompt_sum, grad_0, d_keep, u_keep, o_keep = tie(
         q_keep, own_sum, prompt_sum, grad_0, d_keep, u_keep, o_keep
     )
@@ -1064,7 +1078,8 @@
     q_came, d_came, u_came, o_came, q_keep, d_keep, u_keep, o_keep, dq_0, dkp_a, dvp_a = tie(
         q_came, d_came, u_came, o_came, q_keep, d_keep, u_keep, o_keep, dq_0, dkp_a, dvp_a
     )
-    sum_a = prompt_sum[:half] + prompt_part(0, dkp_a, dvp_a)
+    dkvp_a = jnp.concatenate([dkp_a, dvp_a], 1)
+    sum_a = prompt_sum[:half] + prompt_part(0, dkvp_a)
     came_a = swap(sum_a.astype(bf16), TENSOR)
     d_keep, d_send = send_far(plus(d_keep, d_came))
     u_keep, u_send = send_far(plus(u_keep, u_came))
@@ -1084,7 +1099,8 @@
     came_a, d_came, u_came, o_came, q_came = came
     d_keep, u_keep, o_keep, q_keep = keep
     dkp_b, dvp_b, dq_0 = grads
-    sum_b = prompt_sum[half:] + prompt_part(0, dkp_b, dvp_b)
+    dkvp_b = jnp.concatenate([dkp_b, dvp_b], 1)
+    sum_b = prompt_sum[half:] + prompt_part(0, dkvp_b)
     came_b = swap(sum_b.astype(bf16), TENSOR)
 
     def far_end(keep, came):
@@ -1106,10 +1122,10 @@
     d_came, u_came, o_came = came
     d_keep, u_keep, o_keep = keep
     dq_0, dk_0, dv_0, q_send = grads
-    dkp_0, dvp_0 = jnp.concatenate([dkp_a, dkp_b], 0), jnp.concatenate([dvp_a, dvp_b], 0)
-    q_cur = weight_part(dq_0, dk_0, dv_0, dkp_0, dvp_0)
+    dqkv_0 = jnp.concatenate([dq_0, dk_0, dv_0], 1)
+    q_cur = weight_part(dqkv_0, jnp.concatenate([dkvp_a, dkvp_b], 0))
     q_came, q_keep = swap(pick(q_cur, 1 - core, 2), CORE), pick(q_cur, core, 2)
-    own_sum = own_sum + own_part(0, dq_0, dk_0, dv_0)
+    own_sum = own_sum + dot(dqkv_0, qkv[0], NT)
     q_came, q_keep, own_sum, q_send = tie(q_came, q_keep, own_sum, q_send)
     q_cur = plus(q_keep, q_came)
     q_came, q_keep = swap(pick(q_cur, 1 - near, 1), NEAR), pick(q_cur, near, 1)
@@ -1124,7 +1140,18 @@
         middle_grad,
         mods,
     )
-    last_sums, d_keep, u_keep = tie(last_sums, d_keep, u_keep)
+    last_sums, d_keep, u_keep, q_came, q_other, q_keep = tie(
+        last_sums, d_keep, u_keep, q_came, q_other, q_keep
+    )
+    q_cur = q_keep.astype(f32) + q_came.astype(f32) + q_other.astype(f32)
+    q_cur = q_cur.reshape((2,) * len(low_bits) + q_cur.shape[1:])
+
+    def q_step(cur, bit):
+        mine = (far // bit) % 2
+        cur = cur.astype(bf16)
+        return pick(cur, mine, cur.ndim - 3), swap(pick(cur, 1 - mine, cur.ndim - 3), 8 * bit)
+
+    q_keep, q_came = q_step(q_cur, low_bits[0])
     down_grad = (d_keep.astype(f32) + d_came.astype(f32))[0]
     up_grad = (u_keep.astype(f32) + u_came.astype(f32))[0]
     o_keep, o_came = far_end(o_keep, o_came)
@@ -1149,16 +1176,11 @@
     )
     packet = jnp.pad(packet, ((0, 0), (0, 16 - packet.shape[1]), (0, 0)))
     packets = lax.all_to_all(packet, BOTH, 0, 0, tiled=True)
-    q_keep = after(q_keep, packet)
-    q_cur = q_keep.astype(f32) + q_came.astype(f32) + q_other.astype(f32)
-    q_cur = q_cur.reshape((2,) * len(low_bits) + q_cur.shape[1:])
-
-    def q_step(cur, bit):
-        mine = (far // bit) % 2
-        cur = cur.astype(bf16)
-        return pick(cur, mine, cur.ndim - 3), swap(pick(cur, 1 - mine, cur.ndim - 3), 8 * bit)
-
-    q_keep, q_came = q_step(q_cur, low_bits[0])
+    packets, q_keep, q_came = tie(packets, q_keep, q_came)
+    q_cur = q_keep.astype(f32) + q_came.astype(f32)
+    for bit in low_bits[1:]:
+        q_keep, q_came = q_step(q_cur, bit)
+        q_cur = q_keep.astype(f32) + q_came.astype(f32)
     totals = jnp.sum(packets[:, tiles, :12].astype(f32), 0)
     totals = totals[:4] + totals[4:8] + totals[8:12]
     stats = jnp.sqrt(totals[:3] / totals[3])
@@ -1182,11 +1204,6 @@
         table_part.astype(bf16).reshape(devices, table_rows, width), BOTH, 0, 0, tiled=True
     )
     table_grad = jnp.sum(table_pieces.astype(f32), 0)
-    q_keep = after(q_keep, table_part)
-    q_cur = q_keep.astype(f32) + q_came.astype(f32)
-    for bit in low_bits[1:]:
-        q_keep, q_came = q_step(q_cur, bit)
-        q_cur = q_keep.astype(f32) + q_came.astype(f32)
     return (
         block_output,
         input_grad,

time: 440 us -> 425 us (0.966)
  local copies, waits for them, and re-layouts: 46.8 us -> 31.7 us
  matrix products: 27 us -> 21.2 us
    unnamed x194 -> x164, local copies, waits for them, and re-layouts: 29.3 us -> 13.3 us
    ppermute x58, waiting for transfers between devices: 73 us -> 83.9 us  [swap(): return lax.ppermute(x, BOTH, [(i, i ^ bits) for i in range(count)])]
    all_to_all x1, waiting for transfers between devices: 9.17 us -> 0.01 us  [body(): packets = lax.all_to_all(packet, BOTH, 0, 0, tiled=True)]
    pallas_call x2, Pallas kernels: 51.5 us -> 59.1 us  [feed_forward(): pl.pallas_call(lambda *refs: mlp_kernel(first, len(weights), *refs), grid...]
    dot_general x26 -> x13, matrix products: 25.6 us -> 19.8 us  [dot(): return lax.dot_general(left, right, dims, preferred_element_type=f32)]
    pallas_call x24 -> x20, Pallas kernels: 19.5 us -> 14 us  [join(): pl.pallas_call(lambda *refs: join_kernel(sizes, *refs), grid_spec=pltpu.P...]
  transfers between devices with their start and end apart: 61 -> 61, of which waited for: 26 -> 25; matrix products, arithmetic and copies ran while one was open for 13% -> 12% of each run, Pallas kernels for 35% -> 38%
where the time goes in v4:
time: 425 us; the launch traced here: 421 us
  Pallas kernels  177 us (42%)
  waiting for transfers between devices  89.4 us (21%)
  starting transfers between devices  78.5 us (18%)
  local copies, waits for them, and re-layouts  31.7 us (7%)
  matrix products  21.2 us (5%)
  other arithmetic  19.2 us (5%)
    ppermute x58, waiting for transfers between devices, swap(): return lax.ppermute(x, BOTH, [(i, i ^ bits) for i in range(count)])  83.9 us
    ppermute x58, starting transfers between devices, swap(): return lax.ppermute(x, BOTH, [(i, i ^ bits) for i in range(count)])  66 us
    pallas_call x2, Pallas kernels, feed_forward(): pl.pallas_call(lambda *refs: mlp_kernel(first, len(weights), *refs), grid...  59.1 us
    pallas_call x4, Pallas kernels, attend_back(): pl.pallas_call(lambda *refs: backward_kernel(first, last, tiles, own, *re...  38.5 us
    pallas_call x2, Pallas kernels, attend(): pl.pallas_call(forward_kernel, grid_spec=pltpu.PrefetchScalarGridSpec(num...  24.5 us
    pallas_call x2, Pallas kernels, project(): pl.pallas_call(kernel, grid_spec=pltpu.PrefetchScalarGridSpec(num_scalar_...  19.9 us
    dot_general x13, matrix products, dot(): return lax.dot_general(left, right, dims, preferred_element_type=f32)  19.8 us
    pallas_call x20, Pallas kernels, join(): pl.pallas_call(lambda *refs: join_kernel(sizes, *refs), grid_spec=pltpu.P...  14 us
  transfers between devices with their start and end apart: 61, of which 25 were waited for; matrix products, arithmetic and copies ran while one was open for 12% of the time, Pallas kernels for 38%

profile of v4, /device:TPU:0, one launch (start us, length us, event | category | flops | bytes accessed | tf_op | source)
XLA Modules:
  0.0 420.6 jit_solution(1374127205229131426)
XLA Ops:
  3.1 4.1 collective-permute-start
  16.7 5.4 %multiply_sine_fusion = (f32[1024,128]{1,0:T(8,128)}, f32[1024,128]{1,0:T(8,128)}, f32[1024,128]{1,0:T(8,128)}, f32[1024,128]{1,0:T(8,128)}) fusion(f32[1024]{0:T(1024)S(1)} %get-tuple-element.584, f32[128]{0:T(128)S(1)} %fusion.50, f32[1024]{0:T(1024)S(1)} %get-tuple-element.583), kind=kLoop, calls=%fused_computation.49 | loop fusion | flops 262144 | bytes 2105856 | tf_op jit(solution)/shard_map/sin | solution.py:912
  44.2 10.7 %collective-permute-done.5.refs_2_ = bf16[1,48,3456]{2,1,0:T(8,128)(2,1)S(1)} collective-permute-done((bf16[1,48,3456]{2,1,0:T(8,128)(2,1)S(1)}, bf16[1,48,3456]{2,1,0:T(8,128)(2,1)S(1)}, u32[]{:S(2)}, u32[]{:S(2)}) %collective-permute-start.5) | collective-permute-done | bytes 331808 | tf_op jit(solution)/shard_map/ppermute | solution.py:46
  55.6 5.5 %all-to-all-done = f32[32,16,144]{2,1,0:T(8,128)} async-done(((f32[32,16,144]{2,1,0:T(8,128)}), f32[32,16,144]{2,1,0:T(8,128)}, u32[]{:S(2)}, u32[]{:S(2)}) %all-to-all-start) | async-done | bytes 294944 | tf_op jit(solution)/shard_map/all_to_all | solution.py:937
  61.1 5.3 %collective-permute-done.12.refs_2_ = bf16[4,48,1152]{2,1,0:T(8,128)(2,1)S(1)} collective-permute-done((bf16[4,48,1152]{2,1,0:T(8,128)(2,1)S(1)}, bf16[4,48,1152]{2,1,0:T(8,128)(2,1)S(1)}, u32[]{:S(2)}, u32[]{:S(2)}) %collective-permute-start.12) | collective-permute-done | bytes 442400 | tf_op jit(solution)/shard_map/ppermute | solution.py:46
  82.7 4.6 %collective-permute-done.11.refs_2_ = bf16[2,48,3456]{2,1,0:T(8,128)(2,1)S(1)} collective-permute-done((bf16[2,48,3456]{2,1,0:T(8,128)(2,1)S(1)}, bf16[2,48,3456]{2,1,0:T(8,128)(2,1)S(1)}, u32[]{:S(2)}, u32[]{:S(2)}) %collective-permute-start.11) | collective-permute-done | bytes 663584 | tf_op jit(solution)/shard_map/ppermute | solution.py:46
  92.4 11.2 %project.2 = (bf16[2,1024,1152]{2,1,0:T(8,128)(2,1)S(1)}, bf16[1024,768]{1,0:T(8,128)(2,1)S(1)}) custom-call(s32[13]{0:T(128)S(1)} %concatenate.54.info.refs_0_, bf16[1024,768]{1,0:T(8,128)(2,1)S(1)} %copy-done.7, f32[16,4608]{1,0:T(8,128)S(1)} %copy-done.30, bf16[768,1152]{1,0:T(8,128)(2,1)S(1)} %bitcast.212, bf16[768,1152]{1,0:T(8,128)(2,1)S(1)} %bitcast.223, ...), custom_call_target="tpu_custom_call" | custom-call | flops 99999997952 | bytes 1 | tf_op jit(solution)/shard_map/project/pallas_call | solution.py:220
  107.3 8.7 %project.3 = (bf16[2,1024,768]{2,1,0:T(8,128)(2,1)S(1)}, bf16[1024,768]{1,0:T(8,128)(2,1)S(1)}) custom-call(s32[13]{0:T(128)S(1)} %concatenate.54.info.refs_0_, bf16[1024,768]{1,0:T(8,128)(2,1)S(1)} %copy-done.7, bf16[256,768]{1,0:T(8,128)(2,1)S(1)} %copy-done.33, bf16[384,768]{1,0:T(8,128)(2,1)} %collective-permute-done.15.refs_1_, ...), custom_call_target="tpu_custom_call" | custom-call | flops 99999997952 | bytes 1 | tf_op jit(solution)/shard_map/project/pallas_call | solution.py:220
  120.9 12.1 %attend.2 = (bf16[1024,384]{1,0:T(8,128)(2,1)S(1)}, f32[3,2,1024]{2,1,0:T(2,128)S(1)}) custom-call(s32[13]{0:T(128)S(1)} %concatenate.54.info.refs_0_, bf16[2,1024,1152]{2,1,0:T(8,128)(2,1)S(1)} %get-tuple-element.322.refs_0_.refs_3_.refs_4_.refs_1_.refs_9_.refs_10_.refs_5_.refs_6_, ...), custom_call_target="tpu_custom_call" | custom-call | flops 99999997952 | bytes 1 | tf_op jit(solution)/shard_map/attend/pallas_call | solution.py:640
  139.5 12.5 %attend.3 = (bf16[1024,384]{1,0:T(8,128)(2,1)S(1)}, f32[3,2,1024]{2,1,0:T(2,128)S(1)}) custom-call(s32[13]{0:T(128)S(1)} %concatenate.54.info.refs_0_, bf16[2,1024,1152]{2,1,0:T(8,128)(2,1)S(1)} %get-tuple-element.322.refs_0_.refs_3_.refs_4_.refs_1_.refs_9_.refs_10_.refs_5_.refs_6_, ...), custom_call_target="tpu_custom_call" | custom-call | flops 99999997952 | bytes 1 | tf_op jit(solution)/shard_map/attend/pallas_call | solution.py:640
  166.6 29.4 %feed_forward.2 = (f32[1024,768]{1,0:T(8,128)}, f32[1024,768]{1,0:T(8,128)}, bf16[8,48,1536]{2,1,0:T(8,128)(2,1)S(1)}, bf16[8,48,1536]{2,1,0:T(8,128)(2,1)}, bf1...) custom-call(s32[13]{0:T(128)S(1)} %concatenate.54.info.refs_0_, ...), custom_call_target="tpu_custom_call" | custom-call | flops 99999997952 | bytes 1 | tf_op jit(solution)/shard_map/feed_forward/pallas_call | solution.py:380
  202.8 29.8 %feed_forward.3 = (f32[1024,768]{1,0:T(8,128)}, f32[1024,768]{1,0:T(8,128)}, bf16[8,48,1536]{2,1,0:T(8,128)(2,1)S(1)}, bf16[8,48,1536]{2,1,0:T(8,128)(2,1)}, bf1...) custom-call(s32[13]{0:T(128)S(1)} %concatenate.54.info.refs_0_, bf16[1024,768]{1,0:T(8,128)(2,1)} %copy-done.44, ...), custom_call_target="tpu_custom_call" | custom-call | flops 99999997952 | bytes 1 | tf_op jit(solution)/shard_map/feed_forward/pallas_call | solution.py:380
  232.6 12.2 %post.1 = (bf16[1024,768]{1,0:T(8,128)(2,1)}, f32[1024,768]{1,0:T(8,128)}, bf16[1024,384]{1,0:T(8,128)(2,1)S(1)}, bf16[1024,384]{1,0:T(8,128)(2,1)S(1)}, f32[8,8...) custom-call(s32[13]{0:T(128)S(1)} %concatenate.54.info.refs_0_, ...), custom_call_target="tpu_custom_call" | custom-call | flops 99999997952 | bytes 1 | tf_op jit(solution)/shard_map/post/pallas_call | solution.py:468
  254.5 16.7 %attend_back.4 = (bf16[1024,384]{1,0:T(8,128)(2,1)S(1)}, bf16[1024,384]{1,0:T(8,128)(2,1)S(1)}, bf16[1024,384]{1,0:T(8,128)(2,1)S(1)}, bf16[1024,384]{1,0:T(8,128)(2,1)S(1)}, bf16[1024,384]{1,0:T(8,128)(2,1)S(1)}) custom-call(s32[13]{0:T(128)S(1)} %concatenate.54.info.refs_0_, bf16[2,1024,1152]{2,1,0:T(8,128)(2,1)S(1)} %copy-done.38, ...), custom_call_target="tpu_custom_call" | custom-call | flops 99999997952 | bytes 1 | tf_op jit(solution)/shard_map/attend_back/pallas_call | solution.py:811
  271.3 8.3 %collective-permute-done.36 = bf16[2,4,48,1536]{3,2,1,0:T(8,128)(2,1)S(1)} collective-permute-done((bf16[2,4,48,1536]{3,2,1,0:T(8,128)(2,1)S(1)}, bf16[2,4,48,1536]{3,2,1,0:T(8,128)(2,1)S(1)}, u32[]{:S(2)}, u32[]{:S(2)}) %collective-permute-start.36) | collective-permute-done | bytes 1179680 | tf_op jit(solution)/shard_map/ppermute | solution.py:46
  297.3 10.7 %attend_back.5 = (f32[1024,384]{1,0:T(8,128)S(1)}, bf16[512,384]{1,0:T(8,128)(2,1)S(1)}, bf16[512,384]{1,0:T(8,128)(2,1)S(1)}) custom-call(s32[13]{0:T(128)S(1)} %concatenate.54.info.refs_0_, bf16[2,1024,1152]{2,1,0:T(8,128)(2,1)S(1)} %copy-done.38, bf16[1024,384]{1,0:T(8,128)(2,1)S(1)} %get-tuple-element.418.refs_2_, bf16[1024,384]{1,0:T(8,128)(2,1)S(1)} %copy-done.50, ...), custom_call_target="tpu_custom_call" | custom-call | flops 99999997952 | bytes 1 | tf_op jit(solution)/shard_map/attend_back/pallas_call | solution.py:811
  316.7 7.1 %attend_back.6 = (f32[1024,384]{1,0:T(8,128)S(1)}, bf16[512,384]{1,0:T(8,128)(2,1)S(1)}, bf16[512,384]{1,0:T(8,128)(2,1)S(1)}) custom-call(s32[13]{0:T(128)S(1)} %concatenate.54.info.refs_0_, bf16[2,1024,1152]{2,1,0:T(8,128)(2,1)S(1)} %copy-done.38, bf16[1024,384]{1,0:T(8,128)(2,1)S(1)} %get-tuple-element.418.refs_2_, bf16[1024,384]{1,0:T(8,128)(2,1)S(1)} %copy-done.50, ...), custom_call_target="tpu_custom_call" | custom-call | flops 99999997952 | bytes 1 | tf_op jit(solution)/shard_map/attend_back/pallas_call | solution.py:811
  325.1 9.6 %collective-permute-done.43 = bf16[512,768]{1,0:T(8,128)(2,1)S(1)} collective-permute-done((bf16[512,768]{1,0:T(8,128)(2,1)S(1)}, bf16[512,768]{1,0:T(8,128)(2,1)S(1)}, u32[]{:S(2)}, u32[]{:S(2)}) %collective-permute-start.43) | collective-permute-done | bytes 786464 | tf_op jit(solution)/shard_map/ppermute | solution.py:46
  342.5 4.1 attend_back.7
  346.5 4.9 %collective-permute-start.52 = (bf16[512,768]{1,0:T(8,128)(2,1)S(1)}, bf16[512,768]{1,0:T(8,128)(2,1)S(1)}, u32[]{:S(2)}, u32[]{:S(2)}) collective-permute-start(bf16[512,768]{1,0:T(8,128)(2,1)S(1)} %get-tuple-element.581), channel_id=1, source_target_pairs={{0,1},{1,0},{2,3},{3,2},{4,5},{5,4},{6,7},{7,6},{8,9},{9,8},{10,11... | collective-permute-start | bytes 2359304 | tf_op jit(solution)/shard_map/ppermute | solution.py:46
  370.5 4.5 %last.1 = (f32[1024,768]{1,0:T(8,128)}, f32[8,8,768]{2,1,0:T(8,128)S(1)}) custom-call(s32[13]{0:T(128)S(1)} %concatenate.54.info.refs_0_, bf16[1024,768]{1,0:T(8,128)(2,1)S(1)} %copy-done.9, f32[1024,768]{1,0:T(8,128)S(1)} %convolution_add_fusion.own_ref, f32[1024,768]{1,0:T(8,128)S(1)} %pad_maximum_fusion.prompt_ref, ...), custom_call_target="tpu_custom_call" | custom-call | flops 99999997952 | bytes 1 | tf_op jit(solution)/shard_map/last/pallas_call | solution.py:531
  386.4 8.2 %collective-permute-done.55 = bf16[2,48,1152]{2,1,0:T(8,128)(2,1)S(1)} collective-permute-done((bf16[2,48,1152]{2,1,0:T(8,128)(2,1)S(1)}, bf16[2,48,1152]{2,1,0:T(8,128)(2,1)S(1)}, u32[]{:S(2)}, u32[]{:S(2)}) %collective-permute-start.55) | collective-permute-done | bytes 221216 | tf_op jit(solution)/shard_map/ppermute | solution.py:46
  397.4 4.6 %all-to-all-start.2 = ((bf16[32,8,768]{2,1,0:T(8,128)(2,1)}), bf16[32,8,768]{2,1,0:T(8,128)(2,1)S(1)}, u32[]{:S(2)}, u32[]{:S(2)}) async-start(bf16[32,8,768]{2,1,0:T(8,128)(2,1)} %fusion.8), calls=%async_computation.2 | async-start | bytes 786432 | tf_op jit(solution)/shard_map/all_to_all | solution.py:1203
  406.6 12.3 %collective-permute-done.56 = bf16[48,1152]{1,0:T(8,128)(2,1)S(1)} collective-permute-done((bf16[48,1152]{1,0:T(8,128)(2,1)S(1)}, bf16[48,1152]{1,0:T(8,128)(2,1)S(1)}, u32[]{:S(2)}, u32[]{:S(2)}) %collective-permute-start.56) | collective-permute-done | bytes 110624 | tf_op jit(solution)/shard_map/ppermute | solution.py:46
  (411 shorter events, 174.4 us)
Async XLA Ops:
  29.1 26.5 %collective-permute-start.4 = (bf16[4,48,1152]{2,1,0:T(8,128)(2,1)S(1)}, bf16[4,48,1152]{2,1,0:T(8,128)(2,1)S(1)}, u32[]{:S(2)}, u32[]{:S(2)}) collective-permute-start(bf16[4,48,1152]{2,1,0:T(8,128)(2,1)S(1)} %bitcast.251), channel_id=1, source_target_pairs={{0,1},{1,0},{2,3},{3,2},{4,5},{5,4},{6,7},{7,6},{8,9},{9,8},{10,11... | collective-permute-start | bytes 1327112 | tf_op jit(solution)/shard_map/ppermute | solution.py:46
  30.7 25.0 %collective-permute-start.3 = (bf16[4,48,1152]{2,1,0:T(8,128)(2,1)S(1)}, bf16[4,48,1152]{2,1,0:T(8,128)(2,1)S(1)}, u32[]{:S(2)}, u32[]{:S(2)}) collective-permute-start(bf16[4,48,1152]{2,1,0:T(8,128)(2,1)S(1)} %bitcast.252), channel_id=1, source_target_pairs={{0,4},{1,5},{2,6},{3,7},{4,0},{5,1},{6,2},{7,3},{8,12},{9,13},{10,... | collective-permute-start | bytes 1327112 | tf_op jit(solution)/shard_map/ppermute | solution.py:46
  31.8 23.1 %collective-permute-start.5 = (bf16[1,48,3456]{2,1,0:T(8,128)(2,1)S(1)}, bf16[1,48,3456]{2,1,0:T(8,128)(2,1)S(1)}, u32[]{:S(2)}, u32[]{:S(2)}) collective-permute-start(bf16[1,48,3456]{2,1,0:T(8,128)(2,1)S(1)} %maximum_bitcast_fusion.refs_1_), channel_id=1, source_target_pairs={{0,16},{1,17},{2,18},{3,19},{4,20},{5,21},{6,22},{7,23},{8,24},{9,... | collective-permute-start | bytes 995336 | tf_op jit(solution)/shard_map/ppermute | solution.py:46
  39.5 21.6 %all-to-all-start = ((f32[32,16,144]{2,1,0:T(8,128)}), f32[32,16,144]{2,1,0:T(8,128)}, u32[]{:S(2)}, u32[]{:S(2)}) async-start(f32[32,16,144]{2,1,0:T(8,128)} %bitcast.268), calls=%async_computation | async-start | bytes 1048576 | tf_op jit(solution)/shard_map/all_to_all | solution.py:937
  68.3 19.1 %collective-permute-start.11 = (bf16[2,48,3456]{2,1,0:T(8,128)(2,1)S(1)}, bf16[2,48,3456]{2,1,0:T(8,128)(2,1)S(1)}, u32[]{:S(2)}, u32[]{:S(2)}) collective-permute-start(bf16[2,48,3456]{2,1,0:T(8,128)(2,1)S(1)} %bitcast.221), channel_id=1, source_target_pairs={{0,8},{1,9},{2,10},{3,11},{4,12},{5,13},{6,14},{7,15},{8,0},{9,1},... | collective-permute-start | bytes 1990664 | tf_op jit(solution)/shard_map/ppermute | solution.py:46
  88.3 27.7 %collective-permute-start.19 = (bf16[4,48,384]{2,1,0:T(8,128)(2,1)}, bf16[4,48,384]{2,1,0:T(8,128)(2,1)}, u32[]{:S(2)}, u32[]{:S(2)}) collective-permute-start(bf16[4,48,384]{2,1,0:T(8,128)(2,1)} %bitcast.30.refs_1_), channel_id=1, source_target_pairs={{0,1},{1,0},{2,3},{3,2},{4,5},{5,4},{6,7},{7,6},{8,9},{9,8},{10,11... | collective-permute-start | bytes 442376 | tf_op jit(solution)/shard_map/ppermute | solution.py:46
  89.5 26.6 %collective-permute-start.18 = (bf16[4,48,384]{2,1,0:T(8,128)(2,1)}, bf16[4,48,384]{2,1,0:T(8,128)(2,1)}, u32[]{:S(2)}, u32[]{:S(2)}) collective-permute-start(bf16[4,48,384]{2,1,0:T(8,128)(2,1)} %bitcast.30.refs_1_), channel_id=1, source_target_pairs={{0,4},{1,5},{2,6},{3,7},{4,0},{5,1},{6,2},{7,3},{8,12},{9,13},{10,... | collective-permute-start | bytes 442376 | tf_op jit(solution)/shard_map/ppermute | solution.py:46
  90.8 16.5 %collective-permute-start.17 = (bf16[4,48,1536]{2,1,0:T(8,128)(2,1)S(1)}, bf16[4,48,1536]{2,1,0:T(8,128)(2,1)S(1)}, u32[]{:S(2)}, u32[]{:S(2)}) collective-permute-start(bf16[4,48,1536]{2,1,0:T(8,128)(2,1)S(1)} %bitcast.244), channel_id=1, source_target_pairs={{0,4},{1,5},{2,6},{3,7},{4,0},{5,1},{6,2},{7,3},{8,12},{9,13},{10,... | collective-permute-start | bytes 1769480 | tf_op jit(solution)/shard_map/ppermute | solution.py:46
  116.1 16.9 %collective-permute-start.22 = (bf16[4,48,384]{2,1,0:T(8,128)(2,1)}, bf16[4,48,384]{2,1,0:T(8,128)(2,1)S(1)}, u32[]{:S(2)}, u32[]{:S(2)}) collective-permute-start(bf16[4,48,384]{2,1,0:T(8,128)(2,1)} %collective-permute-done.19.refs_1_), channel_id=1, source_target_pairs={{0,4},{1,5},{2,6},{3,7},{4,0},{5,1},{6,2},{7,3},{8,12},{9,13},{10,... | collective-permute-start | bytes 442376 | tf_op jit(solution)/shard_map/ppermute | solution.py:46
  117.0 17.9 %collective-permute-start.21 = (bf16[4,48,1536]{2,1,0:T(8,128)(2,1)S(1)}, bf16[4,48,1536]{2,1,0:T(8,128)(2,1)S(1)}, u32[]{:S(2)}, u32[]{:S(2)}) collective-permute-start(bf16[4,48,1536]{2,1,0:T(8,128)(2,1)S(1)} %bitcast.245), channel_id=1, source_target_pairs={{0,1},{1,0},{2,3},{3,2},{4,5},{5,4},{6,7},{7,6},{8,9},{9,8},{10,11... | collective-permute-start | bytes 1769480 | tf_op jit(solution)/shard_map/ppermute | solution.py:46
  117.8 17.1 %collective-permute-start.23 = (bf16[8,48,1536]{2,1,0:T(8,128)(2,1)S(1)}, bf16[8,48,1536]{2,1,0:T(8,128)(2,1)S(1)}, u32[]{:S(2)}, u32[]{:S(2)}) collective-permute-start(bf16[8,48,1536]{2,1,0:T(8,128)(2,1)S(1)} %bitcast.227), channel_id=1, source_target_pairs={{0,2},{1,3},{2,0},{3,1},{4,6},{5,7},{6,4},{7,5},{8,10},{9,11},{10,... | collective-permute-start | bytes 3538952 | tf_op jit(solution)/shard_map/ppermute | solution.py:46
  154.3 41.6 %collective-permute-start.29 = (bf16[4,48,1536]{2,1,0:T(8,128)(2,1)}, bf16[4,48,1536]{2,1,0:T(8,128)(2,1)}, u32[]{:S(2)}, u32[]{:S(2)}) collective-permute-start(bf16[4,48,1536]{2,1,0:T(8,128)(2,1)} %collective-permute-done.24.refs_1_), channel_id=1, source_target_pairs={{0,4},{1,5},{2,6},{3,7},{4,0},{5,1},{6,2},{7,3},{8,12},{9,13},{10,... | collective-permute-start | bytes 1769480 | tf_op jit(solution)/shard_map/ppermute | solution.py:46
  156.2 39.7 %collective-permute-start.30 = (bf16[8,48,1536]{2,1,0:T(8,128)(2,1)}, bf16[8,48,1536]{2,1,0:T(8,128)(2,1)}, u32[]{:S(2)}, u32[]{:S(2)}) collective-permute-start(bf16[8,48,1536]{2,1,0:T(8,128)(2,1)} %bitcast.38.refs_7_), channel_id=1, source_target_pairs={{0,2},{1,3},{2,0},{3,1},{4,6},{5,7},{6,4},{7,5},{8,10},{9,11},{10,... | collective-permute-start | bytes 3538952 | tf_op jit(solution)/shard_map/ppermute | solution.py:46
  202.2 30.4 %collective-permute-start.32 = (bf16[8,48,1536]{2,1,0:T(8,128)(2,1)}, bf16[8,48,1536]{2,1,0:T(8,128)(2,1)S(1)}, u32[]{:S(2)}, u32[]{:S(2)}) collective-permute-start(bf16[8,48,1536]{2,1,0:T(8,128)(2,1)} %get-tuple-element.353), channel_id=1, source_target_pairs={{0,2},{1,3},{2,0},{3,1},{4,6},{5,7},{6,4},{7,5},{8,10},{9,11},{10,... | collective-permute-start | bytes 3538952 | tf_op jit(solution)/shard_map/ppermute | solution.py:46
  202.7 29.8 %collective-permute-start.33 = (bf16[8,48,1536]{2,1,0:T(8,128)(2,1)S(1)}, bf16[8,48,1536]{2,1,0:T(8,128)(2,1)}, u32[]{:S(2)}, u32[]{:S(2)}) collective-permute-start(bf16[8,48,1536]{2,1,0:T(8,128)(2,1)S(1)} %copy-done.73), channel_id=1, source_target_pairs={{0,2},{1,3},{2,0},{3,1},{4,6},{5,7},{6,4},{7,5},{8,10},{9,11},{10,... | collective-permute-start | bytes 3538952 | tf_op jit(solution)/shard_map/ppermute | solution.py:46
  250.9 20.4 %collective-permute-start.38 = (bf16[2,8,48,384]{3,2,1,0:T(8,128)(2,1)S(1)}, bf16[2,8,48,384]{3,2,1,0:T(8,128)(2,1)S(1)}, u32[]{:S(2)}, u32[]{:S(2)}) collective-permute-start(bf16[2,8,48,384]{3,2,1,0:T(8,128)(2,1)S(1)} %get-tuple-element.383), channel_id=1, source_target_pairs={{0,2},{1,3},{2,0},{3,1},{4,6},{5,7},{6,4},{7,5},{8,10},{9,11},{10,... | collective-permute-start | bytes 1769480 | tf_op jit(solution)/shard_map/ppermute | solution.py:46
  251.5 28.1 %collective-permute-start.36 = (bf16[2,4,48,1536]{3,2,1,0:T(8,128)(2,1)S(1)}, bf16[2,4,48,1536]{3,2,1,0:T(8,128)(2,1)S(1)}, u32[]{:S(2)}, u32[]{:S(2)}) collective-permute-start(bf16[2,4,48,1536]{3,2,1,0:T(8,128)(2,1)S(1)} %pad_maximum_fusion.4), channel_id=1, source_target_pairs={{0,4},{1,5},{2,6},{3,7},{4,0},{5,1},{6,2},{7,3},{8,12},{9,13},{10,... | collective-permute-start | bytes 3538952 | tf_op jit(solution)/shard_map/ppermute | solution.py:46
  253.0 28.0 %collective-permute-start.37 = (bf16[8,48,1536]{2,1,0:T(8,128)(2,1)S(1)}, bf16[8,48,1536]{2,1,0:T(8,128)(2,1)S(1)}, u32[]{:S(2)}, u32[]{:S(2)}) collective-permute-start(bf16[8,48,1536]{2,1,0:T(8,128)(2,1)S(1)} %add_convert_fusion.1), channel_id=1, source_target_pairs={{0,1},{1,0},{2,3},{3,2},{4,5},{5,4},{6,7},{7,6},{8,9},{9,8},{10,11... | collective-permute-start | bytes 3538952 | tf_op jit(solution)/shard_map/ppermute | solution.py:46
  281.3 26.8 %collective-permute-start.42 = (bf16[2,4,48,384]{3,2,1,0:T(8,128)(2,1)S(1)}, bf16[2,4,48,384]{3,2,1,0:T(8,128)(2,1)S(1)}, u32[]{:S(2)}, u32[]{:S(2)}) collective-permute-start(bf16[2,4,48,384]{3,2,1,0:T(8,128)(2,1)S(1)} %get-tuple-element.555), channel_id=1, source_target_pairs={{0,4},{1,5},{2,6},{3,7},{4,0},{5,1},{6,2},{7,3},{8,12},{9,13},{10,... | collective-permute-start | bytes 884744 | tf_op jit(solution)/shard_map/ppermute | solution.py:46
  282.8 25.3 %collective-permute-start.40 = (bf16[4,48,1536]{2,1,0:T(8,128)(2,1)S(1)}, bf16[4,48,1536]{2,1,0:T(8,128)(2,1)S(1)}, u32[]{:S(2)}, u32[]{:S(2)}) collective-permute-start(bf16[4,48,1536]{2,1,0:T(8,128)(2,1)S(1)} %get-tuple-element.545), channel_id=1, source_target_pairs={{0,1},{1,0},{2,3},{3,2},{4,5},{5,4},{6,7},{7,6},{8,9},{9,8},{10,11... | collective-permute-start | bytes 1769480 | tf_op jit(solution)/shard_map/ppermute | solution.py:46
  284.2 23.9 %collective-permute-start.41 = (bf16[4,48,1536]{2,1,0:T(8,128)(2,1)S(1)}, bf16[4,48,1536]{2,1,0:T(8,128)(2,1)S(1)}, u32[]{:S(2)}, u32[]{:S(2)}) collective-permute-start(bf16[4,48,1536]{2,1,0:T(8,128)(2,1)S(1)} %get-tuple-element.533), channel_id=1, source_target_pairs={{0,4},{1,5},{2,6},{3,7},{4,0},{5,1},{6,2},{7,3},{8,12},{9,13},{10,... | collective-permute-start | bytes 1769480 | tf_op jit(solution)/shard_map/ppermute | solution.py:46
  316.5 18.2 %collective-permute-start.43 = (bf16[512,768]{1,0:T(8,128)(2,1)S(1)}, bf16[512,768]{1,0:T(8,128)(2,1)S(1)}, u32[]{:S(2)}, u32[]{:S(2)}) collective-permute-start(bf16[512,768]{1,0:T(8,128)(2,1)S(1)} %get-tuple-element.579), channel_id=1, source_target_pairs={{0,1},{1,0},{2,3},{3,2},{4,5},{5,4},{6,7},{7,6},{8,9},{9,8},{10,11... | collective-permute-start | bytes 2359304 | tf_op jit(solution)/shard_map/ppermute | solution.py:46
  346.5 20.1 %collective-permute-start.52 = (bf16[512,768]{1,0:T(8,128)(2,1)S(1)}, bf16[512,768]{1,0:T(8,128)(2,1)S(1)}, u32[]{:S(2)}, u32[]{:S(2)}) collective-permute-start(bf16[512,768]{1,0:T(8,128)(2,1)S(1)} %get-tuple-element.581), channel_id=1, source_target_pairs={{0,1},{1,0},{2,3},{3,2},{4,5},{5,4},{6,7},{7,6},{8,9},{9,8},{10,11... | collective-permute-start | bytes 2359304 | tf_op jit(solution)/shard_map/ppermute | solution.py:46
  397.4 22.3 %all-to-all-start.2 = ((bf16[32,8,768]{2,1,0:T(8,128)(2,1)}), bf16[32,8,768]{2,1,0:T(8,128)(2,1)S(1)}, u32[]{:S(2)}, u32[]{:S(2)}) async-start(bf16[32,8,768]{2,1,0:T(8,128)(2,1)} %fusion.8), calls=%async_computation.2 | async-start | bytes 786432 | tf_op jit(solution)/shard_map/all_to_all | solution.py:1203
  (114 other events, 1311.2 us)

commit v5 on v4

--- a/solution.py
+++ b/solution.py
@@ -1068,10 +1068,9 @@
     q_cur = weight_part(dqkv_1, dkvp_1)
     q_came = swap(pick(q_cur, 1 - core, 2), CORE)
     q_keep = pick(q_cur, core, 2)
-    own_sum = dot(dqkv_1, qkv[1], NT)
     prompt_sum = prompt_part(1, dkvp_1)
-    q_keep, own_sum, prompt_sum, grad_0, d_keep, u_keep, o_keep = tie(
-        q_keep, own_sum, prompt_sum, grad_0, d_keep, u_keep, o_keep
+    q_keep, prompt_sum, grad_0, d_keep, u_keep, o_keep = tie(
+        q_keep, prompt_sum, grad_0, d_keep, u_keep, o_keep
     )
 
     dq_0, dkp_a, dvp_a = back(0, grad_0, (0, 1), False, None, False)
@@ -1125,7 +1124,7 @@
     dqkv_0 = jnp.concatenate([dq_0, dk_0, dv_0], 1)
     q_cur = weight_part(dqkv_0, jnp.concatenate([dkvp_a, dkvp_b], 0))
     q_came, q_keep = swap(pick(q_cur, 1 - core, 2), CORE), pick(q_cur, core, 2)
-    own_sum = own_sum + dot(dqkv_0, qkv[0], NT)
+    own_sum = dot(after(dqkv_1, dq_0), qkv[1], NT) + dot(dqkv_0, qkv[0], NT)
     q_came, q_keep, own_sum, q_send = tie(q_came, q_keep, own_sum, q_send)
     q_cur = plus(q_keep, q_came)
     q_came, q_keep = swap(pick(q_cur, 1 - near, 1), NEAR), pick(q_cur, near, 1)

time: 425 us -> 421 us (level)
    unnamed x164 -> x172, local copies, waits for them, and re-layouts: 13.3 us -> 12.6 us
where the time goes in v5:
time: 421 us; the launch traced here: 417 us
  Pallas kernels  177 us (42%)
  waiting for transfers between devices  89.3 us (21%)
  starting transfers between devices  77.3 us (18%)
  local copies, waits for them, and re-layouts  31.1 us (7%)
  matrix products  19.6 us (5%)
  other arithmetic  19.2 us (5%)
    ppermute x58, waiting for transfers between devices, swap(): return lax.ppermute(x, BOTH, [(i, i ^ bits) for i in range(count)])  83.8 us
    ppermute x58, starting transfers between devices, swap(): return lax.ppermute(x, BOTH, [(i, i ^ bits) for i in range(count)])  65.3 us
    pallas_call x2, Pallas kernels, feed_forward(): pl.pallas_call(lambda *refs: mlp_kernel(first, len(weights), *refs), grid...  59.2 us
    pallas_call x4, Pallas kernels, attend_back(): pl.pallas_call(lambda *refs: backward_kernel(first, last, tiles, own, *re...  38.5 us
    pallas_call x2, Pallas kernels, attend(): pl.pallas_call(forward_kernel, grid_spec=pltpu.PrefetchScalarGridSpec(num...  24.5 us
    pallas_call x2, Pallas kernels, project(): pl.pallas_call(kernel, grid_spec=pltpu.PrefetchScalarGridSpec(num_scalar_...  19.9 us
    dot_general x13, matrix products, dot(): return lax.dot_general(left, right, dims, preferred_element_type=f32)  18.2 us
    pallas_call x20, Pallas kernels, join(): pl.pallas_call(lambda *refs: join_kernel(sizes, *refs), grid_spec=pltpu.P...  14 us
  transfers between devices with their start and end apart: 61, of which 25 were waited for; matrix products, arithmetic and copies ran while one was open for 12% of the time, Pallas kernels for 38%

profile of v5, /device:TPU:0, one launch (start us, length us, event | category | flops | bytes accessed | tf_op | source)
XLA Modules:
  0.0 417.1 jit_solution(10994890063380933046)
XLA Ops:
  3.1 4.1 collective-permute-start
  16.7 5.4 %multiply_sine_fusion = (f32[1024,128]{1,0:T(8,128)}, f32[1024,128]{1,0:T(8,128)}, f32[1024,128]{1,0:T(8,128)}, f32[1024,128]{1,0:T(8,128)}) fusion(f32[1024]{0:T(1024)S(1)} %get-tuple-element.584, f32[128]{0:T(128)S(1)} %fusion.50, f32[1024]{0:T(1024)S(1)} %get-tuple-element.583), kind=kLoop, calls=%fused_computation.49 | loop fusion | flops 262144 | bytes 2105856 | tf_op jit(solution)/shard_map/sin | solution.py:912
  44.2 10.7 %collective-permute-done.5.refs_2_ = bf16[1,48,3456]{2,1,0:T(8,128)(2,1)S(1)} collective-permute-done((bf16[1,48,3456]{2,1,0:T(8,128)(2,1)S(1)}, bf16[1,48,3456]{2,1,0:T(8,128)(2,1)S(1)}, u32[]{:S(2)}, u32[]{:S(2)}) %collective-permute-start.5) | collective-permute-done | bytes 331808 | tf_op jit(solution)/shard_map/ppermute | solution.py:46
  55.6 5.5 %all-to-all-done = f32[32,16,144]{2,1,0:T(8,128)} async-done(((f32[32,16,144]{2,1,0:T(8,128)}), f32[32,16,144]{2,1,0:T(8,128)}, u32[]{:S(2)}, u32[]{:S(2)}) %all-to-all-start) | async-done | bytes 294944 | tf_op jit(solution)/shard_map/all_to_all | solution.py:937
  61.1 5.3 %collective-permute-done.12.refs_2_ = bf16[4,48,1152]{2,1,0:T(8,128)(2,1)S(1)} collective-permute-done((bf16[4,48,1152]{2,1,0:T(8,128)(2,1)S(1)}, bf16[4,48,1152]{2,1,0:T(8,128)(2,1)S(1)}, u32[]{:S(2)}, u32[]{:S(2)}) %collective-permute-start.12) | collective-permute-done | bytes 442400 | tf_op jit(solution)/shard_map/ppermute | solution.py:46
  82.8 4.6 %collective-permute-done.11.refs_2_ = bf16[2,48,3456]{2,1,0:T(8,128)(2,1)S(1)} collective-permute-done((bf16[2,48,3456]{2,1,0:T(8,128)(2,1)S(1)}, bf16[2,48,3456]{2,1,0:T(8,128)(2,1)S(1)}, u32[]{:S(2)}, u32[]{:S(2)}) %collective-permute-start.11) | collective-permute-done | bytes 663584 | tf_op jit(solution)/shard_map/ppermute | solution.py:46
  92.4 11.2 %project.2 = (bf16[2,1024,1152]{2,1,0:T(8,128)(2,1)S(1)}, bf16[1024,768]{1,0:T(8,128)(2,1)S(1)}) custom-call(s32[13]{0:T(128)S(1)} %concatenate.54.info.refs_0_, bf16[1024,768]{1,0:T(8,128)(2,1)S(1)} %copy-done.8, f32[16,4608]{1,0:T(8,128)S(1)} %copy-done.31, bf16[768,1152]{1,0:T(8,128)(2,1)S(1)} %bitcast.212, bf16[768,1152]{1,0:T(8,128)(2,1)S(1)} %bitcast.223, ...), custom_call_target="tpu_custom_call" | custom-call | flops 99999997952 | bytes 1 | tf_op jit(solution)/shard_map/project/pallas_call | solution.py:220
  107.3 8.7 %project.3 = (bf16[2,1024,768]{2,1,0:T(8,128)(2,1)S(1)}, bf16[1024,768]{1,0:T(8,128)(2,1)S(1)}) custom-call(s32[13]{0:T(128)S(1)} %concatenate.54.info.refs_0_, bf16[1024,768]{1,0:T(8,128)(2,1)S(1)} %copy-done.8, bf16[256,768]{1,0:T(8,128)(2,1)S(1)} %copy-done.34, bf16[384,768]{1,0:T(8,128)(2,1)} %collective-permute-done.15.refs_1_, ...), custom_call_target="tpu_custom_call" | custom-call | flops 99999997952 | bytes 1 | tf_op jit(solution)/shard_map/project/pallas_call | solution.py:220
  120.9 12.0 %attend.2 = (bf16[1024,384]{1,0:T(8,128)(2,1)S(1)}, f32[3,2,1024]{2,1,0:T(2,128)S(1)}) custom-call(s32[13]{0:T(128)S(1)} %concatenate.54.info.refs_0_, bf16[2,1024,1152]{2,1,0:T(8,128)(2,1)S(1)} %get-tuple-element.322.refs_0_.refs_3_.refs_4_.refs_1_.refs_9_.refs_10_.refs_5_.refs_6_, ...), custom_call_target="tpu_custom_call" | custom-call | flops 99999997952 | bytes 1 | tf_op jit(solution)/shard_map/attend/pallas_call | solution.py:640
  139.5 12.5 %attend.3 = (bf16[1024,384]{1,0:T(8,128)(2,1)S(1)}, f32[3,2,1024]{2,1,0:T(2,128)S(1)}) custom-call(s32[13]{0:T(128)S(1)} %concatenate.54.info.refs_0_, bf16[2,1024,1152]{2,1,0:T(8,128)(2,1)S(1)} %get-tuple-element.322.refs_0_.refs_3_.refs_4_.refs_1_.refs_9_.refs_10_.refs_5_.refs_6_, ...), custom_call_target="tpu_custom_call" | custom-call | flops 99999997952 | bytes 1 | tf_op jit(solution)/shard_map/attend/pallas_call | solution.py:640
  166.6 29.4 %feed_forward.2 = (f32[1024,768]{1,0:T(8,128)}, f32[1024,768]{1,0:T(8,128)}, bf16[8,48,1536]{2,1,0:T(8,128)(2,1)S(1)}, bf16[8,48,1536]{2,1,0:T(8,128)(2,1)}, bf1...) custom-call(s32[13]{0:T(128)S(1)} %concatenate.54.info.refs_0_, ...), custom_call_target="tpu_custom_call" | custom-call | flops 99999997952 | bytes 1 | tf_op jit(solution)/shard_map/feed_forward/pallas_call | solution.py:380
  202.8 29.8 %feed_forward.3 = (f32[1024,768]{1,0:T(8,128)}, f32[1024,768]{1,0:T(8,128)}, bf16[8,48,1536]{2,1,0:T(8,128)(2,1)S(1)}, bf16[8,48,1536]{2,1,0:T(8,128)(2,1)}, bf1...) custom-call(s32[13]{0:T(128)S(1)} %concatenate.54.info.refs_0_, bf16[1024,768]{1,0:T(8,128)(2,1)} %copy-done.45, ...), custom_call_target="tpu_custom_call" | custom-call | flops 99999997952 | bytes 1 | tf_op jit(solution)/shard_map/feed_forward/pallas_call | solution.py:380
  232.7 12.2 %post.1 = (bf16[1024,768]{1,0:T(8,128)(2,1)}, f32[1024,768]{1,0:T(8,128)}, bf16[1024,384]{1,0:T(8,128)(2,1)S(1)}, bf16[1024,384]{1,0:T(8,128)(2,1)S(1)}, f32[8,8...) custom-call(s32[13]{0:T(128)S(1)} %concatenate.54.info.refs_0_, ...), custom_call_target="tpu_custom_call" | custom-call | flops 99999997952 | bytes 1 | tf_op jit(solution)/shard_map/post/pallas_call | solution.py:468
  254.6 16.7 %attend_back.4 = (bf16[1024,384]{1,0:T(8,128)(2,1)S(1)}, bf16[1024,384]{1,0:T(8,128)(2,1)S(1)}, bf16[1024,384]{1,0:T(8,128)(2,1)S(1)}, bf16[1024,384]{1,0:T(8,128)(2,1)S(1)}, bf16[1024,384]{1,0:T(8,128)(2,1)S(1)}) custom-call(s32[13]{0:T(128)S(1)} %concatenate.54.info.refs_0_, bf16[2,1024,1152]{2,1,0:T(8,128)(2,1)S(1)} %copy-done.39, ...), custom_call_target="tpu_custom_call" | custom-call | flops 99999997952 | bytes 1 | tf_op jit(solution)/shard_map/attend_back/pallas_call | solution.py:811
  271.3 8.3 %collective-permute-done.36 = bf16[2,4,48,1536]{3,2,1,0:T(8,128)(2,1)S(1)} collective-permute-done((bf16[2,4,48,1536]{3,2,1,0:T(8,128)(2,1)S(1)}, bf16[2,4,48,1536]{3,2,1,0:T(8,128)(2,1)S(1)}, u32[]{:S(2)}, u32[]{:S(2)}) %collective-permute-start.36) | collective-permute-done | bytes 1179680 | tf_op jit(solution)/shard_map/ppermute | solution.py:46
  293.5 10.7 %attend_back.5 = (f32[1024,384]{1,0:T(8,128)S(1)}, bf16[512,384]{1,0:T(8,128)(2,1)S(1)}, bf16[512,384]{1,0:T(8,128)(2,1)S(1)}) custom-call(s32[13]{0:T(128)S(1)} %concatenate.54.info.refs_0_, bf16[2,1024,1152]{2,1,0:T(8,128)(2,1)S(1)} %copy-done.39, bf16[1024,384]{1,0:T(8,128)(2,1)S(1)} %get-tuple-element.418.refs_2_, bf16[1024,384]{1,0:T(8,128)(2,1)S(1)} %copy-done.51, ...), custom_call_target="tpu_custom_call" | custom-call | flops 99999997952 | bytes 1 | tf_op jit(solution)/shard_map/attend_back/pallas_call | solution.py:811
  312.9 7.1 %attend_back.6 = (f32[1024,384]{1,0:T(8,128)S(1)}, bf16[512,384]{1,0:T(8,128)(2,1)S(1)}, bf16[512,384]{1,0:T(8,128)(2,1)S(1)}) custom-call(s32[13]{0:T(128)S(1)} %concatenate.54.info.refs_0_, bf16[2,1024,1152]{2,1,0:T(8,128)(2,1)S(1)} %copy-done.39, bf16[1024,384]{1,0:T(8,128)(2,1)S(1)} %get-tuple-element.418.refs_2_, bf16[1024,384]{1,0:T(8,128)(2,1)S(1)} %copy-done.51, ...), custom_call_target="tpu_custom_call" | custom-call | flops 99999997952 | bytes 1 | tf_op jit(solution)/shard_map/attend_back/pallas_call | solution.py:811
  321.2 9.7 %collective-permute-done.43 = bf16[512,768]{1,0:T(8,128)(2,1)S(1)} collective-permute-done((bf16[512,768]{1,0:T(8,128)(2,1)S(1)}, bf16[512,768]{1,0:T(8,128)(2,1)S(1)}, u32[]{:S(2)}, u32[]{:S(2)}) %collective-permute-start.43) | collective-permute-done | bytes 786464 | tf_op jit(solution)/shard_map/ppermute | solution.py:46
  338.6 4.1 attend_back.7
  342.7 4.9 %collective-permute-start.52 = (bf16[512,768]{1,0:T(8,128)(2,1)S(1)}, bf16[512,768]{1,0:T(8,128)(2,1)S(1)}, u32[]{:S(2)}, u32[]{:S(2)}) collective-permute-start(bf16[512,768]{1,0:T(8,128)(2,1)S(1)} %get-tuple-element.581), channel_id=1, source_target_pairs={{0,1},{1,0},{2,3},{3,2},{4,5},{5,4},{6,7},{7,6},{8,9},{9,8},{10,11... | collective-permute-start | bytes 2359304 | tf_op jit(solution)/shard_map/ppermute | solution.py:46
  365.9 4.5 %last.1 = (f32[1024,768]{1,0:T(8,128)}, f32[8,8,768]{2,1,0:T(8,128)S(1)}) custom-call(s32[13]{0:T(128)S(1)} %concatenate.54.info.refs_0_, bf16[1024,768]{1,0:T(8,128)(2,1)S(1)} %copy-done.10, f32[1024,768]{1,0:T(8,128)S(1)} %convolution_add_fusion.own_ref, f32[1024,768]{1,0:T(8,128)S(1)} %pad_maximum_fusion.prompt_ref, ...), custom_call_target="tpu_custom_call" | custom-call | flops 99999997952 | bytes 1 | tf_op jit(solution)/shard_map/last/pallas_call | solution.py:531
  382.9 8.2 %collective-permute-done.55 = bf16[2,48,1152]{2,1,0:T(8,128)(2,1)S(1)} collective-permute-done((bf16[2,48,1152]{2,1,0:T(8,128)(2,1)S(1)}, bf16[2,48,1152]{2,1,0:T(8,128)(2,1)S(1)}, u32[]{:S(2)}, u32[]{:S(2)}) %collective-permute-start.55) | collective-permute-done | bytes 221216 | tf_op jit(solution)/shard_map/ppermute | solution.py:46
  393.9 4.6 %all-to-all-start.2 = ((bf16[32,8,768]{2,1,0:T(8,128)(2,1)}), bf16[32,8,768]{2,1,0:T(8,128)(2,1)S(1)}, u32[]{:S(2)}, u32[]{:S(2)}) async-start(bf16[32,8,768]{2,1,0:T(8,128)(2,1)} %fusion.8), calls=%async_computation.2 | async-start | bytes 786432 | tf_op jit(solution)/shard_map/all_to_all | solution.py:1202
  403.1 12.3 %collective-permute-done.56 = bf16[48,1152]{1,0:T(8,128)(2,1)S(1)} collective-permute-done((bf16[48,1152]{1,0:T(8,128)(2,1)S(1)}, bf16[48,1152]{1,0:T(8,128)(2,1)S(1)}, u32[]{:S(2)}, u32[]{:S(2)}) %collective-permute-start.56) | collective-permute-done | bytes 110624 | tf_op jit(solution)/shard_map/ppermute | solution.py:46
  (419 shorter events, 170.8 us)
Async XLA Ops:
  29.1 26.5 %collective-permute-start.4 = (bf16[4,48,1152]{2,1,0:T(8,128)(2,1)S(1)}, bf16[4,48,1152]{2,1,0:T(8,128)(2,1)S(1)}, u32[]{:S(2)}, u32[]{:S(2)}) collective-permute-start(bf16[4,48,1152]{2,1,0:T(8,128)(2,1)S(1)} %bitcast.251), channel_id=1, source_target_pairs={{0,1},{1,0},{2,3},{3,2},{4,5},{5,4},{6,7},{7,6},{8,9},{9,8},{10,11... | collective-permute-start | bytes 1327112 | tf_op jit(solution)/shard_map/ppermute | solution.py:46
  30.7 25.0 %collective-permute-start.3 = (bf16[4,48,1152]{2,1,0:T(8,128)(2,1)S(1)}, bf16[4,48,1152]{2,1,0:T(8,128)(2,1)S(1)}, u32[]{:S(2)}, u32[]{:S(2)}) collective-permute-start(bf16[4,48,1152]{2,1,0:T(8,128)(2,1)S(1)} %bitcast.252), channel_id=1, source_target_pairs={{0,4},{1,5},{2,6},{3,7},{4,0},{5,1},{6,2},{7,3},{8,12},{9,13},{10,... | collective-permute-start | bytes 1327112 | tf_op jit(solution)/shard_map/ppermute | solution.py:46
  31.8 23.1 %collective-permute-start.5 = (bf16[1,48,3456]{2,1,0:T(8,128)(2,1)S(1)}, bf16[1,48,3456]{2,1,0:T(8,128)(2,1)S(1)}, u32[]{:S(2)}, u32[]{:S(2)}) collective-permute-start(bf16[1,48,3456]{2,1,0:T(8,128)(2,1)S(1)} %maximum_bitcast_fusion.refs_1_), channel_id=1, source_target_pairs={{0,16},{1,17},{2,18},{3,19},{4,20},{5,21},{6,22},{7,23},{8,24},{9,... | collective-permute-start | bytes 995336 | tf_op jit(solution)/shard_map/ppermute | solution.py:46
  39.5 21.6 %all-to-all-start = ((f32[32,16,144]{2,1,0:T(8,128)}), f32[32,16,144]{2,1,0:T(8,128)}, u32[]{:S(2)}, u32[]{:S(2)}) async-start(f32[32,16,144]{2,1,0:T(8,128)} %bitcast.268), calls=%async_computation | async-start | bytes 1048576 | tf_op jit(solution)/shard_map/all_to_all | solution.py:937
  68.3 19.1 %collective-permute-start.11 = (bf16[2,48,3456]{2,1,0:T(8,128)(2,1)S(1)}, bf16[2,48,3456]{2,1,0:T(8,128)(2,1)S(1)}, u32[]{:S(2)}, u32[]{:S(2)}) collective-permute-start(bf16[2,48,3456]{2,1,0:T(8,128)(2,1)S(1)} %bitcast.221), channel_id=1, source_target_pairs={{0,8},{1,9},{2,10},{3,11},{4,12},{5,13},{6,14},{7,15},{8,0},{9,1},... | collective-permute-start | bytes 1990664 | tf_op jit(solution)/shard_map/ppermute | solution.py:46
  88.3 27.7 %collective-permute-start.19 = (bf16[4,48,384]{2,1,0:T(8,128)(2,1)}, bf16[4,48,384]{2,1,0:T(8,128)(2,1)}, u32[]{:S(2)}, u32[]{:S(2)}) collective-permute-start(bf16[4,48,384]{2,1,0:T(8,128)(2,1)} %bitcast.30.refs_1_), channel_id=1, source_target_pairs={{0,1},{1,0},{2,3},{3,2},{4,5},{5,4},{6,7},{7,6},{8,9},{9,8},{10,11... | collective-permute-start | bytes 442376 | tf_op jit(solution)/shard_map/ppermute | solution.py:46
  89.5 26.6 %collective-permute-start.18 = (bf16[4,48,384]{2,1,0:T(8,128)(2,1)}, bf16[4,48,384]{2,1,0:T(8,128)(2,1)}, u32[]{:S(2)}, u32[]{:S(2)}) collective-permute-start(bf16[4,48,384]{2,1,0:T(8,128)(2,1)} %bitcast.30.refs_1_), channel_id=1, source_target_pairs={{0,4},{1,5},{2,6},{3,7},{4,0},{5,1},{6,2},{7,3},{8,12},{9,13},{10,... | collective-permute-start | bytes 442376 | tf_op jit(solution)/shard_map/ppermute | solution.py:46
  90.8 16.5 %collective-permute-start.17 = (bf16[4,48,1536]{2,1,0:T(8,128)(2,1)S(1)}, bf16[4,48,1536]{2,1,0:T(8,128)(2,1)S(1)}, u32[]{:S(2)}, u32[]{:S(2)}) collective-permute-start(bf16[4,48,1536]{2,1,0:T(8,128)(2,1)S(1)} %bitcast.244), channel_id=1, source_target_pairs={{0,4},{1,5},{2,6},{3,7},{4,0},{5,1},{6,2},{7,3},{8,12},{9,13},{10,... | collective-permute-start | bytes 1769480 | tf_op jit(solution)/shard_map/ppermute | solution.py:46
  116.1 16.9 %collective-permute-start.22 = (bf16[4,48,384]{2,1,0:T(8,128)(2,1)}, bf16[4,48,384]{2,1,0:T(8,128)(2,1)S(1)}, u32[]{:S(2)}, u32[]{:S(2)}) collective-permute-start(bf16[4,48,384]{2,1,0:T(8,128)(2,1)} %collective-permute-done.19.refs_1_), channel_id=1, source_target_pairs={{0,4},{1,5},{2,6},{3,7},{4,0},{5,1},{6,2},{7,3},{8,12},{9,13},{10,... | collective-permute-start | bytes 442376 | tf_op jit(solution)/shard_map/ppermute | solution.py:46
  117.0 17.9 %collective-permute-start.21 = (bf16[4,48,1536]{2,1,0:T(8,128)(2,1)S(1)}, bf16[4,48,1536]{2,1,0:T(8,128)(2,1)S(1)}, u32[]{:S(2)}, u32[]{:S(2)}) collective-permute-start(bf16[4,48,1536]{2,1,0:T(8,128)(2,1)S(1)} %bitcast.245), channel_id=1, source_target_pairs={{0,1},{1,0},{2,3},{3,2},{4,5},{5,4},{6,7},{7,6},{8,9},{9,8},{10,11... | collective-permute-start | bytes 1769480 | tf_op jit(solution)/shard_map/ppermute | solution.py:46
  117.8 17.1 %collective-permute-start.23 = (bf16[8,48,1536]{2,1,0:T(8,128)(2,1)S(1)}, bf16[8,48,1536]{2,1,0:T(8,128)(2,1)S(1)}, u32[]{:S(2)}, u32[]{:S(2)}) collective-permute-start(bf16[8,48,1536]{2,1,0:T(8,128)(2,1)S(1)} %bitcast.227), channel_id=1, source_target_pairs={{0,2},{1,3},{2,0},{3,1},{4,6},{5,7},{6,4},{7,5},{8,10},{9,11},{10,... | collective-permute-start | bytes 3538952 | tf_op jit(solution)/shard_map/ppermute | solution.py:46
  154.3 41.6 %collective-permute-start.29 = (bf16[4,48,1536]{2,1,0:T(8,128)(2,1)}, bf16[4,48,1536]{2,1,0:T(8,128)(2,1)}, u32[]{:S(2)}, u32[]{:S(2)}) collective-permute-start(bf16[4,48,1536]{2,1,0:T(8,128)(2,1)} %collective-permute-done.24.refs_1_), channel_id=1, source_target_pairs={{0,4},{1,5},{2,6},{3,7},{4,0},{5,1},{6,2},{7,3},{8,12},{9,13},{10,... | collective-permute-start | bytes 1769480 | tf_op jit(solution)/shard_map/ppermute | solution.py:46
  156.3 39.7 %collective-permute-start.30 = (bf16[8,48,1536]{2,1,0:T(8,128)(2,1)}, bf16[8,48,1536]{2,1,0:T(8,128)(2,1)}, u32[]{:S(2)}, u32[]{:S(2)}) collective-permute-start(bf16[8,48,1536]{2,1,0:T(8,128)(2,1)} %bitcast.38.refs_7_), channel_id=1, source_target_pairs={{0,2},{1,3},{2,0},{3,1},{4,6},{5,7},{6,4},{7,5},{8,10},{9,11},{10,... | collective-permute-start | bytes 3538952 | tf_op jit(solution)/shard_map/ppermute | solution.py:46
  202.2 30.4 %collective-permute-start.32 = (bf16[8,48,1536]{2,1,0:T(8,128)(2,1)}, bf16[8,48,1536]{2,1,0:T(8,128)(2,1)S(1)}, u32[]{:S(2)}, u32[]{:S(2)}) collective-permute-start(bf16[8,48,1536]{2,1,0:T(8,128)(2,1)} %get-tuple-element.353), channel_id=1, source_target_pairs={{0,2},{1,3},{2,0},{3,1},{4,6},{5,7},{6,4},{7,5},{8,10},{9,11},{10,... | collective-permute-start | bytes 3538952 | tf_op jit(solution)/shard_map/ppermute | solution.py:46
  202.7 29.9 %collective-permute-start.33 = (bf16[8,48,1536]{2,1,0:T(8,128)(2,1)S(1)}, bf16[8,48,1536]{2,1,0:T(8,128)(2,1)}, u32[]{:S(2)}, u32[]{:S(2)}) collective-permute-start(bf16[8,48,1536]{2,1,0:T(8,128)(2,1)S(1)} %copy-done.78), channel_id=1, source_target_pairs={{0,2},{1,3},{2,0},{3,1},{4,6},{5,7},{6,4},{7,5},{8,10},{9,11},{10,... | collective-permute-start | bytes 3538952 | tf_op jit(solution)/shard_map/ppermute | solution.py:46
  251.0 20.4 %collective-permute-start.38 = (bf16[2,8,48,384]{3,2,1,0:T(8,128)(2,1)S(1)}, bf16[2,8,48,384]{3,2,1,0:T(8,128)(2,1)S(1)}, u32[]{:S(2)}, u32[]{:S(2)}) collective-permute-start(bf16[2,8,48,384]{3,2,1,0:T(8,128)(2,1)S(1)} %get-tuple-element.383), channel_id=1, source_target_pairs={{0,2},{1,3},{2,0},{3,1},{4,6},{5,7},{6,4},{7,5},{8,10},{9,11},{10,... | collective-permute-start | bytes 1769480 | tf_op jit(solution)/shard_map/ppermute | solution.py:46
  251.5 28.1 %collective-permute-start.36 = (bf16[2,4,48,1536]{3,2,1,0:T(8,128)(2,1)S(1)}, bf16[2,4,48,1536]{3,2,1,0:T(8,128)(2,1)S(1)}, u32[]{:S(2)}, u32[]{:S(2)}) collective-permute-start(bf16[2,4,48,1536]{3,2,1,0:T(8,128)(2,1)S(1)} %pad_maximum_fusion.4), channel_id=1, source_target_pairs={{0,4},{1,5},{2,6},{3,7},{4,0},{5,1},{6,2},{7,3},{8,12},{9,13},{10,... | collective-permute-start | bytes 3538952 | tf_op jit(solution)/shard_map/ppermute | solution.py:46
  253.1 28.0 %collective-permute-start.37 = (bf16[8,48,1536]{2,1,0:T(8,128)(2,1)S(1)}, bf16[8,48,1536]{2,1,0:T(8,128)(2,1)S(1)}, u32[]{:S(2)}, u32[]{:S(2)}) collective-permute-start(bf16[8,48,1536]{2,1,0:T(8,128)(2,1)S(1)} %add_convert_fusion.1), channel_id=1, source_target_pairs={{0,1},{1,0},{2,3},{3,2},{4,5},{5,4},{6,7},{7,6},{8,9},{9,8},{10,11... | collective-permute-start | bytes 3538952 | tf_op jit(solution)/shard_map/ppermute | solution.py:46
  281.3 22.9 %collective-permute-start.42 = (bf16[2,4,48,384]{3,2,1,0:T(8,128)(2,1)S(1)}, bf16[2,4,48,384]{3,2,1,0:T(8,128)(2,1)S(1)}, u32[]{:S(2)}, u32[]{:S(2)}) collective-permute-start(bf16[2,4,48,384]{3,2,1,0:T(8,128)(2,1)S(1)} %get-tuple-element.555), channel_id=1, source_target_pairs={{0,4},{1,5},{2,6},{3,7},{4,0},{5,1},{6,2},{7,3},{8,12},{9,13},{10,... | collective-permute-start | bytes 884744 | tf_op jit(solution)/shard_map/ppermute | solution.py:46
  282.8 21.4 %collective-permute-start.40 = (bf16[4,48,1536]{2,1,0:T(8,128)(2,1)S(1)}, bf16[4,48,1536]{2,1,0:T(8,128)(2,1)S(1)}, u32[]{:S(2)}, u32[]{:S(2)}) collective-permute-start(bf16[4,48,1536]{2,1,0:T(8,128)(2,1)S(1)} %get-tuple-element.545), channel_id=1, source_target_pairs={{0,1},{1,0},{2,3},{3,2},{4,5},{5,4},{6,7},{7,6},{8,9},{9,8},{10,11... | collective-permute-start | bytes 1769480 | tf_op jit(solution)/shard_map/ppermute | solution.py:46
  284.2 20.0 %collective-permute-start.41 = (bf16[4,48,1536]{2,1,0:T(8,128)(2,1)S(1)}, bf16[4,48,1536]{2,1,0:T(8,128)(2,1)S(1)}, u32[]{:S(2)}, u32[]{:S(2)}) collective-permute-start(bf16[4,48,1536]{2,1,0:T(8,128)(2,1)S(1)} %get-tuple-element.533), channel_id=1, source_target_pairs={{0,4},{1,5},{2,6},{3,7},{4,0},{5,1},{6,2},{7,3},{8,12},{9,13},{10,... | collective-permute-start | bytes 1769480 | tf_op jit(solution)/shard_map/ppermute | solution.py:46
  312.7 18.2 %collective-permute-start.43 = (bf16[512,768]{1,0:T(8,128)(2,1)S(1)}, bf16[512,768]{1,0:T(8,128)(2,1)S(1)}, u32[]{:S(2)}, u32[]{:S(2)}) collective-permute-start(bf16[512,768]{1,0:T(8,128)(2,1)S(1)} %get-tuple-element.579), channel_id=1, source_target_pairs={{0,1},{1,0},{2,3},{3,2},{4,5},{5,4},{6,7},{7,6},{8,9},{9,8},{10,11... | collective-permute-start | bytes 2359304 | tf_op jit(solution)/shard_map/ppermute | solution.py:46
  342.7 20.0 %collective-permute-start.52 = (bf16[512,768]{1,0:T(8,128)(2,1)S(1)}, bf16[512,768]{1,0:T(8,128)(2,1)S(1)}, u32[]{:S(2)}, u32[]{:S(2)}) collective-permute-start(bf16[512,768]{1,0:T(8,128)(2,1)S(1)} %get-tuple-element.581), channel_id=1, source_target_pairs={{0,1},{1,0},{2,3},{3,2},{4,5},{5,4},{6,7},{7,6},{8,9},{9,8},{10,11... | collective-permute-start | bytes 2359304 | tf_op jit(solution)/shard_map/ppermute | solution.py:46
  393.9 22.3 %all-to-all-start.2 = ((bf16[32,8,768]{2,1,0:T(8,128)(2,1)}), bf16[32,8,768]{2,1,0:T(8,128)(2,1)S(1)}, u32[]{:S(2)}, u32[]{:S(2)}) async-start(bf16[32,8,768]{2,1,0:T(8,128)(2,1)} %fusion.8), calls=%async_computation.2 | async-start | bytes 786432 | tf_op jit(solution)/shard_map/all_to_all | solution.py:1202
  (118 other events, 1328.2 us)

commit v6 on v5

--- a/solution.py
+++ b/solution.py
@@ -931,9 +931,12 @@
     chosen = (step_pad[:, None] == row_ids[None, :]).astype(bf16)
     cond = dot(chosen, table_full).astype(bf16)
     col_width = w_mod.shape[1]
-    col_part = dot(cond, w_mod).reshape(dp_count, 1, 16, col_width)
-    col_part = jnp.broadcast_to(col_part, (dp_count, tensor_count, 16, col_width))
-    col_part = col_part.reshape(devices, 16, col_width).astype(f32)
+    col_part = dot(cond, w_mod).reshape(dp_count, 16, col_width)
+    prompt_cols = jnp.pad(col_part[:, 0], ((0, 0), (0, -col_width % NCONT)))
+    prompt_cols = prompt_cols.reshape(dp_count, NCONT, -1)
+    col_part = jnp.concatenate([col_part[:, 1:SEGS], prompt_cols], 2)[:, None]
+    col_part = jnp.broadcast_to(col_part, (dp_count, tensor_count) + col_part.shape[2:])
+    col_part = col_part.reshape((devices,) + col_part.shape[2:])
     arrived = lax.all_to_all(col_part, BOTH, 0, 0, tiled=True)
     qkv_far, qkv_near, rest, rest_came, tables, info, _ = tie(
         qkv_far, qkv_near, rest, rest_came, tables, info, col_part
@@ -944,7 +947,10 @@
         rest_came = swap(rest, 8 * far_rest[0])
 
     qkv_far, qkv_near, arrived, came, x_parts = tie(qkv_far, qkv_near, arrived, came, x_parts)
-    mods = jnp.transpose(arrived, (1, 0, 2)).reshape(16, 6 * width)
+    mods = jnp.transpose(arrived[..., :col_width], (1, 0, 2)).reshape(NCONT, 6 * width)
+    prompt_cols = arrived[..., col_width:].reshape(devices, -1)[:, :col_width]
+    mods = jnp.concatenate([prompt_cols.reshape(1, 6 * width), mods], 0)
+    mods = jnp.pad(mods, ((0, 16 - SEGS), (0, 0)))
     came.append(swap(x_parts[1], TENSOR))
     qkv_own = join(qkv_far, qkv_near[0], near)
     qkv_other = join(qkv_near[1], qkv_near[2], near)

time: 421 us -> 418 us (level)
  blocking collectives: 0 us -> 15.6 us
  waiting for transfers between devices: 89.3 us -> 75.9 us
  starting transfers between devices: 77.3 us -> 71.6 us
    all_to_all x0 -> x1, blocking collectives: none -> 15.6 us  [body(): arrived = lax.all_to_all(col_part, BOTH, 0, 0, tiled=True)]
    ppermute x58, waiting for transfers between devices: 83.8 us -> 75.9 us  [swap(): return lax.ppermute(x, BOTH, [(i, i ^ bits) for i in range(count)])]
    all_to_all x1 -> x0, waiting for transfers between devices: 5.47 us -> none  [body(): arrived = lax.all_to_all(col_part, BOTH, 0, 0, tiled=True)]
  transfers between devices with their start and end apart: 61 -> 60, of which waited for: 25 -> 23; matrix products, arithmetic and copies ran while one was open for 12% -> 12% of each run, Pallas kernels for 38% -> 39%
where the time goes in v6:
time: 418 us; the launch traced here: 414 us
  Pallas kernels  177 us (42%)
  waiting for transfers between devices  75.9 us (18%)
  starting transfers between devices  71.6 us (17%)
  local copies, waits for them, and re-layouts  30.4 us (7%)
  other arithmetic  20.3 us (5%)
  matrix products  19.6 us (5%)
  blocking collectives  15.6 us (4%)
    ppermute x58, waiting for transfers between devices, swap(): return lax.ppermute(x, BOTH, [(i, i ^ bits) for i in range(count)])  75.9 us
    ppermute x58, starting transfers between devices, swap(): return lax.ppermute(x, BOTH, [(i, i ^ bits) for i in range(count)])  63 us
    pallas_call x2, Pallas kernels, feed_forward(): pl.pallas_call(lambda *refs: mlp_kernel(first, len(weights), *refs), grid...  59.3 us
    pallas_call x4, Pallas kernels, attend_back(): pl.pallas_call(lambda *refs: backward_kernel(first, last, tiles, own, *re...  38.5 us
    pallas_call x2, Pallas kernels, attend(): pl.pallas_call(forward_kernel, grid_spec=pltpu.PrefetchScalarGridSpec(num...  24.7 us
    pallas_call x2, Pallas kernels, project(): pl.pallas_call(kernel, grid_spec=pltpu.PrefetchScalarGridSpec(num_scalar_...  19.9 us
    dot_general x13, matrix products, dot(): return lax.dot_general(left, right, dims, preferred_element_type=f32)  18.2 us
    all_to_all x1, blocking collectives, body(): arrived = lax.all_to_all(col_part, BOTH, 0, 0, tiled=True)  15.6 us
  transfers between devices with their start and end apart: 60, of which 23 were waited for; matrix products, arithmetic and copies ran while one was open for 12% of the time, Pallas kernels for 39%

profile of v6, /device:TPU:0, one launch (start us, length us, event | category | flops | bytes accessed | tf_op | source)
XLA Modules:
  0.0 414.2 jit_solution(10835881121527453743)
XLA Ops:
  3.1 4.1 collective-permute-start
  16.7 5.4 %multiply_sine_fusion = (f32[1024,128]{1,0:T(8,128)}, f32[1024,128]{1,0:T(8,128)}, f32[1024,128]{1,0:T(8,128)}, f32[1024,128]{1,0:T(8,128)}) fusion(f32[1024]{0:T(1024)S(1)} %get-tuple-element.584, f32[128]{0:T(128)S(1)} %fusion.50, f32[1024]{0:T(1024)S(1)} %get-tuple-element.583), kind=kLoop, calls=%fused_computation.49 | loop fusion | flops 262144 | bytes 2105856 | tf_op jit(solution)/shard_map/sin | solution.py:912
  39.5 10.9 %collective-permute-done.5.refs_2_ = bf16[1,48,3456]{2,1,0:T(8,128)(2,1)S(1)} collective-permute-done((bf16[1,48,3456]{2,1,0:T(8,128)(2,1)S(1)}, bf16[1,48,3456]{2,1,0:T(8,128)(2,1)S(1)}, u32[]{:S(2)}, u32[]{:S(2)}) %collective-permute-start.5) | collective-permute-done | bytes 331808 | tf_op jit(solution)/shard_map/ppermute | solution.py:46
  51.8 15.6 %all_to_all.15 = f32[32,8,162]{2,1,0:T(8,128)S(1)} all-to-all(f32[32,8,162]{2,1,0:T(8,128)S(1)} %bitcast.271), channel_id=1, replica_groups=mesh['dp'=16,'tensor'=2] {'dp','tensor'}, dimensions={0} | all-to-all | bytes 331776 | tf_op jit(solution)/shard_map/all_to_all | solution.py:940
  90.8 11.2 %project.2 = (bf16[2,1024,1152]{2,1,0:T(8,128)(2,1)S(1)}, bf16[1024,768]{1,0:T(8,128)(2,1)S(1)}) custom-call(s32[13]{0:T(128)S(1)} %concatenate.60.info.refs_0_, bf16[1024,768]{1,0:T(8,128)(2,1)S(1)} %copy-done.8, f32[16,4608]{1,0:T(8,128)S(1)} %select_maximum_fusion.mods_ref.refs_3_, bf16[768,1152]{1,0:T(8,128)(2,1)S(1)} %bitcast.213, ...), custom_call_target="tpu_custom_call" | custom-call | flops 99999997952 | bytes 1 | tf_op jit(solution)/shard_map/project/pallas_call | solution.py:220
  105.6 8.7 %project.3 = (bf16[2,1024,768]{2,1,0:T(8,128)(2,1)S(1)}, bf16[1024,768]{1,0:T(8,128)(2,1)S(1)}) custom-call(s32[13]{0:T(128)S(1)} %concatenate.60.info.refs_0_, bf16[1024,768]{1,0:T(8,128)(2,1)S(1)} %copy-done.8, bf16[256,768]{1,0:T(8,128)(2,1)S(1)} %copy-done.34, bf16[384,768]{1,0:T(8,128)(2,1)} %collective-permute-done.15.refs_1_, ...), custom_call_target="tpu_custom_call" | custom-call | flops 99999997952 | bytes 1 | tf_op jit(solution)/shard_map/project/pallas_call | solution.py:220
  119.3 12.3 %attend.2 = (bf16[1024,384]{1,0:T(8,128)(2,1)S(1)}, f32[3,2,1024]{2,1,0:T(2,128)S(1)}) custom-call(s32[13]{0:T(128)S(1)} %concatenate.60.info.refs_0_, bf16[2,1024,1152]{2,1,0:T(8,128)(2,1)S(1)} %get-tuple-element.322.refs_0_.refs_3_.refs_4_.refs_1_.refs_9_.refs_10_.refs_5_.refs_6_, ...), custom_call_target="tpu_custom_call" | custom-call | flops 99999997952 | bytes 1 | tf_op jit(solution)/shard_map/attend/pallas_call | solution.py:640
  137.8 12.5 %attend.3 = (bf16[1024,384]{1,0:T(8,128)(2,1)S(1)}, f32[3,2,1024]{2,1,0:T(2,128)S(1)}) custom-call(s32[13]{0:T(128)S(1)} %concatenate.60.info.refs_0_, bf16[2,1024,1152]{2,1,0:T(8,128)(2,1)S(1)} %get-tuple-element.322.refs_0_.refs_3_.refs_4_.refs_1_.refs_9_.refs_10_.refs_5_.refs_6_, ...), custom_call_target="tpu_custom_call" | custom-call | flops 99999997952 | bytes 1 | tf_op jit(solution)/shard_map/attend/pallas_call | solution.py:640
  156.3 3.9 middle_norm.1
  164.8 29.5 %feed_forward.2 = (f32[1024,768]{1,0:T(8,128)}, f32[1024,768]{1,0:T(8,128)}, bf16[8,48,1536]{2,1,0:T(8,128)(2,1)S(1)}, bf16[8,48,1536]{2,1,0:T(8,128)(2,1)}, bf1...) custom-call(s32[13]{0:T(128)S(1)} %concatenate.60.info.refs_0_, ...), custom_call_target="tpu_custom_call" | custom-call | flops 99999997952 | bytes 1 | tf_op jit(solution)/shard_map/feed_forward/pallas_call | solution.py:380
  201.1 29.9 %feed_forward.3 = (f32[1024,768]{1,0:T(8,128)}, f32[1024,768]{1,0:T(8,128)}, bf16[8,48,1536]{2,1,0:T(8,128)(2,1)S(1)}, bf16[8,48,1536]{2,1,0:T(8,128)(2,1)}, bf1...) custom-call(s32[13]{0:T(128)S(1)} %concatenate.60.info.refs_0_, bf16[1024,768]{1,0:T(8,128)(2,1)} %copy-done.45, ...), custom_call_target="tpu_custom_call" | custom-call | flops 99999997952 | bytes 1 | tf_op jit(solution)/shard_map/feed_forward/pallas_call | solution.py:380
  231.0 12.2 %post.1 = (bf16[1024,768]{1,0:T(8,128)(2,1)}, f32[1024,768]{1,0:T(8,128)}, bf16[1024,384]{1,0:T(8,128)(2,1)S(1)}, bf16[1024,384]{1,0:T(8,128)(2,1)S(1)}, f32[8,8...) custom-call(s32[13]{0:T(128)S(1)} %concatenate.60.info.refs_0_, ...), custom_call_target="tpu_custom_call" | custom-call | flops 99999997952 | bytes 1 | tf_op jit(solution)/shard_map/post/pallas_call | solution.py:468
  253.0 16.7 %attend_back.4 = (bf16[1024,384]{1,0:T(8,128)(2,1)S(1)}, bf16[1024,384]{1,0:T(8,128)(2,1)S(1)}, bf16[1024,384]{1,0:T(8,128)(2,1)S(1)}, bf16[1024,384]{1,0:T(8,128)(2,1)S(1)}, bf16[1024,384]{1,0:T(8,128)(2,1)S(1)}) custom-call(s32[13]{0:T(128)S(1)} %concatenate.60.info.refs_0_, bf16[2,1024,1152]{2,1,0:T(8,128)(2,1)S(1)} %copy-done.39, ...), custom_call_target="tpu_custom_call" | custom-call | flops 99999997952 | bytes 1 | tf_op jit(solution)/shard_map/attend_back/pallas_call | solution.py:811
  269.7 8.2 %collective-permute-done.36 = bf16[2,4,48,1536]{3,2,1,0:T(8,128)(2,1)S(1)} collective-permute-done((bf16[2,4,48,1536]{3,2,1,0:T(8,128)(2,1)S(1)}, bf16[2,4,48,1536]{3,2,1,0:T(8,128)(2,1)S(1)}, u32[]{:S(2)}, u32[]{:S(2)}) %collective-permute-start.36) | collective-permute-done | bytes 1179680 | tf_op jit(solution)/shard_map/ppermute | solution.py:46
  292.0 10.7 %attend_back.5 = (f32[1024,384]{1,0:T(8,128)S(1)}, bf16[512,384]{1,0:T(8,128)(2,1)S(1)}, bf16[512,384]{1,0:T(8,128)(2,1)S(1)}) custom-call(s32[13]{0:T(128)S(1)} %concatenate.60.info.refs_0_, bf16[2,1024,1152]{2,1,0:T(8,128)(2,1)S(1)} %copy-done.39, bf16[1024,384]{1,0:T(8,128)(2,1)S(1)} %get-tuple-element.418.refs_2_, bf16[1024,384]{1,0:T(8,128)(2,1)S(1)} %copy-done.51, ...), custom_call_target="tpu_custom_call" | custom-call | flops 99999997952 | bytes 1 | tf_op jit(solution)/shard_map/attend_back/pallas_call | solution.py:811
  311.4 7.1 %attend_back.6 = (f32[1024,384]{1,0:T(8,128)S(1)}, bf16[512,384]{1,0:T(8,128)(2,1)S(1)}, bf16[512,384]{1,0:T(8,128)(2,1)S(1)}) custom-call(s32[13]{0:T(128)S(1)} %concatenate.60.info.refs_0_, bf16[2,1024,1152]{2,1,0:T(8,128)(2,1)S(1)} %copy-done.39, bf16[1024,384]{1,0:T(8,128)(2,1)S(1)} %get-tuple-element.418.refs_2_, bf16[1024,384]{1,0:T(8,128)(2,1)S(1)} %copy-done.51, ...), custom_call_target="tpu_custom_call" | custom-call | flops 99999997952 | bytes 1 | tf_op jit(solution)/shard_map/attend_back/pallas_call | solution.py:811
  319.5 9.7 %collective-permute-done.43 = bf16[512,768]{1,0:T(8,128)(2,1)S(1)} collective-permute-done((bf16[512,768]{1,0:T(8,128)(2,1)S(1)}, bf16[512,768]{1,0:T(8,128)(2,1)S(1)}, u32[]{:S(2)}, u32[]{:S(2)}) %collective-permute-start.43) | collective-permute-done | bytes 786464 | tf_op jit(solution)/shard_map/ppermute | solution.py:46
  335.8 4.1 attend_back.7
  339.9 4.9 %collective-permute-start.52 = (bf16[512,768]{1,0:T(8,128)(2,1)S(1)}, bf16[512,768]{1,0:T(8,128)(2,1)S(1)}, u32[]{:S(2)}, u32[]{:S(2)}) collective-permute-start(bf16[512,768]{1,0:T(8,128)(2,1)S(1)} %get-tuple-element.581), channel_id=1, source_target_pairs={{0,1},{1,0},{2,3},{3,2},{4,5},{5,4},{6,7},{7,6},{8,9},{9,8},{10,11... | collective-permute-start | bytes 2359304 | tf_op jit(solution)/shard_map/ppermute | solution.py:46
  363.0 4.5 %last.1 = (f32[1024,768]{1,0:T(8,128)}, f32[8,8,768]{2,1,0:T(8,128)S(1)}) custom-call(s32[13]{0:T(128)S(1)} %concatenate.60.info.refs_0_, bf16[1024,768]{1,0:T(8,128)(2,1)S(1)} %copy-done.10, f32[1024,768]{1,0:T(8,128)S(1)} %convolution_add_fusion.own_ref, f32[1024,768]{1,0:T(8,128)S(1)} %pad_maximum_fusion.prompt_ref, ...), custom_call_target="tpu_custom_call" | custom-call | flops 99999997952 | bytes 1 | tf_op jit(solution)/shard_map/last/pallas_call | solution.py:531
  372.4 4.0 all-to-all-start.1
  380.0 8.2 %collective-permute-done.55 = bf16[2,48,1152]{2,1,0:T(8,128)(2,1)S(1)} collective-permute-done((bf16[2,48,1152]{2,1,0:T(8,128)(2,1)S(1)}, bf16[2,48,1152]{2,1,0:T(8,128)(2,1)S(1)}, u32[]{:S(2)}, u32[]{:S(2)}) %collective-permute-start.55) | collective-permute-done | bytes 221216 | tf_op jit(solution)/shard_map/ppermute | solution.py:46
  391.0 4.6 %all-to-all-start.2 = ((bf16[32,8,768]{2,1,0:T(8,128)(2,1)}), bf16[32,8,768]{2,1,0:T(8,128)(2,1)S(1)}, u32[]{:S(2)}, u32[]{:S(2)}) async-start(bf16[32,8,768]{2,1,0:T(8,128)(2,1)} %fusion.8), calls=%async_computation.2 | async-start | bytes 786432 | tf_op jit(solution)/shard_map/all_to_all | solution.py:1208
  400.2 12.3 %collective-permute-done.56 = bf16[48,1152]{1,0:T(8,128)(2,1)S(1)} collective-permute-done((bf16[48,1152]{1,0:T(8,128)(2,1)S(1)}, bf16[48,1152]{1,0:T(8,128)(2,1)S(1)}, u32[]{:S(2)}, u32[]{:S(2)}) %collective-permute-start.56) | collective-permute-done | bytes 110624 | tf_op jit(solution)/shard_map/ppermute | solution.py:46
  (426 shorter events, 159.3 us)
Async XLA Ops:
  29.8 20.6 %collective-permute-start.4 = (bf16[4,48,1152]{2,1,0:T(8,128)(2,1)S(1)}, bf16[4,48,1152]{2,1,0:T(8,128)(2,1)S(1)}, u32[]{:S(2)}, u32[]{:S(2)}) collective-permute-start(bf16[4,48,1152]{2,1,0:T(8,128)(2,1)S(1)} %bitcast.252), channel_id=1, source_target_pairs={{0,1},{1,0},{2,3},{3,2},{4,5},{5,4},{6,7},{7,6},{8,9},{9,8},{10,11... | collective-permute-start | bytes 1327112 | tf_op jit(solution)/shard_map/ppermute | solution.py:46
  31.3 19.1 %collective-permute-start.3 = (bf16[4,48,1152]{2,1,0:T(8,128)(2,1)S(1)}, bf16[4,48,1152]{2,1,0:T(8,128)(2,1)S(1)}, u32[]{:S(2)}, u32[]{:S(2)}) collective-permute-start(bf16[4,48,1152]{2,1,0:T(8,128)(2,1)S(1)} %bitcast.253), channel_id=1, source_target_pairs={{0,4},{1,5},{2,6},{3,7},{4,0},{5,1},{6,2},{7,3},{8,12},{9,13},{10,... | collective-permute-start | bytes 1327112 | tf_op jit(solution)/shard_map/ppermute | solution.py:46
  32.4 17.9 %collective-permute-start.5 = (bf16[1,48,3456]{2,1,0:T(8,128)(2,1)S(1)}, bf16[1,48,3456]{2,1,0:T(8,128)(2,1)S(1)}, u32[]{:S(2)}, u32[]{:S(2)}) collective-permute-start(bf16[1,48,3456]{2,1,0:T(8,128)(2,1)S(1)} %maximum_bitcast_fusion.refs_1_), channel_id=1, source_target_pairs={{0,16},{1,17},{2,18},{3,19},{4,20},{5,21},{6,22},{7,23},{8,24},{9,... | collective-permute-start | bytes 995336 | tf_op jit(solution)/shard_map/ppermute | solution.py:46
  50.4 17.0 %collective-permute-start.12 = (bf16[4,48,1152]{2,1,0:T(8,128)(2,1)S(1)}, bf16[4,48,1152]{2,1,0:T(8,128)(2,1)S(1)}, u32[]{:S(2)}, u32[]{:S(2)}) collective-permute-start(bf16[4,48,1152]{2,1,0:T(8,128)(2,1)S(1)} %bitcast.254), channel_id=1, source_target_pairs={{0,5},{1,4},{2,7},{3,6},{4,1},{5,0},{6,3},{7,2},{8,13},{9,12},{10,... | collective-permute-start | bytes 1327112 | tf_op jit(solution)/shard_map/ppermute | solution.py:46
  68.7 17.3 %collective-permute-start.11 = (bf16[2,48,3456]{2,1,0:T(8,128)(2,1)S(1)}, bf16[2,48,3456]{2,1,0:T(8,128)(2,1)S(1)}, u32[]{:S(2)}, u32[]{:S(2)}) collective-permute-start(bf16[2,48,3456]{2,1,0:T(8,128)(2,1)S(1)} %bitcast.222), channel_id=1, source_target_pairs={{0,8},{1,9},{2,10},{3,11},{4,12},{5,13},{6,14},{7,15},{8,0},{9,1},... | collective-permute-start | bytes 1990664 | tf_op jit(solution)/shard_map/ppermute | solution.py:46
  86.7 27.6 %collective-permute-start.19 = (bf16[4,48,384]{2,1,0:T(8,128)(2,1)}, bf16[4,48,384]{2,1,0:T(8,128)(2,1)}, u32[]{:S(2)}, u32[]{:S(2)}) collective-permute-start(bf16[4,48,384]{2,1,0:T(8,128)(2,1)} %bitcast.30.refs_1_), channel_id=1, source_target_pairs={{0,1},{1,0},{2,3},{3,2},{4,5},{5,4},{6,7},{7,6},{8,9},{9,8},{10,11... | collective-permute-start | bytes 442376 | tf_op jit(solution)/shard_map/ppermute | solution.py:46
  87.5 26.9 %collective-permute-start.18 = (bf16[4,48,384]{2,1,0:T(8,128)(2,1)}, bf16[4,48,384]{2,1,0:T(8,128)(2,1)}, u32[]{:S(2)}, u32[]{:S(2)}) collective-permute-start(bf16[4,48,384]{2,1,0:T(8,128)(2,1)} %bitcast.30.refs_1_), channel_id=1, source_target_pairs={{0,4},{1,5},{2,6},{3,7},{4,0},{5,1},{6,2},{7,3},{8,12},{9,13},{10,... | collective-permute-start | bytes 442376 | tf_op jit(solution)/shard_map/ppermute | solution.py:46
  88.4 16.6 %collective-permute-start.16 = (bf16[384,768]{1,0:T(8,128)(2,1)S(1)}, bf16[384,768]{1,0:T(8,128)(2,1)S(1)}, u32[]{:S(2)}, u32[]{:S(2)}) collective-permute-start(bf16[384,768]{1,0:T(8,128)(2,1)S(1)} %copy-done.62), channel_id=1, source_target_pairs={{0,1},{1,0},{2,3},{3,2},{4,5},{5,4},{6,7},{7,6},{8,9},{9,8},{10,11... | collective-permute-start | bytes 1769480 | tf_op jit(solution)/shard_map/ppermute | solution.py:46
  114.4 17.2 %collective-permute-start.22 = (bf16[4,48,384]{2,1,0:T(8,128)(2,1)}, bf16[4,48,384]{2,1,0:T(8,128)(2,1)S(1)}, u32[]{:S(2)}, u32[]{:S(2)}) collective-permute-start(bf16[4,48,384]{2,1,0:T(8,128)(2,1)} %collective-permute-done.19.refs_1_), channel_id=1, source_target_pairs={{0,4},{1,5},{2,6},{3,7},{4,0},{5,1},{6,2},{7,3},{8,12},{9,13},{10,... | collective-permute-start | bytes 442376 | tf_op jit(solution)/shard_map/ppermute | solution.py:46
  115.3 17.7 %collective-permute-start.21 = (bf16[4,48,1536]{2,1,0:T(8,128)(2,1)S(1)}, bf16[4,48,1536]{2,1,0:T(8,128)(2,1)S(1)}, u32[]{:S(2)}, u32[]{:S(2)}) collective-permute-start(bf16[4,48,1536]{2,1,0:T(8,128)(2,1)S(1)} %bitcast.246), channel_id=1, source_target_pairs={{0,1},{1,0},{2,3},{3,2},{4,5},{5,4},{6,7},{7,6},{8,9},{9,8},{10,11... | collective-permute-start | bytes 1769480 | tf_op jit(solution)/shard_map/ppermute | solution.py:46
  116.1 16.9 %collective-permute-start.23 = (bf16[8,48,1536]{2,1,0:T(8,128)(2,1)S(1)}, bf16[8,48,1536]{2,1,0:T(8,128)(2,1)S(1)}, u32[]{:S(2)}, u32[]{:S(2)}) collective-permute-start(bf16[8,48,1536]{2,1,0:T(8,128)(2,1)S(1)} %bitcast.228), channel_id=1, source_target_pairs={{0,2},{1,3},{2,0},{3,1},{4,6},{5,7},{6,4},{7,5},{8,10},{9,11},{10,... | collective-permute-start | bytes 3538952 | tf_op jit(solution)/shard_map/ppermute | solution.py:46
  152.6 41.6 %collective-permute-start.29 = (bf16[4,48,1536]{2,1,0:T(8,128)(2,1)}, bf16[4,48,1536]{2,1,0:T(8,128)(2,1)}, u32[]{:S(2)}, u32[]{:S(2)}) collective-permute-start(bf16[4,48,1536]{2,1,0:T(8,128)(2,1)} %collective-permute-done.24.refs_1_), channel_id=1, source_target_pairs={{0,4},{1,5},{2,6},{3,7},{4,0},{5,1},{6,2},{7,3},{8,12},{9,13},{10,... | collective-permute-start | bytes 1769480 | tf_op jit(solution)/shard_map/ppermute | solution.py:46
  154.5 39.8 %collective-permute-start.30 = (bf16[8,48,1536]{2,1,0:T(8,128)(2,1)}, bf16[8,48,1536]{2,1,0:T(8,128)(2,1)}, u32[]{:S(2)}, u32[]{:S(2)}) collective-permute-start(bf16[8,48,1536]{2,1,0:T(8,128)(2,1)} %bitcast.38.refs_7_), channel_id=1, source_target_pairs={{0,2},{1,3},{2,0},{3,1},{4,6},{5,7},{6,4},{7,5},{8,10},{9,11},{10,... | collective-permute-start | bytes 3538952 | tf_op jit(solution)/shard_map/ppermute | solution.py:46
  200.5 30.4 %collective-permute-start.32 = (bf16[8,48,1536]{2,1,0:T(8,128)(2,1)}, bf16[8,48,1536]{2,1,0:T(8,128)(2,1)S(1)}, u32[]{:S(2)}, u32[]{:S(2)}) collective-permute-start(bf16[8,48,1536]{2,1,0:T(8,128)(2,1)} %get-tuple-element.353), channel_id=1, source_target_pairs={{0,2},{1,3},{2,0},{3,1},{4,6},{5,7},{6,4},{7,5},{8,10},{9,11},{10,... | collective-permute-start | bytes 3538952 | tf_op jit(solution)/shard_map/ppermute | solution.py:46
  201.0 29.9 %collective-permute-start.33 = (bf16[8,48,1536]{2,1,0:T(8,128)(2,1)S(1)}, bf16[8,48,1536]{2,1,0:T(8,128)(2,1)}, u32[]{:S(2)}, u32[]{:S(2)}) collective-permute-start(bf16[8,48,1536]{2,1,0:T(8,128)(2,1)S(1)} %copy-done.78), channel_id=1, source_target_pairs={{0,2},{1,3},{2,0},{3,1},{4,6},{5,7},{6,4},{7,5},{8,10},{9,11},{10,... | collective-permute-start | bytes 3538952 | tf_op jit(solution)/shard_map/ppermute | solution.py:46
  249.3 20.4 %collective-permute-start.38 = (bf16[2,8,48,384]{3,2,1,0:T(8,128)(2,1)S(1)}, bf16[2,8,48,384]{3,2,1,0:T(8,128)(2,1)S(1)}, u32[]{:S(2)}, u32[]{:S(2)}) collective-permute-start(bf16[2,8,48,384]{3,2,1,0:T(8,128)(2,1)S(1)} %get-tuple-element.383), channel_id=1, source_target_pairs={{0,2},{1,3},{2,0},{3,1},{4,6},{5,7},{6,4},{7,5},{8,10},{9,11},{10,... | collective-permute-start | bytes 1769480 | tf_op jit(solution)/shard_map/ppermute | solution.py:46
  249.8 28.1 %collective-permute-start.36 = (bf16[2,4,48,1536]{3,2,1,0:T(8,128)(2,1)S(1)}, bf16[2,4,48,1536]{3,2,1,0:T(8,128)(2,1)S(1)}, u32[]{:S(2)}, u32[]{:S(2)}) collective-permute-start(bf16[2,4,48,1536]{3,2,1,0:T(8,128)(2,1)S(1)} %pad_maximum_fusion.4), channel_id=1, source_target_pairs={{0,4},{1,5},{2,6},{3,7},{4,0},{5,1},{6,2},{7,3},{8,12},{9,13},{10,... | collective-permute-start | bytes 3538952 | tf_op jit(solution)/shard_map/ppermute | solution.py:46
  251.5 27.9 %collective-permute-start.37 = (bf16[8,48,1536]{2,1,0:T(8,128)(2,1)S(1)}, bf16[8,48,1536]{2,1,0:T(8,128)(2,1)S(1)}, u32[]{:S(2)}, u32[]{:S(2)}) collective-permute-start(bf16[8,48,1536]{2,1,0:T(8,128)(2,1)S(1)} %add_convert_fusion.1), channel_id=1, source_target_pairs={{0,1},{1,0},{2,3},{3,2},{4,5},{5,4},{6,7},{7,6},{8,9},{9,8},{10,11... | collective-permute-start | bytes 3538952 | tf_op jit(solution)/shard_map/ppermute | solution.py:46
  279.6 23.1 %collective-permute-start.42 = (bf16[2,4,48,384]{3,2,1,0:T(8,128)(2,1)S(1)}, bf16[2,4,48,384]{3,2,1,0:T(8,128)(2,1)S(1)}, u32[]{:S(2)}, u32[]{:S(2)}) collective-permute-start(bf16[2,4,48,384]{3,2,1,0:T(8,128)(2,1)S(1)} %get-tuple-element.555), channel_id=1, source_target_pairs={{0,4},{1,5},{2,6},{3,7},{4,0},{5,1},{6,2},{7,3},{8,12},{9,13},{10,... | collective-permute-start | bytes 884744 | tf_op jit(solution)/shard_map/ppermute | solution.py:46
  281.2 21.5 %collective-permute-start.40 = (bf16[4,48,1536]{2,1,0:T(8,128)(2,1)S(1)}, bf16[4,48,1536]{2,1,0:T(8,128)(2,1)S(1)}, u32[]{:S(2)}, u32[]{:S(2)}) collective-permute-start(bf16[4,48,1536]{2,1,0:T(8,128)(2,1)S(1)} %get-tuple-element.545), channel_id=1, source_target_pairs={{0,1},{1,0},{2,3},{3,2},{4,5},{5,4},{6,7},{7,6},{8,9},{9,8},{10,11... | collective-permute-start | bytes 1769480 | tf_op jit(solution)/shard_map/ppermute | solution.py:46
  282.8 20.0 %collective-permute-start.41 = (bf16[4,48,1536]{2,1,0:T(8,128)(2,1)S(1)}, bf16[4,48,1536]{2,1,0:T(8,128)(2,1)S(1)}, u32[]{:S(2)}, u32[]{:S(2)}) collective-permute-start(bf16[4,48,1536]{2,1,0:T(8,128)(2,1)S(1)} %get-tuple-element.533), channel_id=1, source_target_pairs={{0,4},{1,5},{2,6},{3,7},{4,0},{5,1},{6,2},{7,3},{8,12},{9,13},{10,... | collective-permute-start | bytes 1769480 | tf_op jit(solution)/shard_map/ppermute | solution.py:46
  311.0 18.2 %collective-permute-start.43 = (bf16[512,768]{1,0:T(8,128)(2,1)S(1)}, bf16[512,768]{1,0:T(8,128)(2,1)S(1)}, u32[]{:S(2)}, u32[]{:S(2)}) collective-permute-start(bf16[512,768]{1,0:T(8,128)(2,1)S(1)} %get-tuple-element.579), channel_id=1, source_target_pairs={{0,1},{1,0},{2,3},{3,2},{4,5},{5,4},{6,7},{7,6},{8,9},{9,8},{10,11... | collective-permute-start | bytes 2359304 | tf_op jit(solution)/shard_map/ppermute | solution.py:46
  339.9 19.8 %collective-permute-start.52 = (bf16[512,768]{1,0:T(8,128)(2,1)S(1)}, bf16[512,768]{1,0:T(8,128)(2,1)S(1)}, u32[]{:S(2)}, u32[]{:S(2)}) collective-permute-start(bf16[512,768]{1,0:T(8,128)(2,1)S(1)} %get-tuple-element.581), channel_id=1, source_target_pairs={{0,1},{1,0},{2,3},{3,2},{4,5},{5,4},{6,7},{7,6},{8,9},{9,8},{10,11... | collective-permute-start | bytes 2359304 | tf_op jit(solution)/shard_map/ppermute | solution.py:46
  391.0 22.3 %all-to-all-start.2 = ((bf16[32,8,768]{2,1,0:T(8,128)(2,1)}), bf16[32,8,768]{2,1,0:T(8,128)(2,1)S(1)}, u32[]{:S(2)}, u32[]{:S(2)}) async-start(bf16[32,8,768]{2,1,0:T(8,128)(2,1)} %fusion.8), calls=%async_computation.2 | async-start | bytes 786432 | tf_op jit(solution)/shard_map/all_to_all | solution.py:1208
  (117 other events, 1355.7 us)
